TPU v7x, 256 devices: a whole 4x4x8 slice. The times are simulated.
256 devices in a mesh: visit: 64 (over z, x, core), band: 4 (over y).
Axes of the slice: x: 4, y: 4, z: 8, core: 2. Of those that a mesh axis runs over, the one named last changes fastest.
Arguments:
- source: bfloat16 [64, 2, 160, 8448], P('visit', None, 'band'), may hold values from -6 to 6
- row_start: int32 [64, 128], P('visit', 'band'), may hold values from 0 to 36
- row_weight: bfloat16 [64, 4, 128], P('visit', None, 'band'), may hold values from -0.25 to 0.75
- col_start: int32 [64, 8192], P('visit'), may hold values from 0 to 252
- col_weight: bfloat16 [64, 4, 8192], P('visit'), may hold values from -0.25 to 0.75
- col_offset: int32 [64, 64], P('visit'), may hold values from 0 to 127
- g_taps: bfloat16 [16, 21], replicated, may hold values from -1.25 to 1.25
- h_taps: bfloat16 [16, 21], replicated, may hold values from -1.25 to 1.25
- coef_table: float32 [16, 16, 6], replicated, may hold values from -1.5 to 1.5
- table_ids: int32 [64, 2], P('visit'), may hold values from 0 to 15
- vis_weight: float32 [64, 2], replicated, may hold values from 0.1 to 10
- coverage: int32 [64, 64], replicated, may hold values from 0 to 1, as said below
Outputs:
- coadd: float32 [2, 128, 8192], P(None, 'band', 'visit')
Inputs may be any that keep to these rules, and one draw needn't show every extreme that they name: `coverage`: each visit misses one run of consecutive patches, wrapping, of length 0 to 32, and always intersects the patch of its own index.
All inputs are finite; a program needn't handle non-finite values.
Results may differ from a plain program's by a relative error of at most 0.0057.
Values may be sent and summed in bfloat16 or wider, within the bound.
No kernel may reach another device: no remote copies, remote signals or barrier semaphores. Data moves between devices by JAX's collectives and lax.ppermute only.
A program may use at most 128 MiB of HBM per device.

v0:
```python
import jax
import jax.numpy as jnp
from jax import lax
from jax.sharding import PartitionSpec as P


def extended_2(cells, sides, width):
    for axis, dim in sides:
        count = lax.axis_size(axis)
        ends = count - 1
        head = lax.slice_in_dim(cells, 0, width, axis=dim)
        tail = lax.slice_in_dim(cells, cells.shape[dim] - width, cells.shape[dim], axis=dim)
        cells = jnp.concatenate(
            [
                lax.ppermute(tail, axis, [(i, (i + 1) % count) for i in range(ends)]),
                cells,
                lax.ppermute(head, axis, [((i + 1) % count, i) for i in range(ends)]),
            ],
            axis=dim,
        )
    return cells


def local(
    source,
    row_start,
    row_weight,
    col_start,
    col_weight,
    col_offset,
    g_taps,
    h_taps,
    coef_table,
    table_ids,
    vis_weight,
    coverage,
):
    band_count = source.shape[1]
    src_rows = source.shape[2]
    out_rows = row_start.shape[1]
    width_total = col_start.shape[1]
    block_count = col_offset.shape[1]
    block_width = width_total // block_count
    tap_count = g_taps.shape[1]
    basis_count = g_taps.shape[0]
    margin = tap_count // 2
    table_rows = coef_table.shape[0]
    relative = lax.broadcasted_iota(jnp.int32, (out_rows, src_rows), 1) - row_start[0][:, None]
    row_wts = row_weight[0].astype(jnp.float32)
    band_rows = sum(
        (jnp.where(relative == shift, row_wts[shift][:, None], 0.0) for shift in range(4))
    ).astype(jnp.bfloat16)
    rowres = jnp.einsum(
        "is,nsx->nix", band_rows, source[0], preferred_element_type=jnp.float32
    ).astype(jnp.bfloat16)
    starts = jnp.arange(block_count, dtype=jnp.int32) * block_width + col_offset[0]
    windows = jax.vmap(lambda first: lax.dynamic_slice_in_dim(rowres, first, 2 * block_width, 2))(
        starts
    )
    block_start = col_start[0].reshape(block_count, block_width)
    block_wts = col_weight[0].astype(jnp.float32).reshape(4, block_count, block_width)
    column_rel = (
        lax.broadcasted_iota(jnp.int32, (block_count, 2 * block_width, block_width), 1)
        - block_start[:, None, :]
    )
    band_cols = sum(
        (jnp.where(column_rel == shift, block_wts[shift][:, None, :], 0.0) for shift in range(4))
    ).astype(jnp.bfloat16)
    resampled = jnp.einsum("cnrw,cwk->nrck", windows, band_cols, preferred_element_type=jnp.float32)
    resampled = resampled.reshape(band_count, out_rows, width_total).astype(jnp.bfloat16)
    haloed = extended_2(resampled, (("band", 1),), margin)
    halo_rows = out_rows + 2 * margin
    extended = jnp.pad(haloed, ((0, 0), (0, 0), (block_width, block_width)))
    source_col = lax.broadcasted_iota(jnp.int32, (block_width, block_width), 0)
    target_col = lax.broadcasted_iota(jnp.int32, (block_width, block_width), 1)
    h_float = h_taps.astype(jnp.float32)

    def toeplitz(offset):
        lag = source_col - target_col + offset * block_width + margin
        return sum(
            (
                jnp.where((lag == shift)[:, None, :], h_float[:, shift][None, :, None], 0.0)
                for shift in range(tap_count)
            )
        ).astype(jnp.bfloat16)

    toeplitz_sides = [toeplitz(offset) for offset in (-1, 0, 1)]
    row_lag = lax.broadcasted_iota(jnp.int32, (out_rows, halo_rows), 1) - lax.broadcasted_iota(
        jnp.int32, (out_rows, halo_rows), 0
    )
    g_float = g_taps.astype(jnp.float32)
    toeplitz_rows = sum(
        (
            jnp.where((row_lag == shift)[None, :, :], g_float[:, shift][:, None, None], 0.0)
            for shift in range(tap_count)
        )
    ).astype(jnp.bfloat16)
    picker = (table_ids[0][:, None] == jnp.arange(table_rows, dtype=jnp.int32)[None, :]).astype(
        jnp.float32
    )
    coefs = jnp.einsum("nq,qbt->nbt", picker, coef_table, precision=lax.Precision.HIGHEST)
    rows_whole = out_rows * lax.axis_size("band")
    first_row = (lax.axis_index("band") * out_rows).astype(jnp.float32)
    ycoord = (first_row + jnp.arange(out_rows, dtype=jnp.float32) + 0.5) * (2.0 / rows_whole) - 1.0
    per_group = 8
    group_count = block_count // per_group
    group_width = per_group * block_width

    def one_group(group):
        first = group * group_width
        piece = lax.dynamic_slice_in_dim(extended, first, group_width + 2 * block_width, 2)
        piece = piece.reshape(band_count, halo_rows, per_group + 2, block_width)
        across = sum(
            (
                jnp.einsum(
                    "nsqw,wbk->nbsqk",
                    piece[:, :, side : side + per_group],
                    toeplitz_sides[side],
                    preferred_element_type=jnp.float32,
                )
                for side in range(3)
            )
        )
        across = across.astype(jnp.bfloat16)
        smooth = jnp.einsum(
            "bis,nbsqk->nbiqk", toeplitz_rows, across, preferred_element_type=jnp.float32
        )
        smooth = smooth.reshape(band_count, basis_count, out_rows, group_width)
        xcoord = (first.astype(jnp.float32) + jnp.arange(group_width, dtype=jnp.float32) + 0.5) * (
            2.0 / width_total
        ) - 1.0
        xgrid = jnp.ones((out_rows, 1), jnp.float32) * xcoord[None, :]
        ygrid = ycoord[:, None] * jnp.ones((1, group_width), jnp.float32)
        polys = jnp.stack(
            [jnp.ones_like(xgrid), xgrid, ygrid, xgrid * xgrid, xgrid * ygrid, ygrid * ygrid]
        )
        inner = jnp.einsum("nbt,nbik->ntik", coefs, smooth, precision=lax.Precision.HIGHEST)
        return jnp.sum(polys[None] * inner, axis=1).astype(jnp.bfloat16)

    grouped = lax.map(one_group, jnp.arange(group_count, dtype=jnp.int32))
    matched = jnp.moveaxis(grouped, 0, 2).reshape(band_count, out_rows, width_total)
    patch_count = lax.axis_size("visit")
    patch_width = width_total // patch_count
    visit_index = lax.axis_index("visit")
    pieces = matched.reshape(band_count, out_rows, patch_count, patch_width).transpose(2, 0, 1, 3)
    cover_float = coverage.astype(jnp.float32)
    denom = jnp.einsum("vj,vn->nj", cover_float, vis_weight, precision=lax.Precision.HIGHEST)
    mine = lax.dynamic_index_in_dim(denom, visit_index, 1, keepdims=False)
    own_cover = lax.dynamic_index_in_dim(cover_float, visit_index, 0, keepdims=False)
    own_weight = lax.dynamic_index_in_dim(vis_weight, visit_index, 0, keepdims=False)
    factor = own_cover[:, None] * own_weight[None, :]
    part = pieces.astype(jnp.float32)
    total = lax.psum_scatter(
        part * factor[:, :, None, None], "visit", scatter_dimension=0, tiled=True
    )[0]
    return total / mine[:, None, None]


def solution(mesh):
    in_specs = (
        P("visit", None, "band", None),
        P("visit", "band"),
        P("visit", None, "band"),
        P("visit", None),
        P("visit", None, None),
        P("visit", None),
        P(),
        P(),
        P(),
        P("visit", None),
        P(),
        P(),
    )
    out_specs = P(None, "band", "visit")
    return jax.shard_map(local, mesh=mesh, in_specs=in_specs, out_specs=out_specs, check_vma=False)
```

profile of v0, /device:TPU:24, one launch (start us, length us, event | category | flops | bytes accessed | tf_op | source)
XLA Modules:
  0.0 618.7 jit_solution(2071383150128890292)
XLA Ops:
  9.0 7.0 %copy.27 = bf16[2,32,8448]{1,0,2:T(2,128)(2,1)} copy(bf16[2,32,8448]{2,1,0:T(8,128)(2,1)S(1)} %fusion.254) | data formatting | bytes 2162688 | tf_op jit(solution)/shard_map/convert_element_type | solution.py:55
  16.2 21.4 %gather_fusion = bf16[64,2,32,256]{2,1,3,0:T(2,128)(2,1)} fusion(bf16[2,32,8448]{1,0,2:T(2,128)(2,1)} %copy.27, s32[64]{0:T(128)S(1)} %fusion.397), kind=kCustom, calls=%fused_computation | custom fusion | bytes 4195072 | tf_op jit(solution)/shard_map/vmap()/gather | solution.py:57
  37.6 7.3 %fusion.278 = bf16[64,2,4,8,128]{4,3,2,1,0:T(8,128)(2,1)S(1)} fusion(bf16[64,2,32,256]{2,1,3,0:T(2,128)(2,1)} %gather_fusion, f32[64,128]{1,0:T(8,128)S(1)} %bitcast.152, f32[64,128]{1,0:T(8,128)S(1)} %bitcast.151, f32[64,128]{1,0:T(8,128)S(1)} %bitcast.150, f32[64,128]{1,0:T(8,128)S(1)} %bitcast.149, s32[64,128]{1,0:T(8,128)S(1)} %bitcast.154), kind=kOutput, calls=%fused_computation.235 | convolution fusion | flops 296222720 | bytes 3309568 | tf_op jit(solution)/shard_map/cnrw,cwk->nrck/dot_general | solution.py:69
  83.8 375.6 %while.14 = (s32[]{:T(128)}, bf16[8,2,32,1024]{3,2,1,0:T(8,128)(2,1)S(1)}, s32[8]{0:T(128)}, bf16[2,52,8448]{2,0,1:T(2,128)(2,1)}, f32[2,16,6]{1,2,0:T(8,128)S(1...) while((s32[]{:T(128)}, ...), condition=%wide.region_2.3_spmd.clone.clone, body=%wide.region_0.2_spmd.clone.clone.sunk | while | flops 1533191296 | bytes 60045232 | solution.py:140
  87.4 6.3 %fusion.435 = f32[2,52,8,16,128]{4,1,2,0,3:T(8,128)} fusion(f32[16]{0:T(128)} %get-tuple-element.2888, f32[16]{0:T(128)} %get-tuple-element.2886, f32[16]{0:T(128)} %get-tuple-element.2884, f32[16]{0:T(128)} %get-tuple-element.2882, f32[16]{0:T(128)} %get-tuple-element.2880, f32[16]{0:T(128)} %get-tuple-element.2878, f32[16]{0:T(128)} %get-tuple-element.2876, ...), kind=kOutput, calls=%fused_computation.18.clone.1 | convolution fusion | flops 447217664 | bytes 7374144 | tf_op jit(solution)/shard_map/while/body/eval_jaxpr/nsqw,wbk->nbsqk/dot_general | solution.py:115
  93.7 6.8 %fusion.436 = f32[2,52,8,16,128]{4,1,2,0,3:T(8,128)} fusion(f32[16]{0:T(128)} %get-tuple-element.2888, f32[16]{0:T(128)} %get-tuple-element.2886, f32[16]{0:T(128)} %get-tuple-element.2884, f32[16]{0:T(128)} %get-tuple-element.2882, f32[16]{0:T(128)} %get-tuple-element.2880, f32[16]{0:T(128)} %get-tuple-element.2878, f32[16]{0:T(128)} %get-tuple-element.2876, ...), kind=kOutput, calls=%fused_computation.20.clone.1 | convolution fusion | flops 447217664 | bytes 7374144 | tf_op jit(solution)/shard_map/while/body/eval_jaxpr/nsqw,wbk->nbsqk/dot_general | solution.py:115
  100.5 11.9 %fusion.437 = f32[2,16,32,8,128]{4,2,3,0,1:T(8,128)} fusion(f32[2,52,8,16,128]{4,1,2,0,3:T(8,128)} %fusion.435, f32[2,52,8,16,128]{4,1,2,0,3:T(8,128)} %fusion.436, f32[16]{0:T(128)} %get-tuple-element.2888, f32[16]{0:T(128)} %get-tuple-element.2886, f32[16]{0:T(128)} %get-tuple-element.2884, f32[16]{0:T(128)} %get-tuple-element.2882, ...), kind=kOutput, calls=%fused_computation.11.clone.1 | convolution fusion | flops 562499584 | bytes 18420480 | tf_op jit(solution)/shard_map/while/body/eval_jaxpr/bis,nbsqk->nbiqk/dot_general | solution.py:125
  112.4 6.5 %copy.69 = f32[2,16,32,8,128]{4,3,1,2,0:T(8,128)} copy(f32[2,16,32,8,128]{4,2,3,0,1:T(8,128)} %fusion.437) | data formatting | bytes 8388608 | tf_op jit(solution)/shard_map/while/body/eval_jaxpr/reshape | solution.py:128
  125.8 5.1 fusion.438
  134.3 6.3 %fusion.435 = f32[2,52,8,16,128]{4,1,2,0,3:T(8,128)} fusion(f32[16]{0:T(128)} %get-tuple-element.2888, f32[16]{0:T(128)} %get-tuple-element.2886, f32[16]{0:T(128)} %get-tuple-element.2884, f32[16]{0:T(128)} %get-tuple-element.2882, f32[16]{0:T(128)} %get-tuple-element.2880, f32[16]{0:T(128)} %get-tuple-element.2878, f32[16]{0:T(128)} %get-tuple-element.2876, ...), kind=kOutput, calls=%fused_computation.18.clone.1 | convolution fusion | flops 447217664 | bytes 7374144 | tf_op jit(solution)/shard_map/while/body/eval_jaxpr/nsqw,wbk->nbsqk/dot_general | solution.py:115
  140.6 6.7 %fusion.436 = f32[2,52,8,16,128]{4,1,2,0,3:T(8,128)} fusion(f32[16]{0:T(128)} %get-tuple-element.2888, f32[16]{0:T(128)} %get-tuple-element.2886, f32[16]{0:T(128)} %get-tuple-element.2884, f32[16]{0:T(128)} %get-tuple-element.2882, f32[16]{0:T(128)} %get-tuple-element.2880, f32[16]{0:T(128)} %get-tuple-element.2878, f32[16]{0:T(128)} %get-tuple-element.2876, ...), kind=kOutput, calls=%fused_computation.20.clone.1 | convolution fusion | flops 447217664 | bytes 7374144 | tf_op jit(solution)/shard_map/while/body/eval_jaxpr/nsqw,wbk->nbsqk/dot_general | solution.py:115
  147.4 11.9 %fusion.437 = f32[2,16,32,8,128]{4,2,3,0,1:T(8,128)} fusion(f32[2,52,8,16,128]{4,1,2,0,3:T(8,128)} %fusion.435, f32[2,52,8,16,128]{4,1,2,0,3:T(8,128)} %fusion.436, f32[16]{0:T(128)} %get-tuple-element.2888, f32[16]{0:T(128)} %get-tuple-element.2886, f32[16]{0:T(128)} %get-tuple-element.2884, f32[16]{0:T(128)} %get-tuple-element.2882, ...), kind=kOutput, calls=%fused_computation.11.clone.1 | convolution fusion | flops 562499584 | bytes 18420480 | tf_op jit(solution)/shard_map/while/body/eval_jaxpr/bis,nbsqk->nbiqk/dot_general | solution.py:125
  159.3 6.5 %copy.69 = f32[2,16,32,8,128]{4,3,1,2,0:T(8,128)} copy(f32[2,16,32,8,128]{4,2,3,0,1:T(8,128)} %fusion.437) | data formatting | bytes 8388608 | tf_op jit(solution)/shard_map/while/body/eval_jaxpr/reshape | solution.py:128
  165.9 4.9 reshape.719
  172.7 5.1 fusion.438
  181.2 6.3 %fusion.435 = f32[2,52,8,16,128]{4,1,2,0,3:T(8,128)} fusion(f32[16]{0:T(128)} %get-tuple-element.2888, f32[16]{0:T(128)} %get-tuple-element.2886, f32[16]{0:T(128)} %get-tuple-element.2884, f32[16]{0:T(128)} %get-tuple-element.2882, f32[16]{0:T(128)} %get-tuple-element.2880, f32[16]{0:T(128)} %get-tuple-element.2878, f32[16]{0:T(128)} %get-tuple-element.2876, ...), kind=kOutput, calls=%fused_computation.18.clone.1 | convolution fusion | flops 447217664 | bytes 7374144 | tf_op jit(solution)/shard_map/while/body/eval_jaxpr/nsqw,wbk->nbsqk/dot_general | solution.py:115
  187.5 6.7 %fusion.436 = f32[2,52,8,16,128]{4,1,2,0,3:T(8,128)} fusion(f32[16]{0:T(128)} %get-tuple-element.2888, f32[16]{0:T(128)} %get-tuple-element.2886, f32[16]{0:T(128)} %get-tuple-element.2884, f32[16]{0:T(128)} %get-tuple-element.2882, f32[16]{0:T(128)} %get-tuple-element.2880, f32[16]{0:T(128)} %get-tuple-element.2878, f32[16]{0:T(128)} %get-tuple-element.2876, ...), kind=kOutput, calls=%fused_computation.20.clone.1 | convolution fusion | flops 447217664 | bytes 7374144 | tf_op jit(solution)/shard_map/while/body/eval_jaxpr/nsqw,wbk->nbsqk/dot_general | solution.py:115
  194.3 11.9 %fusion.437 = f32[2,16,32,8,128]{4,2,3,0,1:T(8,128)} fusion(f32[2,52,8,16,128]{4,1,2,0,3:T(8,128)} %fusion.435, f32[2,52,8,16,128]{4,1,2,0,3:T(8,128)} %fusion.436, f32[16]{0:T(128)} %get-tuple-element.2888, f32[16]{0:T(128)} %get-tuple-element.2886, f32[16]{0:T(128)} %get-tuple-element.2884, f32[16]{0:T(128)} %get-tuple-element.2882, ...), kind=kOutput, calls=%fused_computation.11.clone.1 | convolution fusion | flops 562499584 | bytes 18420480 | tf_op jit(solution)/shard_map/while/body/eval_jaxpr/bis,nbsqk->nbiqk/dot_general | solution.py:125
  206.2 6.5 %copy.69 = f32[2,16,32,8,128]{4,3,1,2,0:T(8,128)} copy(f32[2,16,32,8,128]{4,2,3,0,1:T(8,128)} %fusion.437) | data formatting | bytes 8388608 | tf_op jit(solution)/shard_map/while/body/eval_jaxpr/reshape | solution.py:128
  212.7 4.9 reshape.719
  219.6 5.1 fusion.438
  228.1 6.3 %fusion.435 = f32[2,52,8,16,128]{4,1,2,0,3:T(8,128)} fusion(f32[16]{0:T(128)} %get-tuple-element.2888, f32[16]{0:T(128)} %get-tuple-element.2886, f32[16]{0:T(128)} %get-tuple-element.2884, f32[16]{0:T(128)} %get-tuple-element.2882, f32[16]{0:T(128)} %get-tuple-element.2880, f32[16]{0:T(128)} %get-tuple-element.2878, f32[16]{0:T(128)} %get-tuple-element.2876, ...), kind=kOutput, calls=%fused_computation.18.clone.1 | convolution fusion | flops 447217664 | bytes 7374144 | tf_op jit(solution)/shard_map/while/body/eval_jaxpr/nsqw,wbk->nbsqk/dot_general | solution.py:115
  234.4 6.7 %fusion.436 = f32[2,52,8,16,128]{4,1,2,0,3:T(8,128)} fusion(f32[16]{0:T(128)} %get-tuple-element.2888, f32[16]{0:T(128)} %get-tuple-element.2886, f32[16]{0:T(128)} %get-tuple-element.2884, f32[16]{0:T(128)} %get-tuple-element.2882, f32[16]{0:T(128)} %get-tuple-element.2880, f32[16]{0:T(128)} %get-tuple-element.2878, f32[16]{0:T(128)} %get-tuple-element.2876, ...), kind=kOutput, calls=%fused_computation.20.clone.1 | convolution fusion | flops 447217664 | bytes 7374144 | tf_op jit(solution)/shard_map/while/body/eval_jaxpr/nsqw,wbk->nbsqk/dot_general | solution.py:115
  241.2 11.9 %fusion.437 = f32[2,16,32,8,128]{4,2,3,0,1:T(8,128)} fusion(f32[2,52,8,16,128]{4,1,2,0,3:T(8,128)} %fusion.435, f32[2,52,8,16,128]{4,1,2,0,3:T(8,128)} %fusion.436, f32[16]{0:T(128)} %get-tuple-element.2888, f32[16]{0:T(128)} %get-tuple-element.2886, f32[16]{0:T(128)} %get-tuple-element.2884, f32[16]{0:T(128)} %get-tuple-element.2882, ...), kind=kOutput, calls=%fused_computation.11.clone.1 | convolution fusion | flops 562499584 | bytes 18420480 | tf_op jit(solution)/shard_map/while/body/eval_jaxpr/bis,nbsqk->nbiqk/dot_general | solution.py:125
  253.1 6.5 %copy.69 = f32[2,16,32,8,128]{4,3,1,2,0:T(8,128)} copy(f32[2,16,32,8,128]{4,2,3,0,1:T(8,128)} %fusion.437) | data formatting | bytes 8388608 | tf_op jit(solution)/shard_map/while/body/eval_jaxpr/reshape | solution.py:128
  259.6 4.9 reshape.719
  266.5 5.1 fusion.438
  275.0 6.3 %fusion.435 = f32[2,52,8,16,128]{4,1,2,0,3:T(8,128)} fusion(f32[16]{0:T(128)} %get-tuple-element.2888, f32[16]{0:T(128)} %get-tuple-element.2886, f32[16]{0:T(128)} %get-tuple-element.2884, f32[16]{0:T(128)} %get-tuple-element.2882, f32[16]{0:T(128)} %get-tuple-element.2880, f32[16]{0:T(128)} %get-tuple-element.2878, f32[16]{0:T(128)} %get-tuple-element.2876, ...), kind=kOutput, calls=%fused_computation.18.clone.1 | convolution fusion | flops 447217664 | bytes 7374144 | tf_op jit(solution)/shard_map/while/body/eval_jaxpr/nsqw,wbk->nbsqk/dot_general | solution.py:115
  281.3 6.7 %fusion.436 = f32[2,52,8,16,128]{4,1,2,0,3:T(8,128)} fusion(f32[16]{0:T(128)} %get-tuple-element.2888, f32[16]{0:T(128)} %get-tuple-element.2886, f32[16]{0:T(128)} %get-tuple-element.2884, f32[16]{0:T(128)} %get-tuple-element.2882, f32[16]{0:T(128)} %get-tuple-element.2880, f32[16]{0:T(128)} %get-tuple-element.2878, f32[16]{0:T(128)} %get-tuple-element.2876, ...), kind=kOutput, calls=%fused_computation.20.clone.1 | convolution fusion | flops 447217664 | bytes 7374144 | tf_op jit(solution)/shard_map/while/body/eval_jaxpr/nsqw,wbk->nbsqk/dot_general | solution.py:115
  288.0 11.9 %fusion.437 = f32[2,16,32,8,128]{4,2,3,0,1:T(8,128)} fusion(f32[2,52,8,16,128]{4,1,2,0,3:T(8,128)} %fusion.435, f32[2,52,8,16,128]{4,1,2,0,3:T(8,128)} %fusion.436, f32[16]{0:T(128)} %get-tuple-element.2888, f32[16]{0:T(128)} %get-tuple-element.2886, f32[16]{0:T(128)} %get-tuple-element.2884, f32[16]{0:T(128)} %get-tuple-element.2882, ...), kind=kOutput, calls=%fused_computation.11.clone.1 | convolution fusion | flops 562499584 | bytes 18420480 | tf_op jit(solution)/shard_map/while/body/eval_jaxpr/bis,nbsqk->nbiqk/dot_general | solution.py:125
  300.0 6.5 %copy.69 = f32[2,16,32,8,128]{4,3,1,2,0:T(8,128)} copy(f32[2,16,32,8,128]{4,2,3,0,1:T(8,128)} %fusion.437) | data formatting | bytes 8388608 | tf_op jit(solution)/shard_map/while/body/eval_jaxpr/reshape | solution.py:128
  313.4 5.1 fusion.438
  321.9 6.3 %fusion.435 = f32[2,52,8,16,128]{4,1,2,0,3:T(8,128)} fusion(f32[16]{0:T(128)} %get-tuple-element.2888, f32[16]{0:T(128)} %get-tuple-element.2886, f32[16]{0:T(128)} %get-tuple-element.2884, f32[16]{0:T(128)} %get-tuple-element.2882, f32[16]{0:T(128)} %get-tuple-element.2880, f32[16]{0:T(128)} %get-tuple-element.2878, f32[16]{0:T(128)} %get-tuple-element.2876, ...), kind=kOutput, calls=%fused_computation.18.clone.1 | convolution fusion | flops 447217664 | bytes 7374144 | tf_op jit(solution)/shard_map/while/body/eval_jaxpr/nsqw,wbk->nbsqk/dot_general | solution.py:115
  328.2 6.7 %fusion.436 = f32[2,52,8,16,128]{4,1,2,0,3:T(8,128)} fusion(f32[16]{0:T(128)} %get-tuple-element.2888, f32[16]{0:T(128)} %get-tuple-element.2886, f32[16]{0:T(128)} %get-tuple-element.2884, f32[16]{0:T(128)} %get-tuple-element.2882, f32[16]{0:T(128)} %get-tuple-element.2880, f32[16]{0:T(128)} %get-tuple-element.2878, f32[16]{0:T(128)} %get-tuple-element.2876, ...), kind=kOutput, calls=%fused_computation.20.clone.1 | convolution fusion | flops 447217664 | bytes 7374144 | tf_op jit(solution)/shard_map/while/body/eval_jaxpr/nsqw,wbk->nbsqk/dot_general | solution.py:115
  334.9 11.9 %fusion.437 = f32[2,16,32,8,128]{4,2,3,0,1:T(8,128)} fusion(f32[2,52,8,16,128]{4,1,2,0,3:T(8,128)} %fusion.435, f32[2,52,8,16,128]{4,1,2,0,3:T(8,128)} %fusion.436, f32[16]{0:T(128)} %get-tuple-element.2888, f32[16]{0:T(128)} %get-tuple-element.2886, f32[16]{0:T(128)} %get-tuple-element.2884, f32[16]{0:T(128)} %get-tuple-element.2882, ...), kind=kOutput, calls=%fused_computation.11.clone.1 | convolution fusion | flops 562499584 | bytes 18420480 | tf_op jit(solution)/shard_map/while/body/eval_jaxpr/bis,nbsqk->nbiqk/dot_general | solution.py:125
  346.9 6.5 %copy.69 = f32[2,16,32,8,128]{4,3,1,2,0:T(8,128)} copy(f32[2,16,32,8,128]{4,2,3,0,1:T(8,128)} %fusion.437) | data formatting | bytes 8388608 | tf_op jit(solution)/shard_map/while/body/eval_jaxpr/reshape | solution.py:128
  360.3 5.1 fusion.438
  368.7 6.3 %fusion.435 = f32[2,52,8,16,128]{4,1,2,0,3:T(8,128)} fusion(f32[16]{0:T(128)} %get-tuple-element.2888, f32[16]{0:T(128)} %get-tuple-element.2886, f32[16]{0:T(128)} %get-tuple-element.2884, f32[16]{0:T(128)} %get-tuple-element.2882, f32[16]{0:T(128)} %get-tuple-element.2880, f32[16]{0:T(128)} %get-tuple-element.2878, f32[16]{0:T(128)} %get-tuple-element.2876, ...), kind=kOutput, calls=%fused_computation.18.clone.1 | convolution fusion | flops 447217664 | bytes 7374144 | tf_op jit(solution)/shard_map/while/body/eval_jaxpr/nsqw,wbk->nbsqk/dot_general | solution.py:115
  375.1 6.7 %fusion.436 = f32[2,52,8,16,128]{4,1,2,0,3:T(8,128)} fusion(f32[16]{0:T(128)} %get-tuple-element.2888, f32[16]{0:T(128)} %get-tuple-element.2886, f32[16]{0:T(128)} %get-tuple-element.2884, f32[16]{0:T(128)} %get-tuple-element.2882, f32[16]{0:T(128)} %get-tuple-element.2880, f32[16]{0:T(128)} %get-tuple-element.2878, f32[16]{0:T(128)} %get-tuple-element.2876, ...), kind=kOutput, calls=%fused_computation.20.clone.1 | convolution fusion | flops 447217664 | bytes 7374144 | tf_op jit(solution)/shard_map/while/body/eval_jaxpr/nsqw,wbk->nbsqk/dot_general | solution.py:115
  381.8 11.9 %fusion.437 = f32[2,16,32,8,128]{4,2,3,0,1:T(8,128)} fusion(f32[2,52,8,16,128]{4,1,2,0,3:T(8,128)} %fusion.435, f32[2,52,8,16,128]{4,1,2,0,3:T(8,128)} %fusion.436, f32[16]{0:T(128)} %get-tuple-element.2888, f32[16]{0:T(128)} %get-tuple-element.2886, f32[16]{0:T(128)} %get-tuple-element.2884, f32[16]{0:T(128)} %get-tuple-element.2882, ...), kind=kOutput, calls=%fused_computation.11.clone.1 | convolution fusion | flops 562499584 | bytes 18420480 | tf_op jit(solution)/shard_map/while/body/eval_jaxpr/bis,nbsqk->nbiqk/dot_general | solution.py:125
  393.8 6.5 %copy.69 = f32[2,16,32,8,128]{4,3,1,2,0:T(8,128)} copy(f32[2,16,32,8,128]{4,2,3,0,1:T(8,128)} %fusion.437) | data formatting | bytes 8388608 | tf_op jit(solution)/shard_map/while/body/eval_jaxpr/reshape | solution.py:128
  407.1 5.1 fusion.438
  415.6 6.3 %fusion.435 = f32[2,52,8,16,128]{4,1,2,0,3:T(8,128)} fusion(f32[16]{0:T(128)} %get-tuple-element.2888, f32[16]{0:T(128)} %get-tuple-element.2886, f32[16]{0:T(128)} %get-tuple-element.2884, f32[16]{0:T(128)} %get-tuple-element.2882, f32[16]{0:T(128)} %get-tuple-element.2880, f32[16]{0:T(128)} %get-tuple-element.2878, f32[16]{0:T(128)} %get-tuple-element.2876, ...), kind=kOutput, calls=%fused_computation.18.clone.1 | convolution fusion | flops 447217664 | bytes 7374144 | tf_op jit(solution)/shard_map/while/body/eval_jaxpr/nsqw,wbk->nbsqk/dot_general | solution.py:115
  422.0 6.7 %fusion.436 = f32[2,52,8,16,128]{4,1,2,0,3:T(8,128)} fusion(f32[16]{0:T(128)} %get-tuple-element.2888, f32[16]{0:T(128)} %get-tuple-element.2886, f32[16]{0:T(128)} %get-tuple-element.2884, f32[16]{0:T(128)} %get-tuple-element.2882, f32[16]{0:T(128)} %get-tuple-element.2880, f32[16]{0:T(128)} %get-tuple-element.2878, f32[16]{0:T(128)} %get-tuple-element.2876, ...), kind=kOutput, calls=%fused_computation.20.clone.1 | convolution fusion | flops 447217664 | bytes 7374144 | tf_op jit(solution)/shard_map/while/body/eval_jaxpr/nsqw,wbk->nbsqk/dot_general | solution.py:115
  428.7 11.9 %fusion.437 = f32[2,16,32,8,128]{4,2,3,0,1:T(8,128)} fusion(f32[2,52,8,16,128]{4,1,2,0,3:T(8,128)} %fusion.435, f32[2,52,8,16,128]{4,1,2,0,3:T(8,128)} %fusion.436, f32[16]{0:T(128)} %get-tuple-element.2888, f32[16]{0:T(128)} %get-tuple-element.2886, f32[16]{0:T(128)} %get-tuple-element.2884, f32[16]{0:T(128)} %get-tuple-element.2882, ...), kind=kOutput, calls=%fused_computation.11.clone.1 | convolution fusion | flops 562499584 | bytes 18420480 | tf_op jit(solution)/shard_map/while/body/eval_jaxpr/bis,nbsqk->nbiqk/dot_general | solution.py:125
  440.6 6.5 %copy.69 = f32[2,16,32,8,128]{4,3,1,2,0:T(8,128)} copy(f32[2,16,32,8,128]{4,2,3,0,1:T(8,128)} %fusion.437) | data formatting | bytes 8388608 | tf_op jit(solution)/shard_map/while/body/eval_jaxpr/reshape | solution.py:128
  454.0 5.1 fusion.438
  467.2 143.2 %reduce-scatter.4.cloned.1.call-done = f32[1,2,32,128]{3,2,1,0:T(8,128)} async-done(((f32[64,2,32,128]{3,2,1,0:T(8,128)}), f32[1,2,32,128]{3,2,1,0:T(8,128)}) %reduce-scatter.4.cloned.1.call-update) | async-done | bytes 32784
  (235 shorter events, 111.5 us)
Async XLA Ops:
  6.5 1.3 copy-start
  6.5 9.5 %copy-start.17 = (s32[1,64]{1,0:T(1,128)S(1)}, s32[1,64]{1,0:T(1,128)}, u32[]{:S(2)}) copy-start(s32[1,64]{1,0:T(1,128)} %param.19) | copy-start | bytes 772
  6.5 9.5 %copy-start.2 = (bf16[1,4,8192]{2,1,0:T(4,128)(2,1)S(1)}, bf16[1,4,8192]{2,1,0:T(4,128)(2,1)}, u32[]{:S(2)}) copy-start(bf16[1,4,8192]{2,1,0:T(4,128)(2,1)} %param.18) | copy-start | bytes 196612
  6.5 603.9 %reduce-scatter.4.cloned.1.call-start = ((), (), s32[]{:S(2)}) async-start(), calls=%async_computation.1 | async-start | bytes 2129920
  9.0 28.5 %copy-start.16 = (s32[1,8192]{1,0:T(1,128)S(1)}, s32[1,8192]{1,0:T(1,128)}, u32[]{:S(2)}) copy-start(s32[1,8192]{1,0:T(1,128)} %param.17) | copy-start | bytes 98308
  44.9 7.4 %copy-start.11 = (bf16[16,21]{1,0:T(8,128)(2,1)S(1)}, bf16[16,21]{1,0:T(8,128)(2,1)}, u32[]{:S(2)}) copy-start(bf16[16,21]{1,0:T(8,128)(2,1)} %param.21) | copy-start | bytes 2020
  44.9 8.5 %copy-start.12 = (bf16[16,21]{1,0:T(8,128)(2,1)S(1)}, bf16[16,21]{1,0:T(8,128)(2,1)}, u32[]{:S(2)}) copy-start(bf16[16,21]{1,0:T(8,128)(2,1)} %param.20) | copy-start | bytes 2020
  44.9 31.4 %copy-start.18 = (s32[1,2]{1,0:T(1,128)S(1)}, s32[1,2]{1,0:T(1,128)}, u32[]{:S(2)}) copy-start(s32[1,2]{1,0:T(1,128)} %param.23) | copy-start | bytes 28
  45.0 32.4 %copy-start.3 = (s32[64,64]{1,0:T(8,128)S(1)}, s32[64,64]{1,0:T(8,128)}, u32[]{:S(2)}) copy-start(s32[64,64]{1,0:T(8,128)} %param.25) | copy-start | bytes 49156
  45.0 32.4 %copy-start.8 = (f32[64,2]{0,1:T(2,128)S(1)}, f32[64,2]{0,1:T(2,128)}, u32[]{:S(2)}) copy-start(f32[64,2]{0,1:T(2,128)} %param.24) | copy-start | bytes 1540
  46.3 32.0 %collective-permute-start = (bf16[2,10,8192]{2,1,0:T(8,128)(2,1)}, bf16[2,10,8192]{2,1,0:T(8,128)(2,1)S(1)}, u32[]{:S(2)}, u32[]{:S(2)}) collective-permute-start(bf16[2,10,8192]{2,1,0:T(8,128)(2,1)} %get-tuple-element.1667), channel_id=1, source_target_pairs={{0,1},{1,2},{2,3},{4,5},{5,6},{6,7},{8,9},{9,10},{10,11},{12,13},{... | collective-permute-start | bytes 983048 | tf_op jit(solution)/shard_map/ppermute | solution.py:15
  47.6 30.7 %collective-permute-start.1 = (bf16[2,10,8192]{2,1,0:T(8,128)(2,1)}, bf16[2,10,8192]{2,1,0:T(8,128)(2,1)S(1)}, u32[]{:S(2)}, u32[]{:S(2)}) collective-permute-start(bf16[2,10,8192]{2,1,0:T(8,128)(2,1)} %get-tuple-element.1668), channel_id=1, source_target_pairs={{1,0},{2,1},{3,2},{5,4},{6,5},{7,6},{9,8},{10,9},{11,10},{13,12},{... | collective-permute-start | bytes 983048 | tf_op jit(solution)/shard_map/ppermute | solution.py:17
  78.8 5.0 copy-start.5
  78.8 5.0 copy-start.6
  78.8 5.0 copy-start.7
  78.8 5.0 copy-start.13
  78.8 5.0 copy-start.14
  78.8 5.0 copy-start.15
  459.7 4.3 copy-start.10
  464.0 147.9 %copy-start.1 = (bf16[1,2,40,8448]{3,2,1,0:T(8,128)(2,1)S(1)}, bf16[1,2,40,8448]{3,2,1,0:T(8,128)(2,1)}, u32[]{:S(2)}) copy-start(bf16[1,2,40,8448]{3,2,1,0:T(8,128)(2,1)} %param.14) | copy-start | bytes 4055044
  464.3 2.6 copy-start.4
  464.3 2.6 copy-start.9
Sparse Core Ops, SparseCore 0:
  467.0 143.3 reduce-scatter.3
where the time goes:
time: 622 us; the launch traced here: 619 us
  matrix products  250 us (40%)
  local copies, waits for them, and re-layouts  172 us (28%)
  waiting for transfers between devices  143 us (23%)
  other arithmetic  26.2 us (4%)
  between operations  13.8 us (2%)
  loops' own time  6.67 us (1%)
    unnamed x2, waiting for transfers between devices  143 us
    dot_general x16, matrix products, one_group(): jnp.einsum('nsqw,wbk->nbsqk', piece[:, :, side:side + per_group], toeplit...  105 us
    dot_general x8, matrix products, one_group(): jnp.einsum('bis,nbsqk->nbiqk', toeplitz_rows, across, preferred_element_t...  95.4 us
    reshape x16, local copies, waits for them, and re-layouts, one_group(): smooth = smooth.reshape(band_count, basis_count, out_rows, group_width)  91.6 us
    dot_general x8, matrix products, one_group(): jnp.einsum('nbt,nbik->ntik', coefs, smooth, precision=lax.Precision.HIGHEST)  40.7 us
    gather x1, local copies, waits for them, and re-layouts, local(): lax.dynamic_slice_in_dim(rowres, first, 2 * block_width, 2)  21.4 us
    eq x32, other arithmetic, toeplitz(): lag == shift  14.4 us
    another operation x40, local copies, waits for them, and re-layouts, one_group(): jnp.stack([jnp.ones_like(xgrid), xgrid, ygrid, xgrid * xgrid, xgrid * ygr...  13.2 us
  transfers between devices with their start and end apart: 3, of which 1 were waited for; matrix products, arithmetic and copies ran while one was open for 4% of the time, Pallas kernels for 0%

commit v1 on v0

v1 whole, which is shorter than its diff:
```python
import jax
import jax.numpy as jnp
from jax import lax
from jax.sharding import PartitionSpec as P
from jax.experimental import pallas as pl
from jax.experimental.pallas import tpu as pltpu

F32 = jnp.float32
BF16 = jnp.bfloat16
HIGH = lax.Precision.HIGHEST

NB = 2
RB = 32
SR = 40
LANES = 128
ZN, XN, CN = 8, 4, 2
GROUP = XN * CN
GW = GROUP * LANES
HALO = 24
OR = RB + HALO
PR = NB * OR
HALF = LANES // 2


def iota(shape, dim):
    return lax.broadcasted_iota(jnp.int32, shape, dim)


def mm(a, b):
    return jnp.dot(a, b, preferred_element_type=F32)


def compute_kernel(
    off_ref,
    ids_ref,
    source_ref,
    row_start_ref,
    row_weight_ref,
    col_start_ref,
    col_weight_ref,
    g_ref,
    h_ref,
    coef_ref,
    weight_ref,
    cover_ref,
    keep_ref,
    send_ref,
    rowres_ref,
    shifted_ref,
    toep_ref,
    rows_ref,
    scale_ref,
    across_ref,
):
    visit = lax.axis_index("visit")
    band = lax.axis_index("band")
    core = visit % CN
    my_x = (visit // CN) % XN
    my_z = visit // GROUP
    taps = g_ref.shape[1]
    margin = taps // 2
    basis = g_ref.shape[0]
    blocks = off_ref.shape[1]
    width = blocks * LANES
    visits = cover_ref.shape[0]

    start = row_start_ref[...]
    weights = row_weight_ref[0].astype(F32)
    rel = iota((SR, RB), 0) - start
    picked = jnp.zeros((SR, RB), F32)
    for q in range(4):
        picked = jnp.where(rel == q, weights[q : q + 1, :], picked)
    picker = picked.T.astype(BF16)
    chunk = 2 * LANES

    def row_step(j, _):
        cols = pl.ds(pl.multiple_of(j * chunk, chunk), chunk)
        for n in range(NB):
            rowres_ref[n * RB : (n + 1) * RB, cols] = mm(
                picker, source_ref[0, n, :, cols]
            ).astype(BF16)
        return 0

    lax.fori_loop(0, rowres_ref.shape[1] // chunk, row_step, 0, unroll=3)

    low = iota((NB * RB, LANES), 1) < HALF
    tall = 3 * LANES
    tall_iota = iota((tall, LANES), 0)

    def col_step(c, before):
        first = pl.multiple_of(c * LANES, LANES)
        cols = pl.ds(first, LANES)
        at = col_start_ref[0:1, cols] + off_ref[0, c]
        wts = col_weight_ref[0, :, cols].astype(F32)
        rel = tall_iota - at
        spread = jnp.zeros((tall, LANES), F32)
        for q in range(4):
            spread = jnp.where(rel == q, wts[q : q + 1, :], spread)
        res = mm(rowres_ref[:, pl.ds(first, tall)], spread.astype(BF16))
        rolled = pltpu.roll(res, HALF, 1)
        shifted_ref[:, cols] = jnp.where(low, before, rolled).astype(BF16)
        return rolled

    last = lax.fori_loop(0, blocks, col_step, jnp.zeros((NB * RB, LANES), F32), unroll=4)
    shifted_ref[:, width : width + LANES] = jnp.where(low, last, 0.0).astype(BF16)

    tap = iota((2 * LANES, LANES), 0) - iota((2 * LANES, LANES), 1) - (HALF - margin)
    h_all = h_ref[...].astype(F32)
    for b in range(basis):
        acc = jnp.zeros((2 * LANES, LANES), F32)
        for t in range(taps):
            acc = jnp.where(tap == t, h_all[b : b + 1, t : t + 1], acc)
        toep_ref[:, b * LANES : (b + 1) * LANES] = acc.astype(BF16)

    span = basis * RB
    repeat = (iota((basis, span), 1) // RB == iota((basis, span), 0)).astype(F32)
    g_wide = jnp.dot(g_ref[...].astype(F32).T, repeat, precision=HIGH)
    place = iota((OR, span), 0)
    out_row = jnp.where(place < RB + margin, place, place - OR)
    tap = iota((OR, span), 1) % RB - out_row + margin
    valid = (place < RB + margin) | (place >= OR - margin)
    g_taps = jnp.zeros((OR, span), F32)
    for t in range(taps):
        g_taps = jnp.where(tap == t, g_wide[t : t + 1, :], g_taps)
    g_taps = jnp.where(valid, g_taps, 0.0)
    y = ((band * RB + out_row).astype(F32) + 0.5) * (2.0 / (RB * lax.axis_size("band"))) - 1.0
    for n in range(NB):
        table = coef_ref[ids_ref[0, n]]
        c = jnp.dot(table.T, repeat, precision=HIGH)
        in_x = [
            c[0:1] + c[2:3] * y + c[5:6] * (y * y),
            c[1:2] + c[4:5] * y,
            c[3:4] + jnp.zeros_like(y),
        ]
        for k in range(3):
            rows_ref[n, k * OR : (k + 1) * OR, :] = (g_taps * in_x[k]).astype(BF16)

    cover = cover_ref[...].astype(F32)
    mine = jnp.where(iota(cover.shape, 0) == visit, cover, 0.0)
    weight = weight_ref[...]
    dims = (((0,), (0,)), ((), ()))
    denom = lax.dot_general(cover, weight, dims, precision=HIGH)
    own = lax.dot_general(mine, weight, dims, precision=HIGH)
    factor = own / denom
    for n in range(NB):
        scale_ref[n] = jnp.broadcast_to(factor[:, n : n + 1], (visits, LANES))

    def group_step(rel_z, _):
        z = (my_z + rel_z) % ZN
        first = pl.multiple_of(z * GW, GW)
        lhs = jnp.concatenate(
            [shifted_ref[:, pl.ds(first + k * LANES, 2 * LANES)] for k in range(GROUP)], axis=0
        )
        for pair in range(basis // 2):
            res = mm(lhs, toep_ref[:, pair * 2 * LANES : (pair + 1) * 2 * LANES]).astype(BF16)
            for k in range(GROUP):
                for n in range(NB):
                    for b in range(2):
                        across_ref[
                            n,
                            (2 * pair + b) * RB : (2 * pair + b + 1) * RB,
                            k * LANES : (k + 1) * LANES,
                        ] = res[
                            (k * NB + n) * RB : (k * NB + n + 1) * RB,
                            b * LANES : (b + 1) * LANES,
                        ]
        for x in range(XN):
            lanes = slice(x * 2 * LANES, (x + 1) * 2 * LANES)
            col = (first + x * 2 * LANES + iota((1, 2 * LANES), 1)).astype(F32)
            xc = (col + 0.5) * (2.0 / width) - 1.0
            patch = z * GROUP + x * CN
            parts = []
            for n in range(NB):
                res = mm(rows_ref[n], across_ref[n, :, lanes])
                total = res[:OR] + xc * (res[OR : 2 * OR] + xc * res[2 * OR :])
                scale = jnp.concatenate(
                    [scale_ref[n, pl.ds(patch + c, 1), :] for c in range(CN)], axis=1
                )
                parts.append(total * scale)
            full = jnp.concatenate(
                [parts[0][:RB], parts[1][:RB], parts[0][RB:], parts[1][RB:]], axis=0
            )
            even, odd = full[:, :LANES], full[:, LANES:]
            slot = my_x ^ x
            keep_ref[rel_z, slot] = jnp.where(core == 0, even, odd).astype(BF16)
            send_ref[rel_z, slot] = jnp.where(core == 0, odd, even).astype(BF16)
        return 0

    lax.fori_loop(0, ZN, group_step, 0)


def ring(step):
    return [(i, step(i // GROUP, (i // CN) % XN, i % CN)) for i in range(ZN * GROUP)]


def at(z, x, c):
    return (z % ZN) * GROUP + x * CN + c


SIBLING = ring(lambda z, x, c: at(z, x, c ^ 1))
X_A = ring(lambda z, x, c: at(z, x ^ 1, c))
X_B = ring(lambda z, x, c: at(z, x ^ 3, c))
Z_UP = ring(lambda z, x, c: at(z + 1, x, c))
Z_DOWN = ring(lambda z, x, c: at(z - 1, x, c))


def final_kernel(own_ref, up_ref, down_ref, above_ref, below_ref, out_ref):
    total = own_ref[...] + up_ref[...] + down_ref[...]
    lanes = total.shape[1]
    row = iota((16, lanes), 0)
    for n in range(NB):
        rows = total[n * RB : (n + 1) * RB]
        over = above_ref[n * HALO : n * HALO + 16]
        under = below_ref[n * HALO + 8 : (n + 1) * HALO]
        out_ref[n, :16] = rows[:16] + jnp.where(row < 10, over, 0.0)
        out_ref[n, 16:] = rows[16:] + jnp.where(row >= 6, under, 0.0)


def local(
    source,
    row_start,
    row_weight,
    col_start,
    col_weight,
    col_offset,
    g_taps,
    h_taps,
    coef_table,
    table_ids,
    vis_weight,
    coverage,
):
    vmem = pl.BlockSpec(memory_space=pltpu.VMEM)
    smem = pl.BlockSpec(memory_space=pltpu.SMEM)
    basis = g_taps.shape[0]
    width = col_start.shape[1]
    half = jax.ShapeDtypeStruct((ZN, XN, PR, LANES), BF16)
    keep, send = pl.pallas_call(
        compute_kernel,
        out_shape=(half, half),
        in_specs=[smem, smem] + [vmem] * 10,
        out_specs=(vmem, vmem),
        scratch_shapes=[
            pltpu.VMEM((NB * RB, source.shape[3]), BF16),
            pltpu.VMEM((NB * RB, width + LANES), BF16),
            pltpu.VMEM((2 * LANES, basis * LANES), BF16),
            pltpu.VMEM((NB, 3 * OR, basis * RB), BF16),
            pltpu.VMEM((NB, coverage.shape[1], LANES), F32),
            pltpu.VMEM((NB, basis * RB, GW), BF16),
        ],
        compiler_params=pltpu.CompilerParams(vmem_limit_bytes=40 * 1024 * 1024),
    )(
        col_offset,
        table_ids,
        source,
        row_start,
        row_weight,
        col_start,
        col_weight,
        g_taps,
        h_taps,
        coef_table,
        vis_weight,
        coverage,
    )

    got = lax.ppermute(send, "visit", SIBLING)
    both = keep.astype(F32) + got.astype(F32)
    first, second = both[: ZN // 2], both[ZN // 2 :]
    send_a = jnp.stack([first[:, 1], first[:, 2]]).astype(BF16)
    send_b = jnp.stack([second[:, 3], second[:, 2]]).astype(BF16)
    got_a = lax.ppermute(send_a, "visit", X_A).astype(F32)
    got_b = lax.ppermute(send_b, "visit", X_B).astype(F32)
    send_2b = (first[:, 3] + got_a[1]).astype(BF16)
    send_2a = (second[:, 1] + got_b[1]).astype(BF16)
    got_2b = lax.ppermute(send_2b, "visit", X_B).astype(F32)
    got_2a = lax.ppermute(send_2a, "visit", X_A).astype(F32)
    plane = jnp.concatenate(
        [first[:, 0] + got_a[0] + got_2b, second[:, 0] + got_b[0] + got_2a], axis=0
    )

    up = lax.ppermute(plane[4], "visit", Z_UP)
    up = lax.ppermute(plane[3] + up, "visit", Z_UP)
    down = lax.ppermute(plane[5], "visit", Z_DOWN)
    up = lax.ppermute(plane[2] + up, "visit", Z_UP)
    down = lax.ppermute(plane[6] + down, "visit", Z_DOWN)
    up = lax.ppermute(plane[1] + up, "visit", Z_UP)
    down = lax.ppermute(plane[7] + down, "visit", Z_DOWN)
    own = plane[0]

    halo = own[NB * RB :] + up[NB * RB :] + down[NB * RB :]
    count = lax.axis_size("band")
    above = lax.ppermute(halo, "band", [(i, i + 1) for i in range(count - 1)])
    below = lax.ppermute(halo, "band", [(i + 1, i) for i in range(count - 1)])
    return pl.pallas_call(
        final_kernel,
        out_shape=jax.ShapeDtypeStruct((NB, RB, LANES), F32),
        in_specs=[vmem] * 5,
        out_specs=vmem,
    )(own[: NB * RB], up[: NB * RB], down[: NB * RB], above, below)


def solution(mesh):
    in_specs = (
        P("visit", None, "band", None),
        P("visit", "band"),
        P("visit", None, "band"),
        P("visit", None),
        P("visit", None, None),
        P("visit", None),
        P(),
        P(),
        P(),
        P("visit", None),
        P(),
        P(),
    )
    out_specs = P(None, "band", "visit")
    return jax.shard_map(local, mesh=mesh, in_specs=in_specs, out_specs=out_specs, check_vma=False)
```

time: 622 us -> 91 us (0.15)
  matrix products: 250 us -> 0 us
  local copies, waits for them, and re-layouts: 172 us -> 12 us
  waiting for transfers between devices: 143 us -> 30.5 us
  other arithmetic: 26.2 us -> 0.62 us
  Pallas kernels: 0 us -> 24 us
  starting transfers between devices: 6.04 us -> 23.1 us
  between operations: 13.8 us -> 0.17 us
  loops' own time: 6.67 us -> 0 us
    dot_general x36 -> x0, matrix products: 250 us -> none  [the longest x16 105 us: one_group(): jnp.einsum('nsqw,wbk->nbsqk', piece[:, :, side:side + per_group], toeplit...]
    unnamed x2 -> x0, waiting for transfers between devices: 143 us -> none
    reshape x24 -> x0, local copies, waits for them, and re-layouts: 93.1 us -> none  [the longest x16 91.6 us: one_group(): smooth = smooth.reshape(band_count, basis_count, out_rows, group_width)]
    ppermute x2 -> x14, waiting for transfers between devices: 0.01 us -> 30.5 us  [the longest x1 5.76 us: local(): got_b = lax.ppermute(send_b, 'visit', X_B).astype(F32)]
    pallas_call x0 -> x2, Pallas kernels: none -> 24 us  [the longest x1 22.6 us: local(): pl.pallas_call(compute_kernel, out_shape=(half, half), in_specs=[smem, sm...]
    gather x1 -> x0, local copies, waits for them, and re-layouts: 21.4 us -> none  [local(): lax.dynamic_slice_in_dim(rowres, first, 2 * block_width, 2)]
    eq x43 -> x0, other arithmetic: 21 us -> none  [the longest x32 14.4 us: toeplitz(): lag == shift]
    dynamic_slice x17 -> x0, local copies, waits for them, and re-layouts: 19.1 us -> none  [the longest x8 9.8 us: local(): grouped = lax.map(one_group, jnp.arange(group_count, dtype=jnp.int32))]
  transfers between devices with their start and end apart: 3 -> 14, of which waited for: 1 -> 9; matrix products, arithmetic and copies ran while one was open for 4% -> 2% of each run, Pallas kernels for 0% -> 0%
where the time goes in v1:
time: 91 us; the launch traced here: 90.5 us
  waiting for transfers between devices  30.5 us (34%)
  Pallas kernels  24 us (26%)
  starting transfers between devices  23.1 us (25%)
  local copies, waits for them, and re-layouts  12 us (13%)
    pallas_call x1, Pallas kernels, local(): pl.pallas_call(compute_kernel, out_shape=(half, half), in_specs=[smem, sm...  22.6 us
    unnamed x26, local copies, waits for them, and re-layouts  10 us
    ppermute x1, starting transfers between devices, local(): down = lax.ppermute(plane[5], 'visit', Z_DOWN)  5.93 us
    ppermute x1, waiting for transfers between devices, local(): got_b = lax.ppermute(send_b, 'visit', X_B).astype(F32)  5.76 us
    ppermute x1, waiting for transfers between devices, local(): up = lax.ppermute(plane[1] + up, 'visit', Z_UP)  5.36 us
    ppermute x1, waiting for transfers between devices, local(): up = lax.ppermute(plane[4], 'visit', Z_UP)  5.34 us
    ppermute x1, waiting for transfers between devices, local(): got_2a = lax.ppermute(send_2a, 'visit', X_A).astype(F32)  3.53 us
    ppermute x1, starting transfers between devices, local(): down = lax.ppermute(plane[6] + down, 'visit', Z_DOWN)  3.29 us
  transfers between devices with their start and end apart: 14, of which 9 were waited for; matrix products, arithmetic and copies ran while one was open for 2% of the time, Pallas kernels for 0%

profile of v1, /device:TPU:24, one launch (start us, length us, event | category | flops | bytes accessed | tf_op | source)
XLA Modules:
  0.0 90.5 jit_solution(9647415604930640475)
XLA Ops:
  0.0 0.8 copy.14.weight_ref
  0.8 1.0 %copy.13.coef_ref = f32[16,16,6]{2,1,0:T(8,128)S(1)} copy(f32[16,16,6]{1,0,2:T(8,128)} %param.20) | data formatting | bytes 12288 | tf_op args[8]
  1.7 1.3 %copy-done = bf16[1,2,40,8448]{3,2,1,0:T(8,128)(2,1)S(1)} copy-done((bf16[1,2,40,8448]{3,2,1,0:T(8,128)(2,1)S(1)}, bf16[1,2,40,8448]{3,2,1,0:T(8,128)(2,1)}, u32[]{:S(2)}) %copy-start) | copy-done | bytes 1351704
  3.1 0.8 copy-done.1
  3.9 0.8 copy-done.2
  4.7 0.8 copy-done.3
  5.4 0.7 copy-done.4
  6.1 0.7 copy-done.5
  6.8 0.7 copy-done.6
  7.5 0.7 copy-done.7
  8.1 0.7 copy-done.8
  8.8 0.7 copy-done.9
  9.4 22.6 %shard_map.118 = (bf16[8,4,112,128]{3,2,1,0:T(8,128)(2,1)S(1)}, bf16[8,4,112,128]{3,2,1,0:T(8,128)(2,1)S(1)}) custom-call(s32[1,64]{1,0:T(1,128)S(1)} %copy-done.7, s32[1,2]{1,0:T(1,128)S(1)} %copy-done.8, bf16[1,2,40,8448]{3,2,1,0:T(8,128)(2,1)S(1)} %copy-done, s32[1,32]{1,0:T(1,128)S(1)} %copy-done.9, bf16[1,4,32]{2,1,0:T(4,128)(2,1)S(1)} %copy-done.6, ...), custom_call_target="tpu_custom_call" | custom-call | tf_op jit(solution)/shard_map/pallas_call | solution.py:238
  32.0 0.1 copy.16
  32.1 0.1 collective-permute-start
  32.2 2.5 %collective-permute-done = bf16[8,4,112,128]{3,2,0,1:T(8,128)(2,1)S(1)} collective-permute-done((bf16[8,4,112,128]{3,2,0,1:T(8,128)(2,1)S(1)}, bf16[8,4,112,128]{3,2,0,1:T(8,128)(2,1)S(1)}, u32[]{:S(2)}, u32[]{:S(2)}) %collective-permute-start) | collective-permute-done | bytes 917536 | tf_op jit(solution)/shard_map/ppermute | solution.py:267
  34.7 0.3 convert_add_fusion
  35.0 2.8 %collective-permute-start.3 = (bf16[2,4,112,128]{3,2,1,0:T(8,128)(2,1)S(1)}, bf16[2,4,112,128]{3,2,1,0:T(8,128)(2,1)S(1)}, u32[]{:S(2)}, u32[]{:S(2)}) collective-permute-start(bf16[2,4,112,128]{3,2,1,0:T(8,128)(2,1)S(1)} %pad_maximum_fusion.1), channel_id=1, source_target_pairs={{0,24},{4,28},{8,16},{12,20},{16,8},{20,12},{24,0},{28,4},{32,56},... | collective-permute-start | bytes 688136 | tf_op jit(solution)/shard_map/ppermute | solution.py:273
  37.9 0.3 collective-permute-start.1
  38.2 5.8 %collective-permute-done.3 = bf16[2,4,112,128]{3,2,1,0:T(8,128)(2,1)S(1)} collective-permute-done((bf16[2,4,112,128]{3,2,1,0:T(8,128)(2,1)S(1)}, bf16[2,4,112,128]{3,2,1,0:T(8,128)(2,1)S(1)}, u32[]{:S(2)}, u32[]{:S(2)}) %collective-permute-start.3) | collective-permute-done | bytes 229408 | tf_op jit(solution)/shard_map/ppermute | solution.py:273
  44.1 0.4 collective-permute-start.4
  44.4 0.9 %collective-permute-done.1 = bf16[2,4,112,128]{3,2,1,0:T(8,128)(2,1)S(1)} collective-permute-done((bf16[2,4,112,128]{3,2,1,0:T(8,128)(2,1)S(1)}, bf16[2,4,112,128]{3,2,1,0:T(8,128)(2,1)S(1)}, u32[]{:S(2)}, u32[]{:S(2)}) %collective-permute-start.1) | collective-permute-done | bytes 229408 | tf_op jit(solution)/shard_map/ppermute | solution.py:272
  45.4 3.5 %collective-permute-done.4 = bf16[4,112,128]{2,1,0:T(8,128)(2,1)S(1)} collective-permute-done((bf16[4,112,128]{2,1,0:T(8,128)(2,1)S(1)}, bf16[4,112,128]{2,1,0:T(8,128)(2,1)S(1)}, u32[]{:S(2)}, u32[]{:S(2)}) %collective-permute-start.4) | collective-permute-done | bytes 114720 | tf_op jit(solution)/shard_map/ppermute | solution.py:277
  48.9 0.1 fusion.3
  49.0 2.8 %collective-permute-start.2 = (bf16[4,112,128]{2,1,0:T(8,128)(2,1)S(1)}, bf16[4,112,128]{2,1,0:T(8,128)(2,1)S(1)}, u32[]{:S(2)}, u32[]{:S(2)}) collective-permute-start(bf16[4,112,128]{2,1,0:T(8,128)(2,1)S(1)} %get-tuple-element.10), channel_id=1, source_target_pairs={{0,24},{4,28},{8,16},{12,20},{16,8},{20,12},{24,0},{28,4},{32,56},... | collective-permute-start | bytes 344072 | tf_op jit(solution)/shard_map/ppermute | solution.py:276
  51.9 5.9 %collective-permute-start.9 = (f32[112,128]{1,0:T(8,128)S(1)}, f32[112,128]{1,0:T(8,128)S(1)}, u32[]{:S(2)}, u32[]{:S(2)}) collective-permute-start(f32[112,128]{1,0:T(8,128)S(1)} %get-tuple-element.17), channel_id=1, source_target_pairs={{0,224},{4,228},{8,232},{12,236},{16,240},{20,244},{24,248},{28,25... | collective-permute-start | bytes 172040 | tf_op jit(solution)/shard_map/ppermute | solution.py:284
  57.8 0.0 collective-permute-start.5
  57.9 5.3 %collective-permute-done.5 = f32[112,128]{1,0:T(8,128)S(1)} collective-permute-done((f32[112,128]{1,0:T(8,128)S(1)}, f32[112,128]{1,0:T(8,128)S(1)}, u32[]{:S(2)}, u32[]{:S(2)}) %collective-permute-start.5) | collective-permute-done | bytes 57376 | tf_op jit(solution)/shard_map/ppermute | solution.py:282
  63.2 0.1 collective-permute-start.6
  63.3 0.0 collective-permute-done.9
  63.3 3.3 %collective-permute-start.10 = (f32[112,128]{1,0:T(8,128)S(1)}, f32[112,128]{1,0:T(8,128)S(1)}, u32[]{:S(2)}, u32[]{:S(2)}) collective-permute-start(f32[112,128]{1,0:T(8,128)S(1)} %fusion.8), channel_id=1, source_target_pairs={{0,224},{4,228},{8,232},{12,236},{16,240},{20,244},{24,248},{28,25... | collective-permute-start | bytes 172040 | tf_op jit(solution)/shard_map/ppermute | solution.py:286
  66.6 2.5 %collective-permute-done.6 = f32[112,128]{1,0:T(8,128)S(1)} collective-permute-done((f32[112,128]{1,0:T(8,128)S(1)}, f32[112,128]{1,0:T(8,128)S(1)}, u32[]{:S(2)}, u32[]{:S(2)}) %collective-permute-start.6) | collective-permute-done | bytes 57376 | tf_op jit(solution)/shard_map/ppermute | solution.py:283
  69.1 0.1 collective-permute-start.7
  69.2 0.0 collective-permute-done.10
  69.2 3.3 %collective-permute-start.11 = (f32[112,128]{1,0:T(8,128)S(1)}, f32[112,128]{1,0:T(8,128)S(1)}, u32[]{:S(2)}, u32[]{:S(2)}) collective-permute-start(f32[112,128]{1,0:T(8,128)S(1)} %fusion.9), channel_id=1, source_target_pairs={{0,224},{4,228},{8,232},{12,236},{16,240},{20,244},{24,248},{28,25... | collective-permute-start | bytes 172040 | tf_op jit(solution)/shard_map/ppermute | solution.py:288
  72.5 2.1 %collective-permute-done.7 = f32[112,128]{1,0:T(8,128)S(1)} collective-permute-done((f32[112,128]{1,0:T(8,128)S(1)}, f32[112,128]{1,0:T(8,128)S(1)}, u32[]{:S(2)}, u32[]{:S(2)}) %collective-permute-start.7) | collective-permute-done | bytes 57376 | tf_op jit(solution)/shard_map/ppermute | solution.py:285
  74.6 0.1 collective-permute-start.8
  74.7 0.0 collective-permute-done.11
  74.7 5.4 %collective-permute-done.8 = f32[112,128]{1,0:T(8,128)S(1)} collective-permute-done((f32[112,128]{1,0:T(8,128)S(1)}, f32[112,128]{1,0:T(8,128)S(1)}, u32[]{:S(2)}, u32[]{:S(2)}) %collective-permute-start.8) | collective-permute-done | bytes 57376 | tf_op jit(solution)/shard_map/ppermute | solution.py:287
  80.1 2.6 %collective-permute-start.13 = (f32[48,128]{1,0:T(8,128)S(1)}, f32[48,128]{1,0:T(8,128)S(1)}, u32[]{:S(2)}, u32[]{:S(2)}) collective-permute-start(f32[48,128]{1,0:T(8,128)S(1)} %slice_add_fusion), channel_id=1, source_target_pairs={{1,0},{2,1},{3,2},{5,4},{6,5},{7,6},{9,8},{10,9},{11,10},{13,12},{... | collective-permute-start | bytes 73736 | tf_op jit(solution)/shard_map/ppermute | solution.py:294
  82.7 1.3 %collective-permute-start.12 = (f32[48,128]{1,0:T(8,128)S(1)}, f32[48,128]{1,0:T(8,128)S(1)}, u32[]{:S(2)}, u32[]{:S(2)}) collective-permute-start(f32[48,128]{1,0:T(8,128)S(1)} %slice_add_fusion), channel_id=1, source_target_pairs={{0,1},{1,2},{2,3},{4,5},{5,6},{6,7},{8,9},{9,10},{10,11},{12,13},{... | collective-permute-start | bytes 73736 | tf_op jit(solution)/shard_map/ppermute | solution.py:293
  84.0 0.6 slice_bitcast_fusion.19.own_ref
  84.6 0.6 slice.146.down_ref
  85.2 0.6 slice.142.up_ref
  85.8 0.0 collective-permute-done.13.below_ref
  85.9 2.6 %collective-permute-done.12.above_ref = f32[48,128]{1,0:T(8,128)S(1)} collective-permute-done((f32[48,128]{1,0:T(8,128)S(1)}, f32[48,128]{1,0:T(8,128)S(1)}, u32[]{:S(2)}, u32[]{:S(2)}) %collective-permute-start.12) | collective-permute-done | bytes 24608 | tf_op jit(solution)/shard_map/ppermute | solution.py:293
  88.4 0.6 copy-done.11
  89.0 1.4 %shard_map.119 = f32[2,32,128]{2,1,0:T(8,128)} custom-call(f32[64,128]{1,0:T(8,128)} %slice_bitcast_fusion.19.own_ref, f32[64,128]{1,0:T(8,128)} %slice.142.up_ref, f32[64,128]{1,0:T(8,128)} %slice.146.down_ref, f32[48,128]{1,0:T(8,128)} %copy-done.11, f32[48,128]{1,0:T(8,128)} %copy-done.10), custom_call_target="tpu_custom_call" | custom-call | tf_op jit(solution)/shard_map/pallas_call | solution.py:295
  (28 shorter events, 0.3 us)
Async XLA Ops:
  1.7 1.3 %copy-start = (bf16[1,2,40,8448]{3,2,1,0:T(8,128)(2,1)S(1)}, bf16[1,2,40,8448]{3,2,1,0:T(8,128)(2,1)}, u32[]{:S(2)}) copy-start(bf16[1,2,40,8448]{3,2,1,0:T(8,128)(2,1)} %source_ref.1) | copy-start | bytes 4055044
  3.1 0.8 copy-start.1
  3.9 0.8 copy-start.2
  4.7 0.8 copy-start.3
  5.4 0.7 copy-start.4
  6.1 0.7 copy-start.5
  6.8 0.7 copy-start.6
  7.5 0.7 copy-start.7
  8.1 0.7 copy-start.8
  8.8 0.7 copy-start.9
  32.1 2.6 %collective-permute-start = (bf16[8,4,112,128]{3,2,0,1:T(8,128)(2,1)S(1)}, bf16[8,4,112,128]{3,2,0,1:T(8,128)(2,1)S(1)}, u32[]{:S(2)}, u32[]{:S(2)}) collective-permute-start(bf16[8,4,112,128]{3,2,0,1:T(8,128)(2,1)S(1)} %copy.16), channel_id=1, source_target_pairs={{0,4},{4,0},{8,12},{12,8},{16,20},{20,16},{24,28},{28,24},{32,36},... | collective-permute-start | bytes 2752520 | tf_op jit(solution)/shard_map/ppermute | solution.py:267
  35.0 8.9 %collective-permute-start.3 = (bf16[2,4,112,128]{3,2,1,0:T(8,128)(2,1)S(1)}, bf16[2,4,112,128]{3,2,1,0:T(8,128)(2,1)S(1)}, u32[]{:S(2)}, u32[]{:S(2)}) collective-permute-start(bf16[2,4,112,128]{3,2,1,0:T(8,128)(2,1)S(1)} %pad_maximum_fusion.1), channel_id=1, source_target_pairs={{0,24},{4,28},{8,16},{12,20},{16,8},{20,12},{24,0},{28,4},{32,56},... | collective-permute-start | bytes 688136 | tf_op jit(solution)/shard_map/ppermute | solution.py:273
  37.9 7.5 %collective-permute-start.1 = (bf16[2,4,112,128]{3,2,1,0:T(8,128)(2,1)S(1)}, bf16[2,4,112,128]{3,2,1,0:T(8,128)(2,1)S(1)}, u32[]{:S(2)}, u32[]{:S(2)}) collective-permute-start(bf16[2,4,112,128]{3,2,1,0:T(8,128)(2,1)S(1)} %pad_maximum_fusion), channel_id=1, source_target_pairs={{0,8},{4,12},{8,0},{12,4},{16,24},{20,28},{24,16},{28,20},{32,40},... | collective-permute-start | bytes 688136 | tf_op jit(solution)/shard_map/ppermute | solution.py:272
  44.1 4.9 %collective-permute-start.4 = (bf16[4,112,128]{2,1,0:T(8,128)(2,1)S(1)}, bf16[4,112,128]{2,1,0:T(8,128)(2,1)S(1)}, u32[]{:S(2)}, u32[]{:S(2)}) collective-permute-start(bf16[4,112,128]{2,1,0:T(8,128)(2,1)S(1)} %fusion.1), channel_id=1, source_target_pairs={{0,8},{4,12},{8,0},{12,4},{16,24},{20,28},{24,16},{28,20},{32,40},... | collective-permute-start | bytes 344072 | tf_op jit(solution)/shard_map/ppermute | solution.py:277
  49.0 8.8 %collective-permute-start.2 = (bf16[4,112,128]{2,1,0:T(8,128)(2,1)S(1)}, bf16[4,112,128]{2,1,0:T(8,128)(2,1)S(1)}, u32[]{:S(2)}, u32[]{:S(2)}) collective-permute-start(bf16[4,112,128]{2,1,0:T(8,128)(2,1)S(1)} %get-tuple-element.10), channel_id=1, source_target_pairs={{0,24},{4,28},{8,16},{12,20},{16,8},{20,12},{24,0},{28,4},{32,56},... | collective-permute-start | bytes 344072 | tf_op jit(solution)/shard_map/ppermute | solution.py:276
  51.9 11.4 %collective-permute-start.9 = (f32[112,128]{1,0:T(8,128)S(1)}, f32[112,128]{1,0:T(8,128)S(1)}, u32[]{:S(2)}, u32[]{:S(2)}) collective-permute-start(f32[112,128]{1,0:T(8,128)S(1)} %get-tuple-element.17), channel_id=1, source_target_pairs={{0,224},{4,228},{8,232},{12,236},{16,240},{20,244},{24,248},{28,25... | collective-permute-start | bytes 172040 | tf_op jit(solution)/shard_map/ppermute | solution.py:284
  57.8 5.4 %collective-permute-start.5 = (f32[112,128]{1,0:T(8,128)S(1)}, f32[112,128]{1,0:T(8,128)S(1)}, u32[]{:S(2)}, u32[]{:S(2)}) collective-permute-start(f32[112,128]{1,0:T(8,128)S(1)} %get-tuple-element.18), channel_id=1, source_target_pairs={{0,32},{4,36},{8,40},{12,44},{16,48},{20,52},{24,56},{28,60},{32,6... | collective-permute-start | bytes 172040 | tf_op jit(solution)/shard_map/ppermute | solution.py:282
  63.2 5.9 %collective-permute-start.6 = (f32[112,128]{1,0:T(8,128)S(1)}, f32[112,128]{1,0:T(8,128)S(1)}, u32[]{:S(2)}, u32[]{:S(2)}) collective-permute-start(f32[112,128]{1,0:T(8,128)S(1)} %fusion.10), channel_id=1, source_target_pairs={{0,32},{4,36},{8,40},{12,44},{16,48},{20,52},{24,56},{28,60},{32,6... | collective-permute-start | bytes 172040 | tf_op jit(solution)/shard_map/ppermute | solution.py:283
  63.3 5.9 %collective-permute-start.10 = (f32[112,128]{1,0:T(8,128)S(1)}, f32[112,128]{1,0:T(8,128)S(1)}, u32[]{:S(2)}, u32[]{:S(2)}) collective-permute-start(f32[112,128]{1,0:T(8,128)S(1)} %fusion.8), channel_id=1, source_target_pairs={{0,224},{4,228},{8,232},{12,236},{16,240},{20,244},{24,248},{28,25... | collective-permute-start | bytes 172040 | tf_op jit(solution)/shard_map/ppermute | solution.py:286
  69.1 5.5 %collective-permute-start.7 = (f32[112,128]{1,0:T(8,128)S(1)}, f32[112,128]{1,0:T(8,128)S(1)}, u32[]{:S(2)}, u32[]{:S(2)}) collective-permute-start(f32[112,128]{1,0:T(8,128)S(1)} %fusion.11), channel_id=1, source_target_pairs={{0,32},{4,36},{8,40},{12,44},{16,48},{20,52},{24,56},{28,60},{32,6... | collective-permute-start | bytes 172040 | tf_op jit(solution)/shard_map/ppermute | solution.py:285
  69.2 5.5 %collective-permute-start.11 = (f32[112,128]{1,0:T(8,128)S(1)}, f32[112,128]{1,0:T(8,128)S(1)}, u32[]{:S(2)}, u32[]{:S(2)}) collective-permute-start(f32[112,128]{1,0:T(8,128)S(1)} %fusion.9), channel_id=1, source_target_pairs={{0,224},{4,228},{8,232},{12,236},{16,240},{20,244},{24,248},{28,25... | collective-permute-start | bytes 172040 | tf_op jit(solution)/shard_map/ppermute | solution.py:288
  74.6 5.5 %collective-permute-start.8 = (f32[112,128]{1,0:T(8,128)S(1)}, f32[112,128]{1,0:T(8,128)S(1)}, u32[]{:S(2)}, u32[]{:S(2)}) collective-permute-start(f32[112,128]{1,0:T(8,128)S(1)} %fusion.12), channel_id=1, source_target_pairs={{0,32},{4,36},{8,40},{12,44},{16,48},{20,52},{24,56},{28,60},{32,6... | collective-permute-start | bytes 172040 | tf_op jit(solution)/shard_map/ppermute | solution.py:287
  80.1 5.8 %collective-permute-start.13 = (f32[48,128]{1,0:T(8,128)S(1)}, f32[48,128]{1,0:T(8,128)S(1)}, u32[]{:S(2)}, u32[]{:S(2)}) collective-permute-start(f32[48,128]{1,0:T(8,128)S(1)} %slice_add_fusion), channel_id=1, source_target_pairs={{1,0},{2,1},{3,2},{5,4},{6,5},{7,6},{9,8},{10,9},{11,10},{13,12},{... | collective-permute-start | bytes 73736 | tf_op jit(solution)/shard_map/ppermute | solution.py:294
  82.7 5.7 %collective-permute-start.12 = (f32[48,128]{1,0:T(8,128)S(1)}, f32[48,128]{1,0:T(8,128)S(1)}, u32[]{:S(2)}, u32[]{:S(2)}) collective-permute-start(f32[48,128]{1,0:T(8,128)S(1)} %slice_add_fusion), channel_id=1, source_target_pairs={{0,1},{1,2},{2,3},{4,5},{5,6},{6,7},{8,9},{9,10},{10,11},{12,13},{... | collective-permute-start | bytes 73736 | tf_op jit(solution)/shard_map/ppermute | solution.py:293
  85.9 2.6 %copy-start.10 = (f32[48,128]{1,0:T(8,128)}, f32[48,128]{1,0:T(8,128)S(1)}, u32[]{:S(2)}) copy-start(f32[48,128]{1,0:T(8,128)S(1)} %collective-permute-done.13.below_ref) | copy-start | bytes 73732
  88.4 0.6 copy-start.11

commit v2 on v1

v2 whole, which is shorter than its diff:
```python
import jax
import jax.numpy as jnp
from jax import lax
from jax.sharding import PartitionSpec as P
from jax.experimental import pallas as pl
from jax.experimental.pallas import tpu as pltpu

F32 = jnp.float32
BF16 = jnp.bfloat16
HIGH = lax.Precision.HIGHEST

NB = 2
RB = 32
SR = 40
LANES = 128
ZN, XN, CN = 8, 4, 2
GROUP = XN * CN
GW = GROUP * LANES
HALO = 24
OR = RB + HALO
PR = NB * OR
HALF = LANES // 2


def iota(shape, dim):
    return lax.broadcasted_iota(jnp.int32, shape, dim)


def mm(a, b):
    return jnp.dot(a, b, preferred_element_type=F32)


def compute_kernel(
    off_hbm,
    ids_hbm,
    source_hbm,
    row_start_hbm,
    row_weight_hbm,
    col_start_hbm,
    col_weight_hbm,
    g_hbm,
    h_hbm,
    coef_hbm,
    weight_hbm,
    cover_hbm,
    keep_ref,
    send_ref,
    off_ref,
    ids_ref,
    source_ref,
    row_start_ref,
    row_weight_ref,
    col_start_ref,
    col_weight_ref,
    g_ref,
    h_ref,
    coef_ref,
    weight_ref,
    cover_ref,
    rowres_ref,
    shifted_ref,
    toep_ref,
    rows_ref,
    scale_ref,
    across_ref,
    sems,
):
    pairs = [
        (h_hbm, h_ref),
        (g_hbm, g_ref),
        (coef_hbm, coef_ref),
        (ids_hbm, ids_ref),
        (weight_hbm, weight_ref),
        (cover_hbm, cover_ref),
        (row_start_hbm, row_start_ref),
        (row_weight_hbm, row_weight_ref),
        (source_hbm, source_ref),
        (off_hbm, off_ref),
        (col_start_hbm, col_start_ref),
        (col_weight_hbm, col_weight_ref),
    ]
    copies = [pltpu.make_async_copy(a, b, sems.at[i]) for i, (a, b) in enumerate(pairs)]
    for copy in copies:
        copy.start()
    visit = lax.axis_index("visit")
    band = lax.axis_index("band")
    core = visit % CN
    my_x = (visit // CN) % XN
    taps = g_ref.shape[1]
    margin = taps // 2
    basis = g_ref.shape[0]
    blocks = off_ref.shape[1]
    width = blocks * LANES
    visits = cover_ref.shape[0]

    for copy in copies[:6]:
        copy.wait()

    tap = iota((2 * LANES, LANES), 0) - iota((2 * LANES, LANES), 1) - (HALF - margin)
    h_all = h_ref[...].astype(F32)
    for b in range(basis):
        acc = jnp.zeros((2 * LANES, LANES), F32)
        for t in range(taps):
            acc = jnp.where(tap == t, h_all[b : b + 1, t : t + 1], acc)
        toep_ref[:, b * LANES : (b + 1) * LANES] = acc.astype(BF16)

    span = basis * RB
    repeat = (iota((basis, span), 1) // RB == iota((basis, span), 0)).astype(F32)
    g_wide = jnp.dot(g_ref[...].astype(F32).T, repeat, precision=HIGH)
    place = iota((OR, span), 0)
    out_row = jnp.where(place < RB + margin, place, place - OR)
    tap = iota((OR, span), 1) % RB - out_row + margin
    valid = (place < RB + margin) | (place >= OR - margin)
    g_taps = jnp.zeros((OR, span), F32)
    for t in range(taps):
        g_taps = jnp.where(tap == t, g_wide[t : t + 1, :], g_taps)
    g_taps = jnp.where(valid, g_taps, 0.0)
    y = ((band * RB + out_row).astype(F32) + 0.5) * (2.0 / (RB * lax.axis_size("band"))) - 1.0
    for n in range(NB):
        table = coef_ref[:, pl.ds(ids_ref[0, n], 1), :].reshape(coef_ref.shape[0], basis)
        c = jnp.dot(table, repeat, precision=HIGH)
        in_x = [
            c[0:1] + c[2:3] * y + c[5:6] * (y * y),
            c[1:2] + c[4:5] * y,
            c[3:4] + jnp.zeros_like(y),
        ]
        for k in range(3):
            rows_ref[n, k * OR : (k + 1) * OR, :] = (g_taps * in_x[k]).astype(BF16)

    cover = cover_ref[...].astype(F32)
    mine = jnp.where(iota(cover.shape, 0) == visit, cover, 0.0)
    weight = weight_ref[...]
    dims = (((0,), (1,)), ((), ()))
    denom = lax.dot_general(cover, weight, dims, precision=HIGH)
    own = lax.dot_general(mine, weight, dims, precision=HIGH)
    factor = own / denom
    for n in range(NB):
        scale_ref[n] = jnp.broadcast_to(factor[:, n : n + 1], (visits, LANES))

    for copy in copies[6:]:
        copy.wait()

    start = row_start_ref[...]
    weights = row_weight_ref[0].astype(F32)
    rel = iota((SR, RB), 0) - start
    picked = jnp.zeros((SR, RB), F32)
    for q in range(4):
        picked = jnp.where(rel == q, weights[q : q + 1, :], picked)
    picker = picked.T.astype(BF16)
    chunk = 2 * LANES

    def row_step(j, _):
        cols = pl.ds(pl.multiple_of(j * chunk, chunk), chunk)
        for n in range(NB):
            rowres_ref[n * RB : (n + 1) * RB, cols] = mm(
                picker, source_ref[0, n, :, cols]
            ).astype(BF16)
        return 0

    lax.fori_loop(0, rowres_ref.shape[1] // chunk, row_step, 0, unroll=3)

    low = iota((NB * RB, LANES), 1) < HALF
    tall = 3 * LANES
    tall_iota = iota((tall, LANES), 0)

    def col_step(c, before):
        first = pl.multiple_of(c * LANES, LANES)
        cols = pl.ds(first, LANES)
        at = col_start_ref[0:1, cols] + off_ref[0, c]
        wts = col_weight_ref[0, :, cols].astype(F32)
        rel = tall_iota - at
        spread = jnp.zeros((tall, LANES), F32)
        for q in range(4):
            spread = jnp.where(rel == q, wts[q : q + 1, :], spread)
        res = mm(rowres_ref[:, pl.ds(first, tall)], spread.astype(BF16))
        rolled = pltpu.roll(res, HALF, 1)
        shifted_ref[:, cols] = jnp.where(low, before, rolled).astype(BF16)
        return rolled

    last = lax.fori_loop(0, blocks, col_step, jnp.zeros((NB * RB, LANES), F32), unroll=4)
    shifted_ref[:, width : width + LANES] = jnp.where(low, last, 0.0).astype(BF16)

    def group_step(z, _):
        first = pl.multiple_of(z * GW, GW)
        lhs = jnp.concatenate(
            [shifted_ref[:, pl.ds(first + k * LANES, 2 * LANES)] for k in range(GROUP)], axis=0
        )
        for pair in range(basis // 2):
            res = mm(lhs, toep_ref[:, pair * 2 * LANES : (pair + 1) * 2 * LANES]).astype(BF16)
            for k in range(GROUP):
                for n in range(NB):
                    for b in range(2):
                        across_ref[
                            n,
                            (2 * pair + b) * RB : (2 * pair + b + 1) * RB,
                            k * LANES : (k + 1) * LANES,
                        ] = res[
                            (k * NB + n) * RB : (k * NB + n + 1) * RB,
                            b * LANES : (b + 1) * LANES,
                        ]
        for x in range(XN):
            lanes = slice(x * 2 * LANES, (x + 1) * 2 * LANES)
            col = (first + x * 2 * LANES + iota((1, 2 * LANES), 1)).astype(F32)
            xc = (col + 0.5) * (2.0 / width) - 1.0
            patch = z * GROUP + x * CN
            parts = []
            for n in range(NB):
                res = mm(rows_ref[n], across_ref[n, :, lanes])
                total = res[:OR] + xc * (res[OR : 2 * OR] + xc * res[2 * OR :])
                scale = jnp.concatenate(
                    [scale_ref[n, pl.ds(patch + c, 1), :] for c in range(CN)], axis=1
                )
                parts.append(total * scale)
            full = jnp.concatenate(
                [parts[0][:RB], parts[1][:RB], parts[0][RB:], parts[1][RB:]], axis=0
            )
            even, odd = full[:, :LANES], full[:, LANES:]
            slot = my_x ^ x
            keep_ref[slot, z] = jnp.where(core == 0, even, odd)
            send_ref[slot, z] = jnp.where(core == 0, odd, even).astype(BF16)
        return 0

    lax.fori_loop(0, ZN, group_step, 0)


def ring(step):
    return [(i, step(i // GROUP, (i // CN) % XN, i % CN)) for i in range(ZN * GROUP)]


def at(z, x, c):
    return (z % ZN) * GROUP + x * CN + c


SIBLING = ring(lambda z, x, c: at(z, x, c ^ 1))
ACROSS_X = [ring(lambda z, x, c, d=d: at(z, x ^ d, c)) for d in range(1, XN)]
ALONG_Z = [[at(z, x, c) for z in range(ZN)] for x in range(XN) for c in range(CN)]


def local(
    source,
    row_start,
    row_weight,
    col_start,
    col_weight,
    col_offset,
    g_taps,
    h_taps,
    coef_table,
    table_ids,
    vis_weight,
    coverage,
):
    basis = g_taps.shape[0]
    width = col_start.shape[1]
    operands = (
        col_offset,
        table_ids,
        source,
        row_start,
        row_weight,
        col_start,
        col_weight,
        g_taps,
        h_taps,
        coef_table.transpose(2, 0, 1),
        vis_weight.T,
        coverage,
    )
    vmem = pl.BlockSpec(memory_space=pltpu.VMEM)
    local_copies = [
        (pltpu.SMEM if k < 2 else pltpu.VMEM)(a.shape, a.dtype) for k, a in enumerate(operands)
    ]
    keep, send = pl.pallas_call(
        compute_kernel,
        out_shape=(
            jax.ShapeDtypeStruct((XN, ZN, PR, LANES), F32),
            jax.ShapeDtypeStruct((XN, ZN, PR, LANES), BF16),
        ),
        in_specs=[pl.BlockSpec(memory_space=pltpu.HBM)] * len(operands),
        out_specs=(vmem, vmem),
        scratch_shapes=local_copies
        + [
            pltpu.VMEM((NB * RB, source.shape[3]), BF16),
            pltpu.VMEM((NB * RB, width + LANES), BF16),
            pltpu.VMEM((2 * LANES, basis * LANES), BF16),
            pltpu.VMEM((NB, 3 * OR, basis * RB), BF16),
            pltpu.VMEM((NB, coverage.shape[1], LANES), F32),
            pltpu.VMEM((NB, basis * RB, GW), BF16),
            pltpu.SemaphoreType.DMA((len(operands),)),
        ],
        compiler_params=pltpu.CompilerParams(vmem_limit_bytes=40 * 1024 * 1024),
    )(*operands)

    got = lax.ppermute(send, "visit", SIBLING)
    both = keep + got.astype(F32)
    from_x = [
        lax.ppermute(both[d].astype(BF16), "visit", ACROSS_X[d - 1]) for d in range(1, XN)
    ]
    plane = both[0] + sum(part.astype(F32) for part in from_x)
    from_z = lax.all_to_all(
        plane.astype(BF16), "visit", 0, 0, axis_index_groups=ALONG_Z, tiled=True
    )

    halo = jnp.sum(from_z[:, NB * RB :].astype(F32), axis=0)
    count = lax.axis_size("band")
    band = lax.axis_index("band")
    above = lax.ppermute(halo, "band", [(i, (i + 1) % count) for i in range(count)])
    below = lax.ppermute(halo, "band", [((i + 1) % count, i) for i in range(count)])
    own = jnp.sum(from_z[:, : NB * RB].astype(F32), axis=0).reshape(NB, RB, LANES)
    above = above.reshape(NB, HALO, LANES)[:, :10]
    below = below.reshape(NB, HALO, LANES)[:, HALO - 10 :]
    above = jnp.pad(above, ((0, 0), (0, RB - 10), (0, 0)))
    below = jnp.pad(below, ((0, 0), (RB - 10, 0), (0, 0)))
    return own + jnp.where(band > 0, above, 0.0) + jnp.where(band < count - 1, below, 0.0)


def solution(mesh):
    in_specs = (
        P("visit", None, "band", None),
        P("visit", "band"),
        P("visit", None, "band"),
        P("visit", None),
        P("visit", None, None),
        P("visit", None),
        P(),
        P(),
        P(),
        P("visit", None),
        P(),
        P(),
    )
    out_specs = P(None, "band", "visit")
    return jax.shard_map(local, mesh=mesh, in_specs=in_specs, out_specs=out_specs, check_vma=False)
```

time: 91 us -> 78.5 us (0.86)
  starting transfers between devices: 23.1 us -> 15.4 us
  local copies, waits for them, and re-layouts: 12 us -> 9.23 us
  waiting for transfers between devices: 30.5 us -> 28.5 us
  Pallas kernels: 24 us -> 22.8 us
  other arithmetic: 0.62 us -> 1.76 us
    ppermute x13 -> x5, starting transfers between devices: 23.1 us -> 6.89 us  [the longest x3 4.79 us: local(): lax.ppermute(both[d].astype(BF16), 'visit', ACROSS_X[d - 1])]
    ppermute x13 -> x5, waiting for transfers between devices: 28.1 us -> 16 us  [the longest x3 12.8 us: local(): lax.ppermute(both[d].astype(BF16), 'visit', ACROSS_X[d - 1])]
    all_to_all x0 -> x1, waiting for transfers between devices: none -> 10.1 us  [local(): lax.all_to_all(plane.astype(BF16), 'visit', 0, 0, axis_index_groups=ALONG...]
    all_to_all x0 -> x1, starting transfers between devices: none -> 8.46 us  [local(): lax.all_to_all(plane.astype(BF16), 'visit', 0, 0, axis_index_groups=ALONG...]
    slice x3 -> x2, local copies, waits for them, and re-layouts: 1.84 us -> 0.01 us  [the longest x1 0.01 us: local(): below = below.reshape(NB, HALO, LANES)[:, HALO - 10:]]
    pallas_call x2 -> x1, Pallas kernels: 24 us -> 22.8 us  [local(): pl.pallas_call(compute_kernel, out_shape=(jax.ShapeDtypeStruct((XN, ZN, P...]
    unnamed x26 -> x24, local copies, waits for them, and re-layouts: 10 us -> 9.18 us
  transfers between devices with their start and end apart: 14 -> 7, of which waited for: 9 -> 7; matrix products, arithmetic and copies ran while one was open for 2% -> 0% of each run, Pallas kernels for 0% -> 0%
where the time goes in v2:
time: 78.5 us; the launch traced here: 77.8 us
  waiting for transfers between devices  28.5 us (36%)
  Pallas kernels  22.8 us (29%)
  starting transfers between devices  15.4 us (20%)
  local copies, waits for them, and re-layouts  9.23 us (12%)
  other arithmetic  1.76 us (2%)
    pallas_call x1, Pallas kernels, local(): pl.pallas_call(compute_kernel, out_shape=(jax.ShapeDtypeStruct((XN, ZN, P...  22.8 us
    ppermute x3, waiting for transfers between devices, local(): lax.ppermute(both[d].astype(BF16), 'visit', ACROSS_X[d - 1])  12.8 us
    all_to_all x1, waiting for transfers between devices, local(): lax.all_to_all(plane.astype(BF16), 'visit', 0, 0, axis_index_groups=ALONG...  10.1 us
    unnamed x24, local copies, waits for them, and re-layouts  9.18 us
    all_to_all x1, starting transfers between devices, local(): lax.all_to_all(plane.astype(BF16), 'visit', 0, 0, axis_index_groups=ALONG...  8.46 us
    ppermute x3, starting transfers between devices, local(): lax.ppermute(both[d].astype(BF16), 'visit', ACROSS_X[d - 1])  4.79 us
    ppermute x1, waiting for transfers between devices, local(): got = lax.ppermute(send, 'visit', SIBLING)  2.46 us
    ppermute x1, starting transfers between devices, local(): lax.ppermute(halo, 'band', [((i + 1) % count, i) for i in range(count)])  1.81 us
  transfers between devices with their start and end apart: 7, of which 7 were waited for; matrix products, arithmetic and copies ran while one was open for 0% of the time, Pallas kernels for 0%

profile of v2, /device:TPU:24, one launch (start us, length us, event | category | flops | bytes accessed | tf_op | source)
XLA Modules:
  0.0 77.8 jit_solution(2971244925479498657)
XLA Ops:
  0.0 0.0 copy-start
  0.0 1.3 %copy-done = bf16[1,2,40,8448]{3,2,1,0:T(8,128)(2,1)S(1)} copy-done((bf16[1,2,40,8448]{3,2,1,0:T(8,128)(2,1)S(1)}, bf16[1,2,40,8448]{3,2,1,0:T(8,128)(2,1)}, u32[]{:S(2)}) %copy-start) | copy-done | bytes 1351704
  1.3 0.0 copy-start.1
  1.3 0.8 %copy-done.1 = bf16[1,4,8192]{2,1,0:T(4,128)(2,1)S(1)} copy-done((bf16[1,4,8192]{2,1,0:T(4,128)(2,1)S(1)}, bf16[1,4,8192]{2,1,0:T(4,128)(2,1)}, u32[]{:S(2)}) %copy-start.1) | copy-done | bytes 65560
  2.2 0.0 copy-start.2
  2.2 0.8 %copy-done.2 = f32[16,16,6]{1,0,2:T(8,128)S(1)} copy-done((f32[16,16,6]{1,0,2:T(8,128)S(1)}, f32[16,16,6]{1,0,2:T(8,128)}, u32[]{:S(2)}) %copy-start.2) | copy-done | bytes 6168
  3.0 0.0 copy-start.3
  3.0 0.8 copy-done.3
  3.7 0.0 copy-start.4
  3.7 0.8 copy-done.4
  4.5 0.0 copy-start.5
  4.5 0.7 copy-done.5
  5.2 0.0 copy-start.6
  5.2 0.7 copy-done.6
  5.9 0.0 copy-start.7
  5.9 0.7 copy-done.7
  6.5 0.0 copy-start.8
  6.5 0.7 copy-done.8
  7.2 0.0 copy-start.9
  7.2 0.7 copy-done.9
  7.9 0.0 copy-start.10
  7.9 0.7 copy-done.10
  8.5 0.0 copy-start.11
  8.5 0.7 copy-done.11
  9.2 22.8 %shard_map.118 = (f32[4,8,112,128]{3,2,1,0:T(8,128)S(1)}, bf16[4,8,112,128]{3,2,1,0:T(8,128)(2,1)S(1)}) custom-call(s32[1,64]{1,0:T(1,128)S(1)} %copy-done.9, s32[1,2]{1,0:T(1,128)S(1)} %copy-done.10, bf16[1,2,40,8448]{3,2,1,0:T(8,128)(2,1)S(1)} %copy-done, s32[1,32]{1,0:T(1,128)S(1)} %copy-done.11, bf16[1,4,32]{2,1,0:T(4,128)(2,1)S(1)} %copy-done.7, ...), custom_call_target="tpu_custom_call" | custom-call | tf_op jit(solution)/shard_map/pallas_call | solution.py:273
  32.0 0.1 collective-permute-start
  32.1 2.5 %collective-permute-done = bf16[4,8,112,128]{3,2,1,0:T(8,128)(2,1)S(1)} collective-permute-done((bf16[4,8,112,128]{3,2,1,0:T(8,128)(2,1)S(1)}, bf16[4,8,112,128]{3,2,1,0:T(8,128)(2,1)S(1)}, u32[]{:S(2)}, u32[]{:S(2)}) %collective-permute-start) | collective-permute-done | bytes 917536 | tf_op jit(solution)/shard_map/ppermute | solution.py:294
  34.6 0.3 fusion.2
  34.9 1.6 %collective-permute-start.1 = (bf16[8,112,128]{2,1,0:T(8,128)(2,1)S(1)}, bf16[8,112,128]{2,1,0:T(8,128)(2,1)S(1)}, u32[]{:S(2)}, u32[]{:S(2)}) collective-permute-start(bf16[8,112,128]{2,1,0:T(8,128)(2,1)S(1)} %get-tuple-element.11), channel_id=1, source_target_pairs={{0,8},{4,12},{8,0},{12,4},{16,24},{20,28},{24,16},{28,20},{32,40},... | collective-permute-start | bytes 688136 | tf_op jit(solution)/shard_map/ppermute | solution.py:297
  36.5 2.7 %collective-permute-start.2 = (bf16[8,112,128]{2,1,0:T(8,128)(2,1)S(1)}, bf16[8,112,128]{2,1,0:T(8,128)(2,1)S(1)}, u32[]{:S(2)}, u32[]{:S(2)}) collective-permute-start(bf16[8,112,128]{2,1,0:T(8,128)(2,1)S(1)} %get-tuple-element.13), channel_id=1, source_target_pairs={{0,16},{4,20},{8,24},{12,28},{16,0},{20,4},{24,8},{28,12},{32,48},... | collective-permute-start | bytes 688136 | tf_op jit(solution)/shard_map/ppermute | solution.py:297
  39.2 0.5 collective-permute-start.3
  39.7 3.7 %collective-permute-done.1 = bf16[8,112,128]{2,1,0:T(8,128)(2,1)S(1)} collective-permute-done((bf16[8,112,128]{2,1,0:T(8,128)(2,1)S(1)}, bf16[8,112,128]{2,1,0:T(8,128)(2,1)S(1)}, u32[]{:S(2)}, u32[]{:S(2)}) %collective-permute-start.1) | collective-permute-done | bytes 229408 | tf_op jit(solution)/shard_map/ppermute | solution.py:297
  43.4 6.4 %collective-permute-done.2 = bf16[8,112,128]{2,1,0:T(8,128)(2,1)S(1)} collective-permute-done((bf16[8,112,128]{2,1,0:T(8,128)(2,1)S(1)}, bf16[8,112,128]{2,1,0:T(8,128)(2,1)S(1)}, u32[]{:S(2)}, u32[]{:S(2)}) %collective-permute-start.2) | collective-permute-done | bytes 229408 | tf_op jit(solution)/shard_map/ppermute | solution.py:297
  49.9 2.6 %collective-permute-done.3 = bf16[8,112,128]{2,1,0:T(8,128)(2,1)S(1)} collective-permute-done((bf16[8,112,128]{2,1,0:T(8,128)(2,1)S(1)}, bf16[8,112,128]{2,1,0:T(8,128)(2,1)S(1)}, u32[]{:S(2)}, u32[]{:S(2)}) %collective-permute-start.3) | collective-permute-done | bytes 229408 | tf_op jit(solution)/shard_map/ppermute | solution.py:297
  52.4 0.8 %fusion.1 = bf16[8,112,128]{2,1,0:T(8,128)(2,1)} fusion(f32[4,8,112,128]{3,2,1,0:T(8,128)S(1)} %get-tuple-element.10, bf16[8,112,128]{2,1,0:T(8,128)(2,1)S(1)} %collective-permute-done.3, bf16[8,112,128]{2,1,0:T(8,128)(2,1)S(1)} %collective-permute-done.2, bf16[8,112,128]{2,1,0:T(8,128)(2,1)S(1)} %collective-permute-done.1), kind=kLoop, calls=%fused_computation.3 | loop fusion | flops 802816 | bytes 1376256 | tf_op jit(solution)/shard_map/convert_element_type | solution.py:301
  53.2 8.5 %all-to-all-start = ((bf16[8,112,128]{2,1,0:T(8,128)(2,1)}), bf16[8,112,128]{2,1,0:T(8,128)(2,1)S(1)}, u32[]{:S(2)}, u32[]{:S(2)}) async-start(bf16[8,112,128]{2,1,0:T(8,128)(2,1)} %fusion.1), calls=%async_computation | async-start | bytes 458752 | tf_op jit(solution)/shard_map/all_to_all | solution.py:300
  61.7 10.1 %all-to-all-done = bf16[8,112,128]{2,1,0:T(8,128)(2,1)S(1)} async-done(((bf16[8,112,128]{2,1,0:T(8,128)(2,1)}), bf16[8,112,128]{2,1,0:T(8,128)(2,1)S(1)}, u32[]{:S(2)}, u32[]{:S(2)}) %all-to-all-start) | async-done | bytes 229408 | tf_op jit(solution)/shard_map/all_to_all | solution.py:300
  71.9 0.3 collective-permute-start.4
  72.2 1.8 %collective-permute-start.5 = (f32[48,128]{1,0:T(8,128)S(1)}, f32[48,128]{1,0:T(8,128)S(1)}, u32[]{:S(2)}, u32[]{:S(2)}) collective-permute-start(f32[48,128]{1,0:T(8,128)S(1)} %convert_reduce_fusion.1), channel_id=1, source_target_pairs={{1,0},{2,1},{3,2},{0,3},{5,4},{6,5},{7,6},{4,7},{9,8},{10,9},{11,1... | collective-permute-start | bytes 73736 | tf_op jit(solution)/shard_map/ppermute | solution.py:308
  74.0 1.8 %collective-permute-done.4 = f32[48,128]{1,0:T(8,128)S(1)} collective-permute-done((f32[48,128]{1,0:T(8,128)S(1)}, f32[48,128]{1,0:T(8,128)S(1)}, u32[]{:S(2)}, u32[]{:S(2)}) %collective-permute-start.4) | collective-permute-done | bytes 24608 | tf_op jit(solution)/shard_map/ppermute | solution.py:307
  75.8 1.4 %collective-permute-done.5 = f32[48,128]{1,0:T(8,128)S(1)} collective-permute-done((f32[48,128]{1,0:T(8,128)S(1)}, f32[48,128]{1,0:T(8,128)S(1)}, u32[]{:S(2)}, u32[]{:S(2)}) %collective-permute-start.5) | collective-permute-done | bytes 24608 | tf_op jit(solution)/shard_map/ppermute | solution.py:308
  77.2 0.6 select_add_fusion
  (5 shorter events, 0.1 us)
Async XLA Ops:
  0.0 1.3 %copy-start = (bf16[1,2,40,8448]{3,2,1,0:T(8,128)(2,1)S(1)}, bf16[1,2,40,8448]{3,2,1,0:T(8,128)(2,1)}, u32[]{:S(2)}) copy-start(bf16[1,2,40,8448]{3,2,1,0:T(8,128)(2,1)} %source_hbm.1) | copy-start | bytes 4055044
  1.3 0.8 %copy-start.1 = (bf16[1,4,8192]{2,1,0:T(4,128)(2,1)S(1)}, bf16[1,4,8192]{2,1,0:T(4,128)(2,1)}, u32[]{:S(2)}) copy-start(bf16[1,4,8192]{2,1,0:T(4,128)(2,1)} %col_weight_hbm.1) | copy-start | bytes 196612
  2.2 0.8 %copy-start.2 = (f32[16,16,6]{1,0,2:T(8,128)S(1)}, f32[16,16,6]{1,0,2:T(8,128)}, u32[]{:S(2)}) copy-start(f32[16,16,6]{1,0,2:T(8,128)} %param.20) | copy-start | bytes 18436
  3.0 0.8 copy-start.3
  3.7 0.8 copy-start.4
  4.5 0.7 copy-start.5
  5.2 0.7 copy-start.6
  5.9 0.7 copy-start.7
  6.5 0.7 copy-start.8
  7.2 0.7 copy-start.9
  7.9 0.7 copy-start.10
  8.5 0.7 copy-start.11
  32.0 2.6 %collective-permute-start = (bf16[4,8,112,128]{3,2,1,0:T(8,128)(2,1)S(1)}, bf16[4,8,112,128]{3,2,1,0:T(8,128)(2,1)S(1)}, u32[]{:S(2)}, u32[]{:S(2)}) collective-permute-start(bf16[4,8,112,128]{3,2,1,0:T(8,128)(2,1)S(1)} %get-tuple-element.8), channel_id=1, source_target_pairs={{0,4},{4,0},{8,12},{12,8},{16,20},{20,16},{24,28},{28,24},{32,36},... | collective-permute-start | bytes 2752520 | tf_op jit(solution)/shard_map/ppermute | solution.py:294
  34.9 8.5 %collective-permute-start.1 = (bf16[8,112,128]{2,1,0:T(8,128)(2,1)S(1)}, bf16[8,112,128]{2,1,0:T(8,128)(2,1)S(1)}, u32[]{:S(2)}, u32[]{:S(2)}) collective-permute-start(bf16[8,112,128]{2,1,0:T(8,128)(2,1)S(1)} %get-tuple-element.11), channel_id=1, source_target_pairs={{0,8},{4,12},{8,0},{12,4},{16,24},{20,28},{24,16},{28,20},{32,40},... | collective-permute-start | bytes 688136 | tf_op jit(solution)/shard_map/ppermute | solution.py:297
  36.5 13.4 %collective-permute-start.2 = (bf16[8,112,128]{2,1,0:T(8,128)(2,1)S(1)}, bf16[8,112,128]{2,1,0:T(8,128)(2,1)S(1)}, u32[]{:S(2)}, u32[]{:S(2)}) collective-permute-start(bf16[8,112,128]{2,1,0:T(8,128)(2,1)S(1)} %get-tuple-element.13), channel_id=1, source_target_pairs={{0,16},{4,20},{8,24},{12,28},{16,0},{20,4},{24,8},{28,12},{32,48},... | collective-permute-start | bytes 688136 | tf_op jit(solution)/shard_map/ppermute | solution.py:297
  39.2 13.2 %collective-permute-start.3 = (bf16[8,112,128]{2,1,0:T(8,128)(2,1)S(1)}, bf16[8,112,128]{2,1,0:T(8,128)(2,1)S(1)}, u32[]{:S(2)}, u32[]{:S(2)}) collective-permute-start(bf16[8,112,128]{2,1,0:T(8,128)(2,1)S(1)} %get-tuple-element.12), channel_id=1, source_target_pairs={{0,24},{4,28},{8,16},{12,20},{16,8},{20,12},{24,0},{28,4},{32,56},... | collective-permute-start | bytes 688136 | tf_op jit(solution)/shard_map/ppermute | solution.py:297
  53.2 18.6 %all-to-all-start = ((bf16[8,112,128]{2,1,0:T(8,128)(2,1)}), bf16[8,112,128]{2,1,0:T(8,128)(2,1)S(1)}, u32[]{:S(2)}, u32[]{:S(2)}) async-start(bf16[8,112,128]{2,1,0:T(8,128)(2,1)} %fusion.1), calls=%async_computation | async-start | bytes 458752 | tf_op jit(solution)/shard_map/all_to_all | solution.py:300
  71.9 3.9 %collective-permute-start.4 = (f32[48,128]{1,0:T(8,128)S(1)}, f32[48,128]{1,0:T(8,128)S(1)}, u32[]{:S(2)}, u32[]{:S(2)}) collective-permute-start(f32[48,128]{1,0:T(8,128)S(1)} %convert_reduce_fusion.1), channel_id=1, source_target_pairs={{0,1},{1,2},{2,3},{3,0},{4,5},{5,6},{6,7},{7,4},{8,9},{9,10},{10,1... | collective-permute-start | bytes 73736 | tf_op jit(solution)/shard_map/ppermute | solution.py:307
  72.2 5.0 %collective-permute-start.5 = (f32[48,128]{1,0:T(8,128)S(1)}, f32[48,128]{1,0:T(8,128)S(1)}, u32[]{:S(2)}, u32[]{:S(2)}) collective-permute-start(f32[48,128]{1,0:T(8,128)S(1)} %convert_reduce_fusion.1), channel_id=1, source_target_pairs={{1,0},{2,1},{3,2},{0,3},{5,4},{6,5},{7,6},{4,7},{9,8},{10,9},{11,1... | collective-permute-start | bytes 73736 | tf_op jit(solution)/shard_map/ppermute | solution.py:308

commit v3 on v2

v3 whole, which is shorter than its diff:
```python
import jax
import jax.numpy as jnp
from jax import lax
from jax.sharding import PartitionSpec as P
from jax.experimental import pallas as pl
from jax.experimental.pallas import tpu as pltpu

F32 = jnp.float32
I16 = jnp.int16
BF16 = jnp.bfloat16
HIGH = lax.Precision.HIGHEST

NB = 2
RB = 32
SR = 40
LANES = 128
ZN, XN, CN = 8, 4, 2
GROUP = XN * CN
GW = GROUP * LANES
HALO = 24
OR = RB + HALO
PR = NB * OR
HALF = LANES // 2


def iota(shape, dim):
    return lax.broadcasted_iota(jnp.int32, shape, dim)


def mm(a, b):
    return jnp.dot(a, b, preferred_element_type=F32)


def filter_groups(
    first_z, keep_ref, send_ref, shifted_ref, toep_ref, rows_ref, scale_ref, across_ref
):
    visit = lax.axis_index("visit")
    core = visit % CN
    my_x = (visit // CN) % XN
    basis = toep_ref.shape[1] // LANES
    width = shifted_ref.shape[1] - LANES

    def group_step(place, _):
        z = place + first_z
        first = pl.multiple_of(z * GW, GW)
        lhs = jnp.concatenate(
            [shifted_ref[:, pl.ds(first + k * LANES, 2 * LANES)] for k in range(GROUP)], axis=0
        )
        for pair in range(basis // 2):
            res = mm(lhs, toep_ref[:, pair * 2 * LANES : (pair + 1) * 2 * LANES]).astype(BF16)
            for k in range(GROUP):
                for n in range(NB):
                    for b in range(2):
                        across_ref[
                            n,
                            (2 * pair + b) * RB : (2 * pair + b + 1) * RB,
                            k * LANES : (k + 1) * LANES,
                        ] = res[
                            (k * NB + n) * RB : (k * NB + n + 1) * RB,
                            b * LANES : (b + 1) * LANES,
                        ]
        for x in range(XN):
            lanes = slice(x * 2 * LANES, (x + 1) * 2 * LANES)
            col = (first + x * 2 * LANES + iota((1, 2 * LANES), 1)).astype(F32)
            xc = (col + 0.5) * (2.0 / width) - 1.0
            patch = z * GROUP + x * CN
            parts = []
            for n in range(NB):
                res = mm(rows_ref[n], across_ref[n, :, lanes])
                total = res[:OR] + xc * (res[OR : 2 * OR] + xc * res[2 * OR :])
                scale = jnp.concatenate(
                    [scale_ref[n, pl.ds(patch + c, 1), :] for c in range(CN)], axis=1
                )
                parts.append(total * scale)
            full = jnp.concatenate(
                [parts[0][:RB], parts[1][:RB], parts[0][RB:], parts[1][RB:]], axis=0
            )
            even, odd = full[:, :LANES], full[:, LANES:]
            slot = my_x ^ x
            keep_ref[slot, place] = jnp.where(core == 0, even, odd)
            send_ref[slot, place] = jnp.where(core == 0, odd, even).astype(BF16)
        return 0

    lax.fori_loop(0, keep_ref.shape[1], group_step, 0, unroll=2)


def compute_kernel(
    off_hbm,
    ids_hbm,
    source_hbm,
    row_start_hbm,
    row_weight_hbm,
    col_start_hbm,
    col_weight_hbm,
    g_hbm,
    h_hbm,
    coef_hbm,
    weight_hbm,
    cover_hbm,
    keep_ref,
    send_ref,
    off_ref,
    ids_ref,
    source_ref,
    row_start_ref,
    row_weight_ref,
    col_start_ref,
    col_weight_ref,
    g_ref,
    h_ref,
    coef_ref,
    weight_ref,
    cover_ref,
    rowres_ref,
    shifted_ref,
    toep_ref,
    rows_ref,
    scale_ref,
    across_ref,
    sems,
):
    pairs = [
        (h_hbm, h_ref),
        (g_hbm, g_ref),
        (coef_hbm, coef_ref),
        (ids_hbm, ids_ref),
        (weight_hbm, weight_ref),
        (cover_hbm, cover_ref),
        (row_start_hbm, row_start_ref),
        (row_weight_hbm, row_weight_ref),
        (source_hbm, source_ref),
        (off_hbm, off_ref),
        (col_start_hbm, col_start_ref),
        (col_weight_hbm, col_weight_ref),
    ]
    copies = [pltpu.make_async_copy(a, b, sems.at[i]) for i, (a, b) in enumerate(pairs)]
    for copy in copies:
        copy.start()
    visit = lax.axis_index("visit")
    band = lax.axis_index("band")
    taps = g_ref.shape[1]
    margin = taps // 2
    basis = g_ref.shape[0]
    blocks = off_ref.shape[1]
    width = blocks * LANES
    visits = cover_ref.shape[0]

    for copy in copies[:6]:
        copy.wait()

    tile = (2 * LANES, LANES)
    tap = (iota(tile, 0) - iota(tile, 1) - (HALF - margin)).astype(I16)
    h_all = h_ref[...].astype(F32)
    for b in range(basis):
        acc = jnp.zeros(tile, BF16)
        for t in range(taps):
            acc = jnp.where(
                tap == t, jnp.broadcast_to(h_all[b : b + 1, t : t + 1], tile).astype(BF16), acc
            )
        toep_ref[:, b * LANES : (b + 1) * LANES] = acc

    span = basis * RB
    repeat = (iota((basis, span), 1) // RB == iota((basis, span), 0)).astype(F32)
    g_wide = mm(g_ref[...].astype(F32).T.astype(BF16), repeat.astype(BF16))
    place = iota((OR, span), 0)
    out_row = jnp.where(place < RB + margin, place, place - OR)
    tap = iota((OR, span), 1) % RB - out_row + margin
    tract_row = band * RB + out_row
    valid = (place < RB + margin) | (place >= OR - margin)
    valid &= (tract_row >= 0) & (tract_row < RB * lax.axis_size("band"))
    g_taps = jnp.zeros((OR, span), F32)
    for t in range(taps):
        g_taps = jnp.where(tap == t, g_wide[t : t + 1, :], g_taps)
    g_taps = jnp.where(valid, g_taps, 0.0)
    y = (tract_row.astype(F32) + 0.5) * (2.0 / (RB * lax.axis_size("band"))) - 1.0
    for n in range(NB):
        table = coef_ref[:, pl.ds(ids_ref[0, n], 1), :].reshape(coef_ref.shape[0], basis)
        c = jnp.dot(table, repeat, precision=HIGH)
        in_x = [
            c[0:1] + c[2:3] * y + c[5:6] * (y * y),
            c[1:2] + c[4:5] * y,
            c[3:4] + jnp.zeros_like(y),
        ]
        for k in range(3):
            rows_ref[n, k * OR : (k + 1) * OR, :] = (g_taps * in_x[k]).astype(BF16)

    cover = cover_ref[...].astype(F32)
    mine = jnp.where(iota(cover.shape, 0) == visit, cover, 0.0)
    weight = weight_ref[...]
    dims = (((0,), (1,)), ((), ()))
    denom = lax.dot_general(cover, weight, dims, precision=HIGH)
    own = lax.dot_general(mine, weight, dims, precision=HIGH)
    factor = own / denom
    for n in range(NB):
        scale_ref[n] = jnp.broadcast_to(factor[:, n : n + 1], (visits, LANES))

    for copy in copies[6:]:
        copy.wait()

    start = row_start_ref[...]
    weights = row_weight_ref[0].astype(F32)
    rel = iota((SR, RB), 0) - start
    picked = jnp.zeros((SR, RB), F32)
    for q in range(4):
        picked = jnp.where(rel == q, weights[q : q + 1, :], picked)
    picker = picked.T.astype(BF16)
    chunk = 2 * LANES

    def row_step(j, _):
        cols = pl.ds(pl.multiple_of(j * chunk, chunk), chunk)
        for n in range(NB):
            rowres_ref[n * RB : (n + 1) * RB, cols] = mm(
                picker, source_ref[0, n, :, cols]
            ).astype(BF16)
        return 0

    lax.fori_loop(0, rowres_ref.shape[1] // chunk, row_step, 0, unroll=11)

    low = iota((NB * RB, LANES), 1) < HALF
    tall = 3 * LANES
    tall_iota = iota((tall, LANES), 0).astype(I16)

    def col_step(c, before):
        first = pl.multiple_of(c * LANES, LANES)
        cols = pl.ds(first, LANES)
        at = col_start_ref[0:1, cols] + off_ref[0, c]
        wts = col_weight_ref[0, :, cols]
        rel = tall_iota - jnp.broadcast_to(at, (tall, LANES)).astype(I16)
        spread = jnp.zeros((tall, LANES), BF16)
        for q in range(4):
            spread = jnp.where(rel == q, jnp.broadcast_to(wts[q : q + 1, :], (tall, LANES)), spread)
        res = mm(rowres_ref[:, pl.ds(first, tall)], spread)
        rolled = pltpu.roll(res, HALF, 1)
        shifted_ref[:, cols] = jnp.where(low, before, rolled).astype(BF16)
        return rolled

    last = lax.fori_loop(0, blocks, col_step, jnp.zeros((NB * RB, LANES), F32), unroll=16)
    shifted_ref[:, width : width + LANES] = jnp.where(low, last, 0.0).astype(BF16)

    filter_groups(
        0, keep_ref, send_ref, shifted_ref, toep_ref, rows_ref, scale_ref, across_ref
    )


def ring(step):
    return [(i, step(i // GROUP, (i // CN) % XN, i % CN)) for i in range(ZN * GROUP)]


def at(z, x, c):
    return (z % ZN) * GROUP + x * CN + c


SIBLING = ring(lambda z, x, c: at(z, x, c ^ 1))
ACROSS_X = [ring(lambda z, x, c, d=d: at(z, x ^ d, c)) for d in range(1, XN)]
ALONG_Z = [[at(z, x, c) for z in range(ZN)] for x in range(XN) for c in range(CN)]


def exchange_core(keep, send):
    both = keep + lax.ppermute(send, "visit", SIBLING).astype(F32)
    return both[0], [both[d].astype(BF16) for d in range(1, XN)]


def exchange_x(own, sends):
    got = [lax.ppermute(part, "visit", to) for part, to in zip(sends, ACROSS_X)]
    return (own + sum(part.astype(F32) for part in got)).astype(BF16)


def local(
    source,
    row_start,
    row_weight,
    col_start,
    col_weight,
    col_offset,
    g_taps,
    h_taps,
    coef_table,
    table_ids,
    vis_weight,
    coverage,
):
    basis = g_taps.shape[0]
    width = col_start.shape[1]
    operands = (
        col_offset,
        table_ids,
        source,
        row_start,
        row_weight,
        col_start,
        col_weight,
        g_taps,
        h_taps,
        coef_table.transpose(2, 0, 1),
        vis_weight.T,
        coverage,
    )
    vmem = pl.BlockSpec(memory_space=pltpu.VMEM)
    local_copies = [
        (pltpu.SMEM if k < 2 else pltpu.VMEM)(a.shape, a.dtype) for k, a in enumerate(operands)
    ]
    limit = pltpu.CompilerParams(vmem_limit_bytes=20 * 1024 * 1024)
    partial = (
        jax.ShapeDtypeStruct((XN, ZN, PR, LANES), F32),
        jax.ShapeDtypeStruct((XN, ZN, PR, LANES), BF16),
    )
    across = pltpu.VMEM((NB, basis * RB, GW), BF16)
    keep, send = pl.pallas_call(
        compute_kernel,
        out_shape=partial,
        in_specs=[pl.BlockSpec(memory_space=pltpu.HBM)] * len(operands),
        out_specs=(vmem,) * 2,
        scratch_shapes=local_copies
        + [
            pltpu.VMEM((NB * RB, source.shape[3]), BF16),
            pltpu.VMEM((NB * RB, width + LANES), BF16),
            pltpu.VMEM((2 * LANES, basis * LANES), BF16),
            pltpu.VMEM((NB, 3 * OR, basis * RB), BF16),
            pltpu.VMEM((NB, coverage.shape[1], LANES), F32),
            across,
            pltpu.SemaphoreType.DMA((len(operands),)),
        ],
        compiler_params=limit,
    )(*(pltpu.with_memory_space_constraint(a, pltpu.HBM) for a in operands))

    plane = exchange_x(*exchange_core(keep, send))
    from_z = lax.all_to_all(
        plane, "visit", 0, 0, axis_index_groups=ALONG_Z, tiled=True
    )

    halo = jnp.sum(from_z[:, NB * RB :].astype(F32), axis=0)
    count = lax.axis_size("band")
    above = lax.ppermute(halo, "band", [(i, (i + 1) % count) for i in range(count)])
    below = lax.ppermute(halo, "band", [((i + 1) % count, i) for i in range(count)])
    own = jnp.sum(from_z[:, : NB * RB].astype(F32), axis=0).reshape(NB, RB, LANES)
    above = above.reshape(NB, HALO, LANES)[:, :10]
    below = below.reshape(NB, HALO, LANES)[:, HALO - 10 :]
    above = jnp.pad(above, ((0, 0), (0, RB - 10), (0, 0)))
    below = jnp.pad(below, ((0, 0), (RB - 10, 0), (0, 0)))
    return own + above + below


def solution(mesh):
    in_specs = (
        P("visit", None, "band", None),
        P("visit", "band"),
        P("visit", None, "band"),
        P("visit", None),
        P("visit", None, None),
        P("visit", None),
        P(),
        P(),
        P(),
        P("visit", None),
        P(),
        P(),
    )
    out_specs = P(None, "band", "visit")
    return jax.shard_map(local, mesh=mesh, in_specs=in_specs, out_specs=out_specs, check_vma=False)
```

time: 78.5 us -> 61.8 us (0.79)
  the two profiles are of different devices: /device:TPU:24 before, /device:TPU:6 now
where the time goes in v3:
time: 61.8 us; the launch traced here: 61.7 us
  blocking collectives  18.6 us (30%)
  waiting for transfers between devices  17.7 us (29%)
  Pallas kernels  16.9 us (27%)
  starting transfers between devices  7.37 us (12%)
  other arithmetic  1.04 us (2%)
    all_to_all x1, blocking collectives, local(): lax.all_to_all(plane, 'visit', 0, 0, axis_index_groups=ALONG_Z, tiled=True)  18.6 us
    pallas_call x1, Pallas kernels, local(): pl.pallas_call(compute_kernel, out_shape=partial, in_specs=[pl.BlockSpec(...  16.9 us
    ppermute x3, waiting for transfers between devices, exchange_x(): got = [lax.ppermute(part, 'visit', to) for part, to in zip(sends, ACROSS_X)]  10.2 us
    ppermute x3, starting transfers between devices, exchange_x(): got = [lax.ppermute(part, 'visit', to) for part, to in zip(sends, ACROSS_X)]  4.18 us
    ppermute x1, waiting for transfers between devices, local(): lax.ppermute(halo, 'band', [(i, (i + 1) % count) for i in range(count)])  3.51 us
    ppermute x1, starting transfers between devices, local(): lax.ppermute(halo, 'band', [((i + 1) % count, i) for i in range(count)])  3.09 us
    ppermute x1, waiting for transfers between devices, exchange_core(): both = keep + lax.ppermute(send, 'visit', SIBLING).astype(F32)  2.46 us
    ppermute x1, waiting for transfers between devices, local(): lax.ppermute(halo, 'band', [((i + 1) % count, i) for i in range(count)])  1.49 us
  transfers between devices with their start and end apart: 6, of which 6 were waited for; matrix products, arithmetic and copies ran while one was open for 0% of the time, Pallas kernels for 0%

profile of v3, /device:TPU:6, one launch (start us, length us, event | category | flops | bytes accessed | tf_op | source)
XLA Modules:
  0.0 61.7 jit_solution(12662810362227432955)
XLA Ops:
  0.0 16.9 %shard_map.118 = (f32[4,8,112,128]{3,2,1,0:T(8,128)S(1)}, bf16[4,8,112,128]{3,2,1,0:T(8,128)(2,1)S(1)}) custom-call(s32[1,64]{1,0:T(1,128)} %off_hbm.1, s32[1,2]{1,0:T(1,128)} %ids_hbm.1, bf16[1,2,40,8448]{3,2,1,0:T(8,128)(2,1)} %source_hbm.1, s32[1,32]{1,0:T(1,128)} %row_start_hbm.1, bf16[1,4,32]{2,1,0:T(4,128)(2,1)} %row_weight_hbm.1, ...), custom_call_target="tpu_custom_call" | custom-call | tf_op jit(solution)/shard_map/pallas_call | solution.py:308
  16.9 0.1 collective-permute-start
  17.0 2.5 %collective-permute-done = bf16[4,8,112,128]{3,2,1,0:T(8,128)(2,1)S(1)} collective-permute-done((bf16[4,8,112,128]{3,2,1,0:T(8,128)(2,1)S(1)}, bf16[4,8,112,128]{3,2,1,0:T(8,128)(2,1)S(1)}, u32[]{:S(2)}, u32[]{:S(2)}) %collective-permute-start) | collective-permute-done | bytes 917536 | tf_op jit(solution)/shard_map/ppermute | solution.py:259
  19.5 0.3 fusion.2
  19.8 0.9 %collective-permute-start.1 = (bf16[8,112,128]{2,1,0:T(8,128)(2,1)S(1)}, bf16[8,112,128]{2,1,0:T(8,128)(2,1)S(1)}, u32[]{:S(2)}, u32[]{:S(2)}) collective-permute-start(bf16[8,112,128]{2,1,0:T(8,128)(2,1)S(1)} %get-tuple-element.11), channel_id=1, source_target_pairs={{0,8},{4,12},{8,0},{12,4},{16,24},{20,28},{24,16},{28,20},{32,40},... | collective-permute-start | bytes 688136 | tf_op jit(solution)/shard_map/ppermute | solution.py:264
  20.7 1.5 %collective-permute-start.3 = (bf16[8,112,128]{2,1,0:T(8,128)(2,1)S(1)}, bf16[8,112,128]{2,1,0:T(8,128)(2,1)S(1)}, u32[]{:S(2)}, u32[]{:S(2)}) collective-permute-start(bf16[8,112,128]{2,1,0:T(8,128)(2,1)S(1)} %get-tuple-element.12), channel_id=1, source_target_pairs={{0,24},{4,28},{8,16},{12,20},{16,8},{20,12},{24,0},{28,4},{32,56},... | collective-permute-start | bytes 688136 | tf_op jit(solution)/shard_map/ppermute | solution.py:264
  22.2 1.8 %collective-permute-start.2 = (bf16[8,112,128]{2,1,0:T(8,128)(2,1)S(1)}, bf16[8,112,128]{2,1,0:T(8,128)(2,1)S(1)}, u32[]{:S(2)}, u32[]{:S(2)}) collective-permute-start(bf16[8,112,128]{2,1,0:T(8,128)(2,1)S(1)} %get-tuple-element.13), channel_id=1, source_target_pairs={{0,16},{4,20},{8,24},{12,28},{16,0},{20,4},{24,8},{28,12},{32,48},... | collective-permute-start | bytes 688136 | tf_op jit(solution)/shard_map/ppermute | solution.py:264
  24.0 4.4 %collective-permute-done.1 = bf16[8,112,128]{2,1,0:T(8,128)(2,1)S(1)} collective-permute-done((bf16[8,112,128]{2,1,0:T(8,128)(2,1)S(1)}, bf16[8,112,128]{2,1,0:T(8,128)(2,1)S(1)}, u32[]{:S(2)}, u32[]{:S(2)}) %collective-permute-start.1) | collective-permute-done | bytes 229408 | tf_op jit(solution)/shard_map/ppermute | solution.py:264
  28.3 4.0 %collective-permute-done.3 = bf16[8,112,128]{2,1,0:T(8,128)(2,1)S(1)} collective-permute-done((bf16[8,112,128]{2,1,0:T(8,128)(2,1)S(1)}, bf16[8,112,128]{2,1,0:T(8,128)(2,1)S(1)}, u32[]{:S(2)}, u32[]{:S(2)}) %collective-permute-start.3) | collective-permute-done | bytes 229408 | tf_op jit(solution)/shard_map/ppermute | solution.py:264
  32.3 1.9 %collective-permute-done.2 = bf16[8,112,128]{2,1,0:T(8,128)(2,1)S(1)} collective-permute-done((bf16[8,112,128]{2,1,0:T(8,128)(2,1)S(1)}, bf16[8,112,128]{2,1,0:T(8,128)(2,1)S(1)}, u32[]{:S(2)}, u32[]{:S(2)}) %collective-permute-start.2) | collective-permute-done | bytes 229408 | tf_op jit(solution)/shard_map/ppermute | solution.py:264
  34.2 0.1 fusion.1
  34.3 18.6 %all_to_all.5 = bf16[8,112,128]{2,1,0:T(8,128)(2,1)S(1)} all-to-all(bf16[8,112,128]{2,1,0:T(8,128)(2,1)S(1)} %fusion.1), channel_id=1, replica_groups={{0,32,64,96,128,160,192,224},{4,36,68,100,132,164,196,228},{8,40,72,104..., dimensions={0} | all-to-all | bytes 458752 | tf_op jit(solution)/shard_map/all_to_all | solution.py:327
  52.9 3.1 %collective-permute-start.5 = (f32[48,128]{1,0:T(8,128)S(1)}, f32[48,128]{1,0:T(8,128)S(1)}, u32[]{:S(2)}, u32[]{:S(2)}) collective-permute-start(f32[48,128]{1,0:T(8,128)S(1)} %convert_reduce_fusion.1), channel_id=1, source_target_pairs={{1,0},{2,1},{3,2},{0,3},{5,4},{6,5},{7,6},{4,7},{9,8},{10,9},{11,1... | collective-permute-start | bytes 73736 | tf_op jit(solution)/shard_map/ppermute | solution.py:334
  56.0 0.0 collective-permute-start.4
  56.1 1.5 %collective-permute-done.5 = f32[48,128]{1,0:T(8,128)S(1)} collective-permute-done((f32[48,128]{1,0:T(8,128)S(1)}, f32[48,128]{1,0:T(8,128)S(1)}, u32[]{:S(2)}, u32[]{:S(2)}) %collective-permute-start.5) | collective-permute-done | bytes 24608 | tf_op jit(solution)/shard_map/ppermute | solution.py:334
  57.6 3.5 %collective-permute-done.4 = f32[48,128]{1,0:T(8,128)S(1)} collective-permute-done((f32[48,128]{1,0:T(8,128)S(1)}, f32[48,128]{1,0:T(8,128)S(1)}, u32[]{:S(2)}, u32[]{:S(2)}) %collective-permute-start.4) | collective-permute-done | bytes 24608 | tf_op jit(solution)/shard_map/ppermute | solution.py:333
  61.1 0.6 %pad_add_fusion = f32[2,32,128]{2,1,0:T(8,128)} fusion(f32[2,10,128]{2,1,0:T(8,128)S(1)} %slice.42, f32[2,32,128]{2,1,0:T(8,128)S(1)} %bitcast.17, f32[2,10,128]{2,1,0:T(8,128)S(1)} %slice.41), kind=kLoop, calls=%fused_computation.9 | loop fusion | flops 16384 | bytes 86016 | tf_op jit(solution)/shard_map/add | solution.py:340
  (5 shorter events, 0.1 us)
Async XLA Ops:
  16.9 2.6 %collective-permute-start = (bf16[4,8,112,128]{3,2,1,0:T(8,128)(2,1)S(1)}, bf16[4,8,112,128]{3,2,1,0:T(8,128)(2,1)S(1)}, u32[]{:S(2)}, u32[]{:S(2)}) collective-permute-start(bf16[4,8,112,128]{3,2,1,0:T(8,128)(2,1)S(1)} %get-tuple-element.8), channel_id=1, source_target_pairs={{0,4},{4,0},{8,12},{12,8},{16,20},{20,16},{24,28},{28,24},{32,36},... | collective-permute-start | bytes 2752520 | tf_op jit(solution)/shard_map/ppermute | solution.py:259
  19.8 8.5 %collective-permute-start.1 = (bf16[8,112,128]{2,1,0:T(8,128)(2,1)S(1)}, bf16[8,112,128]{2,1,0:T(8,128)(2,1)S(1)}, u32[]{:S(2)}, u32[]{:S(2)}) collective-permute-start(bf16[8,112,128]{2,1,0:T(8,128)(2,1)S(1)} %get-tuple-element.11), channel_id=1, source_target_pairs={{0,8},{4,12},{8,0},{12,4},{16,24},{20,28},{24,16},{28,20},{32,40},... | collective-permute-start | bytes 688136 | tf_op jit(solution)/shard_map/ppermute | solution.py:264
  20.7 11.6 %collective-permute-start.3 = (bf16[8,112,128]{2,1,0:T(8,128)(2,1)S(1)}, bf16[8,112,128]{2,1,0:T(8,128)(2,1)S(1)}, u32[]{:S(2)}, u32[]{:S(2)}) collective-permute-start(bf16[8,112,128]{2,1,0:T(8,128)(2,1)S(1)} %get-tuple-element.12), channel_id=1, source_target_pairs={{0,24},{4,28},{8,16},{12,20},{16,8},{20,12},{24,0},{28,4},{32,56},... | collective-permute-start | bytes 688136 | tf_op jit(solution)/shard_map/ppermute | solution.py:264
  22.2 12.0 %collective-permute-start.2 = (bf16[8,112,128]{2,1,0:T(8,128)(2,1)S(1)}, bf16[8,112,128]{2,1,0:T(8,128)(2,1)S(1)}, u32[]{:S(2)}, u32[]{:S(2)}) collective-permute-start(bf16[8,112,128]{2,1,0:T(8,128)(2,1)S(1)} %get-tuple-element.13), channel_id=1, source_target_pairs={{0,16},{4,20},{8,24},{12,28},{16,0},{20,4},{24,8},{28,12},{32,48},... | collective-permute-start | bytes 688136 | tf_op jit(solution)/shard_map/ppermute | solution.py:264
  52.9 4.6 %collective-permute-start.5 = (f32[48,128]{1,0:T(8,128)S(1)}, f32[48,128]{1,0:T(8,128)S(1)}, u32[]{:S(2)}, u32[]{:S(2)}) collective-permute-start(f32[48,128]{1,0:T(8,128)S(1)} %convert_reduce_fusion.1), channel_id=1, source_target_pairs={{1,0},{2,1},{3,2},{0,3},{5,4},{6,5},{7,6},{4,7},{9,8},{10,9},{11,1... | collective-permute-start | bytes 73736 | tf_op jit(solution)/shard_map/ppermute | solution.py:334
  56.0 5.0 %collective-permute-start.4 = (f32[48,128]{1,0:T(8,128)S(1)}, f32[48,128]{1,0:T(8,128)S(1)}, u32[]{:S(2)}, u32[]{:S(2)}) collective-permute-start(f32[48,128]{1,0:T(8,128)S(1)} %convert_reduce_fusion.1), channel_id=1, source_target_pairs={{0,1},{1,2},{2,3},{3,0},{4,5},{5,6},{6,7},{7,4},{8,9},{9,10},{10,1... | collective-permute-start | bytes 73736 | tf_op jit(solution)/shard_map/ppermute | solution.py:333

commit v4 on v3

--- a/solution.py
+++ b/solution.py
@@ -17,9 +17,8 @@
 ZN, XN, CN = 8, 4, 2
 GROUP = XN * CN
 GW = GROUP * LANES
-HALO = 24
-OR = RB + HALO
-PR = NB * OR
+EDGE = 16
+OR = RB + 2 * EDGE
 HALF = LANES // 2
 
 
@@ -29,59 +28,6 @@
 
 def mm(a, b):
     return jnp.dot(a, b, preferred_element_type=F32)
-
-
-def filter_groups(
-    first_z, keep_ref, send_ref, shifted_ref, toep_ref, rows_ref, scale_ref, across_ref
-):
-    visit = lax.axis_index("visit")
-    core = visit % CN
-    my_x = (visit // CN) % XN
-    basis = toep_ref.shape[1] // LANES
-    width = shifted_ref.shape[1] - LANES
-
-    def group_step(place, _):
-        z = place + first_z
-        first = pl.multiple_of(z * GW, GW)
-        lhs = jnp.concatenate(
-            [shifted_ref[:, pl.ds(first + k * LANES, 2 * LANES)] for k in range(GROUP)], axis=0
-        )
-        for pair in range(basis // 2):
-            res = mm(lhs, toep_ref[:, pair * 2 * LANES : (pair + 1) * 2 * LANES]).astype(BF16)
-            for k in range(GROUP):
-                for n in range(NB):
-                    for b in range(2):
-                        across_ref[
-                            n,
-                            (2 * pair + b) * RB : (2 * pair + b + 1) * RB,
-                            k * LANES : (k + 1) * LANES,
-                        ] = res[
-                            (k * NB + n) * RB : (k * NB + n + 1) * RB,
-                            b * LANES : (b + 1) * LANES,
-                        ]
-        for x in range(XN):
-            lanes = slice(x * 2 * LANES, (x + 1) * 2 * LANES)
-            col = (first + x * 2 * LANES + iota((1, 2 * LANES), 1)).astype(F32)
-            xc = (col + 0.5) * (2.0 / width) - 1.0
-            patch = z * GROUP + x * CN
-            parts = []
-            for n in range(NB):
-                res = mm(rows_ref[n], across_ref[n, :, lanes])
-                total = res[:OR] + xc * (res[OR : 2 * OR] + xc * res[2 * OR :])
-                scale = jnp.concatenate(
-                    [scale_ref[n, pl.ds(patch + c, 1), :] for c in range(CN)], axis=1
-                )
-                parts.append(total * scale)
-            full = jnp.concatenate(
-                [parts[0][:RB], parts[1][:RB], parts[0][RB:], parts[1][RB:]], axis=0
-            )
-            even, odd = full[:, :LANES], full[:, LANES:]
-            slot = my_x ^ x
-            keep_ref[slot, place] = jnp.where(core == 0, even, odd)
-            send_ref[slot, place] = jnp.where(core == 0, odd, even).astype(BF16)
-        return 0
-
-    lax.fori_loop(0, keep_ref.shape[1], group_step, 0, unroll=2)
 
 
 def compute_kernel(
@@ -216,30 +162,96 @@
 
     lax.fori_loop(0, rowres_ref.shape[1] // chunk, row_step, 0, unroll=11)
 
-    low = iota((NB * RB, LANES), 1) < HALF
+    low = iota((NB * RB, 2 * LANES), 1) < HALF
     tall = 3 * LANES
     tall_iota = iota((tall, LANES), 0).astype(I16)
 
     def col_step(c, before):
-        first = pl.multiple_of(c * LANES, LANES)
-        cols = pl.ds(first, LANES)
-        at = col_start_ref[0:1, cols] + off_ref[0, c]
-        wts = col_weight_ref[0, :, cols]
-        rel = tall_iota - jnp.broadcast_to(at, (tall, LANES)).astype(I16)
-        spread = jnp.zeros((tall, LANES), BF16)
-        for q in range(4):
-            spread = jnp.where(rel == q, jnp.broadcast_to(wts[q : q + 1, :], (tall, LANES)), spread)
-        res = mm(rowres_ref[:, pl.ds(first, tall)], spread)
+        if c == blocks // 2:
+            shifted_ref[:, c * 2 * LANES :] = jnp.where(low, before, 0.0).astype(BF16)
+            return before
+        spreads = []
+        for k in range(2):
+            cols = slice((2 * c + k) * LANES, (2 * c + k + 1) * LANES)
+            at = col_start_ref[0:1, cols] + off_ref[0, 2 * c + k]
+            wts = col_weight_ref[0, :, cols]
+            rel = tall_iota - jnp.broadcast_to(at, (tall, LANES)).astype(I16)
+            spread = jnp.zeros((tall, LANES), BF16)
+            for q in range(4):
+                spread = jnp.where(
+                    rel == q, jnp.broadcast_to(wts[q : q + 1, :], (tall, LANES)), spread
+                )
+            spreads.append(spread)
+        none = jnp.zeros((LANES, LANES), BF16)
+        both = jnp.concatenate(
+            [
+                jnp.concatenate([spreads[0], none], axis=0),
+                jnp.concatenate([none, spreads[1]], axis=0),
+            ],
+            axis=1,
+        )
+        first = c * 2 * LANES
+        res = mm(rowres_ref[:, first : first + tall + LANES], both)
         rolled = pltpu.roll(res, HALF, 1)
-        shifted_ref[:, cols] = jnp.where(low, before, rolled).astype(BF16)
+        shifted_ref[:, first : first + 2 * LANES] = jnp.where(low, before, rolled).astype(BF16)
         return rolled
 
-    last = lax.fori_loop(0, blocks, col_step, jnp.zeros((NB * RB, LANES), F32), unroll=16)
-    shifted_ref[:, width : width + LANES] = jnp.where(low, last, 0.0).astype(BF16)
-
-    filter_groups(
-        0, keep_ref, send_ref, shifted_ref, toep_ref, rows_ref, scale_ref, across_ref
-    )
+    core = visit % CN
+    my_x = (visit // CN) % XN
+
+    def window(z):
+        return jnp.concatenate(
+            [
+                shifted_ref[:, (z * GROUP + k) * LANES : (z * GROUP + k + 2) * LANES]
+                for k in range(GROUP)
+            ],
+            axis=0,
+        )
+
+    def filter_columns(z, lhs, pair):
+        res = mm(lhs, toep_ref[:, pair * 2 * LANES : (pair + 1) * 2 * LANES]).astype(BF16)
+        for k in range(GROUP):
+            for n in range(NB):
+                for b in range(2):
+                    across_ref[
+                        z % 2,
+                        n,
+                        (2 * pair + b) * RB : (2 * pair + b + 1) * RB,
+                        k * LANES : (k + 1) * LANES,
+                    ] = res[
+                        (k * NB + n) * RB : (k * NB + n + 1) * RB,
+                        b * LANES : (b + 1) * LANES,
+                    ]
+
+    def filter_rows(z, x, n):
+        col = (z * GW + x * 2 * LANES + iota((1, 2 * LANES), 1)).astype(F32)
+        xc = (col + 0.5) * (2.0 / width) - 1.0
+        patch = z * GROUP + x * CN
+        slot = my_x ^ x
+        res = mm(rows_ref[n], across_ref[z % 2, n, :, x * 2 * LANES : (x + 1) * 2 * LANES])
+        total = res[:OR] + xc * (res[OR : 2 * OR] + xc * res[2 * OR :])
+        scale = jnp.concatenate(
+            [scale_ref[n, patch + c : patch + c + 1, :] for c in range(CN)], axis=1
+        )
+        total = total * scale
+        even, odd = total[:, :LANES], total[:, LANES:]
+        keep_ref[slot, z, n] = jnp.where(core == 0, even, odd)
+        send_ref[slot, z, n] = jnp.where(core == 0, odd, even).astype(BF16)
+
+    before = jnp.zeros((NB * RB, 2 * LANES), F32)
+    ready = GROUP // 2 + 1
+    for c in range(ready):
+        before = col_step(c, before)
+    for z in range(ZN + 1):
+        lhs = window(z) if z < ZN else None
+        for step in range(GROUP):
+            if z < ZN:
+                filter_columns(z, lhs, step)
+            if step % 2 == 0 and ready <= blocks // 2:
+                before = col_step(ready, before)
+                ready += 1
+            if z > 0:
+                filter_rows(z - 1, step // 2, step % 2)
 
 
 def ring(step):
@@ -253,16 +265,6 @@
 SIBLING = ring(lambda z, x, c: at(z, x, c ^ 1))
 ACROSS_X = [ring(lambda z, x, c, d=d: at(z, x ^ d, c)) for d in range(1, XN)]
 ALONG_Z = [[at(z, x, c) for z in range(ZN)] for x in range(XN) for c in range(CN)]
-
-
-def exchange_core(keep, send):
-    both = keep + lax.ppermute(send, "visit", SIBLING).astype(F32)
-    return both[0], [both[d].astype(BF16) for d in range(1, XN)]
-
-
-def exchange_x(own, sends):
-    got = [lax.ppermute(part, "visit", to) for part, to in zip(sends, ACROSS_X)]
-    return (own + sum(part.astype(F32) for part in got)).astype(BF16)
 
 
 def local(
@@ -301,10 +303,10 @@
     ]
     limit = pltpu.CompilerParams(vmem_limit_bytes=20 * 1024 * 1024)
     partial = (
-        jax.ShapeDtypeStruct((XN, ZN, PR, LANES), F32),
-        jax.ShapeDtypeStruct((XN, ZN, PR, LANES), BF16),
+        jax.ShapeDtypeStruct((XN, ZN, NB, OR, LANES), F32),
+        jax.ShapeDtypeStruct((XN, ZN, NB, OR, LANES), BF16),
     )
-    across = pltpu.VMEM((NB, basis * RB, GW), BF16)
+    across = pltpu.VMEM((2, NB, basis * RB, GW), BF16)
     keep, send = pl.pallas_call(
         compute_kernel,
         out_shape=partial,
@@ -313,7 +315,7 @@
         scratch_shapes=local_copies
         + [
             pltpu.VMEM((NB * RB, source.shape[3]), BF16),
-            pltpu.VMEM((NB * RB, width + LANES), BF16),
+            pltpu.VMEM((NB * RB, width + 2 * LANES), BF16),
             pltpu.VMEM((2 * LANES, basis * LANES), BF16),
             pltpu.VMEM((NB, 3 * OR, basis * RB), BF16),
             pltpu.VMEM((NB, coverage.shape[1], LANES), F32),
@@ -323,21 +325,23 @@
         compiler_params=limit,
     )(*(pltpu.with_memory_space_constraint(a, pltpu.HBM) for a in operands))
 
-    plane = exchange_x(*exchange_core(keep, send))
+    both = keep + lax.ppermute(send, "visit", SIBLING).astype(F32)
+
+    count = lax.axis_size("band")
+    after = both[:, :, :, RB : RB + EDGE].astype(BF16)
+    before = both[:, :, :, RB + EDGE :].astype(BF16)
+    after = lax.ppermute(after, "band", [(i, (i + 1) % count) for i in range(count)])
+    before = lax.ppermute(before, "band", [((i + 1) % count, i) for i in range(count)])
+    own = both[:, :, :, :RB] + jnp.concatenate([after, before], axis=3).astype(F32)
+
+    from_x = [
+        lax.ppermute(own[d].astype(BF16), "visit", ACROSS_X[d - 1]) for d in range(1, XN)
+    ]
+    plane = own[0] + sum(part.astype(F32) for part in from_x)
     from_z = lax.all_to_all(
-        plane, "visit", 0, 0, axis_index_groups=ALONG_Z, tiled=True
+        plane.astype(BF16), "visit", 0, 0, axis_index_groups=ALONG_Z, tiled=True
     )
-
-    halo = jnp.sum(from_z[:, NB * RB :].astype(F32), axis=0)
-    count = lax.axis_size("band")
-    above = lax.ppermute(halo, "band", [(i, (i + 1) % count) for i in range(count)])
-    below = lax.ppermute(halo, "band", [((i + 1) % count, i) for i in range(count)])
-    own = jnp.sum(from_z[:, : NB * RB].astype(F32), axis=0).reshape(NB, RB, LANES)
-    above = above.reshape(NB, HALO, LANES)[:, :10]
-    below = below.reshape(NB, HALO, LANES)[:, HALO - 10 :]
-    above = jnp.pad(above, ((0, 0), (0, RB - 10), (0, 0)))
-    below = jnp.pad(below, ((0, 0), (RB - 10, 0), (0, 0)))
-    return own + above + below
+    return jnp.sum(from_z.astype(F32), axis=0)
 
 
 def solution(mesh):

time: 61.8 us -> 56.1 us (0.908)
  the two profiles are of different devices: /device:TPU:6 before, /device:TPU:24 now
where the time goes in v4:
time: 56.1 us; the launch traced here: 55.9 us
  blocking collectives  17.3 us (31%)
  waiting for transfers between devices  16.7 us (30%)
  Pallas kernels  13.8 us (25%)
  starting transfers between devices  6.55 us (12%)
  other arithmetic  1.48 us (3%)
    all_to_all x1, blocking collectives, local(): lax.all_to_all(plane.astype(BF16), 'visit', 0, 0, axis_index_groups=ALONG...  17.3 us
    pallas_call x1, Pallas kernels, local(): pl.pallas_call(compute_kernel, out_shape=partial, in_specs=[pl.BlockSpec(...  13.8 us
    ppermute x1, waiting for transfers between devices, local(): lax.ppermute(after, 'band', [(i, (i + 1) % count) for i in range(count)])  6.32 us
    ppermute x3, waiting for transfers between devices, local(): lax.ppermute(own[d].astype(BF16), 'visit', ACROSS_X[d - 1])  4.85 us
    ppermute x3, starting transfers between devices, local(): lax.ppermute(own[d].astype(BF16), 'visit', ACROSS_X[d - 1])  4.17 us
    ppermute x1, waiting for transfers between devices, local(): lax.ppermute(before, 'band', [((i + 1) % count, i) for i in range(count)])  2.89 us
    ppermute x1, waiting for transfers between devices, local(): both = keep + lax.ppermute(send, 'visit', SIBLING).astype(F32)  2.65 us
    ppermute x1, starting transfers between devices, local(): lax.ppermute(after, 'band', [(i, (i + 1) % count) for i in range(count)])  2.03 us
  transfers between devices with their start and end apart: 6, of which 5 were waited for; matrix products, arithmetic and copies ran while one was open for 0% of the time, Pallas kernels for 0%

profile of v4, /device:TPU:24, one launch (start us, length us, event | category | flops | bytes accessed | tf_op | source)
XLA Modules:
  0.0 55.9 jit_solution(5343938368036015050)
XLA Ops:
  0.0 13.8 %shard_map.118 = (f32[4,8,2,64,128]{4,3,2,1,0:T(8,128)S(1)}, bf16[4,8,2,64,128]{4,3,2,1,0:T(8,128)(2,1)S(1)}) custom-call(s32[1,64]{1,0:T(1,128)} %off_hbm.1, s32[1,2]{1,0:T(1,128)} %ids_hbm.1, bf16[1,2,40,8448]{3,2,1,0:T(8,128)(2,1)} %source_hbm.1, s32[1,32]{1,0:T(1,128)} %row_start_hbm.1, bf16[1,4,32]{2,1,0:T(4,128)(2,1)} %row_weight_hbm.1, ...), custom_call_target="tpu_custom_call" | custom-call | tf_op jit(solution)/shard_map/pallas_call | solution.py:310
  13.8 0.3 collective-permute-start
  14.1 2.6 %collective-permute-done = bf16[4,8,2,64,128]{4,3,2,1,0:T(8,128)(2,1)S(1)} collective-permute-done((bf16[4,8,2,64,128]{4,3,2,1,0:T(8,128)(2,1)S(1)}, bf16[4,8,2,64,128]{4,3,2,1,0:T(8,128)(2,1)S(1)}, u32[]{:S(2)}, u32[]{:S(2)}) %collective-permute-start) | collective-permute-done | bytes 1048608 | tf_op jit(solution)/shard_map/ppermute | solution.py:328
  16.7 0.6 %fusion.3 = (bf16[4,8,2,64,128]{4,3,2,1,0:T(8,128)(2,1)S(1)}, f32[4,8,2,64,128]{4,3,2,1,0:T(8,128)S(1)}) fusion(f32[4,8,2,64,128]{4,3,2,1,0:T(8,128)S(1)} %get-tuple-element.7, bf16[4,8,2,64,128]{4,3,2,1,0:T(8,128)(2,1)S(1)} %collective-permute-done), kind=kLoop, calls=%fused_computation.10 | loop fusion | flops 1572864 | bytes 6291456 | tf_op jit(solution)/shard_map/convert.4
  17.3 2.0 %collective-permute-start.1 = (bf16[4,8,2,16,128]{4,3,2,1,0:T(8,128)(2,1)S(1)}, bf16[4,8,2,16,128]{4,3,2,1,0:T(8,128)(2,1)S(1)}, u32[]{:S(2)}, u32[]{:S(2)}) collective-permute-start(bf16[4,8,2,16,128]{4,3,2,1,0:T(8,128)(2,1)S(1)} %get-tuple-element.13), channel_id=1, source_target_pairs={{0,1},{1,2},{2,3},{3,0},{4,5},{5,6},{6,7},{7,4},{8,9},{9,10},{10,1... | collective-permute-start | bytes 786440 | tf_op jit(solution)/shard_map/ppermute | solution.py:333
  19.4 0.1 collective-permute-start.2
  19.4 6.3 %collective-permute-done.1 = bf16[4,8,2,16,128]{4,3,2,1,0:T(8,128)(2,1)S(1)} collective-permute-done((bf16[4,8,2,16,128]{4,3,2,1,0:T(8,128)(2,1)S(1)}, bf16[4,8,2,16,128]{4,3,2,1,0:T(8,128)(2,1)S(1)}, u32[]{:S(2)}, u32[]{:S(2)}) %collective-permute-start.1) | collective-permute-done | bytes 262176 | tf_op jit(solution)/shard_map/ppermute | solution.py:333
  25.8 2.9 %collective-permute-done.2 = bf16[4,8,2,16,128]{4,3,2,1,0:T(8,128)(2,1)S(1)} collective-permute-done((bf16[4,8,2,16,128]{4,3,2,1,0:T(8,128)(2,1)S(1)}, bf16[4,8,2,16,128]{4,3,2,1,0:T(8,128)(2,1)S(1)}, u32[]{:S(2)}, u32[]{:S(2)}) %collective-permute-start.2) | collective-permute-done | bytes 262176 | tf_op jit(solution)/shard_map/ppermute | solution.py:334
  28.6 0.2 fusion.2
  28.9 0.1 collective-permute-start.3
  29.0 2.0 %collective-permute-start.5 = (bf16[8,2,32,128]{3,2,1,0:T(8,128)(2,1)S(1)}, bf16[8,2,32,128]{3,2,1,0:T(8,128)(2,1)S(1)}, u32[]{:S(2)}, u32[]{:S(2)}) collective-permute-start(bf16[8,2,32,128]{3,2,1,0:T(8,128)(2,1)S(1)} %get-tuple-element.16), channel_id=1, source_target_pairs={{0,24},{4,28},{8,16},{12,20},{16,8},{20,12},{24,0},{28,4},{32,56},... | collective-permute-start | bytes 393224 | tf_op jit(solution)/shard_map/ppermute | solution.py:338
  31.0 2.1 %collective-permute-start.4 = (bf16[8,2,32,128]{3,2,1,0:T(8,128)(2,1)S(1)}, bf16[8,2,32,128]{3,2,1,0:T(8,128)(2,1)S(1)}, u32[]{:S(2)}, u32[]{:S(2)}) collective-permute-start(bf16[8,2,32,128]{3,2,1,0:T(8,128)(2,1)S(1)} %get-tuple-element.17), channel_id=1, source_target_pairs={{0,16},{4,20},{8,24},{12,28},{16,0},{20,4},{24,8},{28,12},{32,48},... | collective-permute-start | bytes 393224 | tf_op jit(solution)/shard_map/ppermute | solution.py:338
  33.1 2.2 %collective-permute-done.3 = bf16[8,2,32,128]{3,2,1,0:T(8,128)(2,1)S(1)} collective-permute-done((bf16[8,2,32,128]{3,2,1,0:T(8,128)(2,1)S(1)}, bf16[8,2,32,128]{3,2,1,0:T(8,128)(2,1)S(1)}, u32[]{:S(2)}, u32[]{:S(2)}) %collective-permute-start.3) | collective-permute-done | bytes 131104 | tf_op jit(solution)/shard_map/ppermute | solution.py:338
  35.3 2.7 %collective-permute-done.5 = bf16[8,2,32,128]{3,2,1,0:T(8,128)(2,1)S(1)} collective-permute-done((bf16[8,2,32,128]{3,2,1,0:T(8,128)(2,1)S(1)}, bf16[8,2,32,128]{3,2,1,0:T(8,128)(2,1)S(1)}, u32[]{:S(2)}, u32[]{:S(2)}) %collective-permute-start.5) | collective-permute-done | bytes 131104 | tf_op jit(solution)/shard_map/ppermute | solution.py:338
  37.9 0.0 collective-permute-done.4
  37.9 0.1 fusion.1
  38.0 17.3 %all_to_all.5 = bf16[8,2,32,128]{3,2,1,0:T(8,128)(2,1)S(1)} all-to-all(bf16[8,2,32,128]{3,2,1,0:T(8,128)(2,1)S(1)} %fusion.1), channel_id=1, replica_groups={{0,32,64,96,128,160,192,224},{4,36,68,100,132,164,196,228},{8,40,72,104..., dimensions={0} | all-to-all | bytes 262144 | tf_op jit(solution)/shard_map/all_to_all | solution.py:341
  55.3 0.6 %convert_reduce_fusion = f32[2,32,128]{2,1,0:T(8,128)} fusion(bf16[8,2,32,128]{3,2,1,0:T(8,128)(2,1)S(1)} %all_to_all.5), kind=kLoop, calls=%fused_computation.5 | loop fusion | flops 122880 | bytes 163840 | tf_op jit(solution)/shard_map/reduce_sum | solution.py:344
  (2 shorter events, 0.1 us)
Async XLA Ops:
  13.8 2.9 %collective-permute-start = (bf16[4,8,2,64,128]{4,3,2,1,0:T(8,128)(2,1)S(1)}, bf16[4,8,2,64,128]{4,3,2,1,0:T(8,128)(2,1)S(1)}, u32[]{:S(2)}, u32[]{:S(2)}) collective-permute-start(bf16[4,8,2,64,128]{4,3,2,1,0:T(8,128)(2,1)S(1)} %get-tuple-element.8), channel_id=1, source_target_pairs={{0,4},{4,0},{8,12},{12,8},{16,20},{20,16},{24,28},{28,24},{32,36},... | collective-permute-start | bytes 3145736 | tf_op jit(solution)/shard_map/ppermute | solution.py:328
  17.3 8.4 %collective-permute-start.1 = (bf16[4,8,2,16,128]{4,3,2,1,0:T(8,128)(2,1)S(1)}, bf16[4,8,2,16,128]{4,3,2,1,0:T(8,128)(2,1)S(1)}, u32[]{:S(2)}, u32[]{:S(2)}) collective-permute-start(bf16[4,8,2,16,128]{4,3,2,1,0:T(8,128)(2,1)S(1)} %get-tuple-element.13), channel_id=1, source_target_pairs={{0,1},{1,2},{2,3},{3,0},{4,5},{5,6},{6,7},{7,4},{8,9},{9,10},{10,1... | collective-permute-start | bytes 786440 | tf_op jit(solution)/shard_map/ppermute | solution.py:333
  19.4 9.3 %collective-permute-start.2 = (bf16[4,8,2,16,128]{4,3,2,1,0:T(8,128)(2,1)S(1)}, bf16[4,8,2,16,128]{4,3,2,1,0:T(8,128)(2,1)S(1)}, u32[]{:S(2)}, u32[]{:S(2)}) collective-permute-start(bf16[4,8,2,16,128]{4,3,2,1,0:T(8,128)(2,1)S(1)} %get-tuple-element.14), channel_id=1, source_target_pairs={{1,0},{2,1},{3,2},{0,3},{5,4},{6,5},{7,6},{4,7},{9,8},{10,9},{11,1... | collective-permute-start | bytes 786440 | tf_op jit(solution)/shard_map/ppermute | solution.py:334
  28.9 6.4 %collective-permute-start.3 = (bf16[8,2,32,128]{3,2,1,0:T(8,128)(2,1)S(1)}, bf16[8,2,32,128]{3,2,1,0:T(8,128)(2,1)S(1)}, u32[]{:S(2)}, u32[]{:S(2)}) collective-permute-start(bf16[8,2,32,128]{3,2,1,0:T(8,128)(2,1)S(1)} %get-tuple-element.15), channel_id=1, source_target_pairs={{0,8},{4,12},{8,0},{12,4},{16,24},{20,28},{24,16},{28,20},{32,40},... | collective-permute-start | bytes 393224 | tf_op jit(solution)/shard_map/ppermute | solution.py:338
  29.0 8.9 %collective-permute-start.5 = (bf16[8,2,32,128]{3,2,1,0:T(8,128)(2,1)S(1)}, bf16[8,2,32,128]{3,2,1,0:T(8,128)(2,1)S(1)}, u32[]{:S(2)}, u32[]{:S(2)}) collective-permute-start(bf16[8,2,32,128]{3,2,1,0:T(8,128)(2,1)S(1)} %get-tuple-element.16), channel_id=1, source_target_pairs={{0,24},{4,28},{8,16},{12,20},{16,8},{20,12},{24,0},{28,4},{32,56},... | collective-permute-start | bytes 393224 | tf_op jit(solution)/shard_map/ppermute | solution.py:338
  31.0 7.0 %collective-permute-start.4 = (bf16[8,2,32,128]{3,2,1,0:T(8,128)(2,1)S(1)}, bf16[8,2,32,128]{3,2,1,0:T(8,128)(2,1)S(1)}, u32[]{:S(2)}, u32[]{:S(2)}) collective-permute-start(bf16[8,2,32,128]{3,2,1,0:T(8,128)(2,1)S(1)} %get-tuple-element.17), channel_id=1, source_target_pairs={{0,16},{4,20},{8,24},{12,28},{16,0},{20,4},{24,8},{28,12},{32,48},... | collective-permute-start | bytes 393224 | tf_op jit(solution)/shard_map/ppermute | solution.py:338

commit v5 on v4

--- a/solution.py
+++ b/solution.py
@@ -44,7 +44,9 @@
     weight_hbm,
     cover_hbm,
     keep_ref,
+    keep_edge_ref,
     send_ref,
+    send_edge_ref,
     off_ref,
     ids_ref,
     source_ref,
@@ -94,8 +96,11 @@
     for copy in copies[:6]:
         copy.wait()
 
-    tile = (2 * LANES, LANES)
-    tap = (iota(tile, 0) - iota(tile, 1) - (HALF - margin)).astype(I16)
+    low_row, high_row = 48, 208
+    tile = (high_row - low_row, LANES)
+    tap = (iota(tile, 0) - iota(tile, 1) - (HALF - margin - low_row)).astype(I16)
+    toep_ref[:low_row] = jnp.zeros((low_row, basis * LANES), BF16)
+    toep_ref[high_row:] = jnp.zeros((2 * LANES - high_row, basis * LANES), BF16)
     h_all = h_ref[...].astype(F32)
     for b in range(basis):
         acc = jnp.zeros(tile, BF16)
@@ -103,7 +108,7 @@
             acc = jnp.where(
                 tap == t, jnp.broadcast_to(h_all[b : b + 1, t : t + 1], tile).astype(BF16), acc
             )
-        toep_ref[:, b * LANES : (b + 1) * LANES] = acc
+        toep_ref[low_row:high_row, b * LANES : (b + 1) * LANES] = acc
 
     span = basis * RB
     repeat = (iota((basis, span), 1) // RB == iota((basis, span), 0)).astype(F32)
@@ -160,7 +165,7 @@
             ).astype(BF16)
         return 0
 
-    lax.fori_loop(0, rowres_ref.shape[1] // chunk, row_step, 0, unroll=11)
+    lax.fori_loop(0, rowres_ref.shape[1] // chunk, row_step, 0, unroll=33)
 
     low = iota((NB * RB, 2 * LANES), 1) < HALF
     tall = 3 * LANES
@@ -235,8 +240,12 @@
         )
         total = total * scale
         even, odd = total[:, :LANES], total[:, LANES:]
-        keep_ref[slot, z, n] = jnp.where(core == 0, even, odd)
-        send_ref[slot, z, n] = jnp.where(core == 0, odd, even).astype(BF16)
+        keep = jnp.where(core == 0, even, odd)
+        keep_ref[slot, z, n] = keep[:RB]
+        keep_edge_ref[slot, z, n] = keep[RB:]
+        send = jnp.where(core == 0, odd, even).astype(BF16)
+        send_ref[slot, z, n] = send[:RB]
+        send_edge_ref[slot, z, n] = send[RB:]
 
     before = jnp.zeros((NB * RB, 2 * LANES), F32)
     ready = GROUP // 2 + 1
@@ -302,16 +311,14 @@
         (pltpu.SMEM if k < 2 else pltpu.VMEM)(a.shape, a.dtype) for k, a in enumerate(operands)
     ]
     limit = pltpu.CompilerParams(vmem_limit_bytes=20 * 1024 * 1024)
-    partial = (
-        jax.ShapeDtypeStruct((XN, ZN, NB, OR, LANES), F32),
-        jax.ShapeDtypeStruct((XN, ZN, NB, OR, LANES), BF16),
-    )
+    wide = jax.ShapeDtypeStruct((XN, ZN, NB, RB, LANES), F32)
+    narrow = jax.ShapeDtypeStruct((XN, ZN, NB, RB, LANES), BF16)
     across = pltpu.VMEM((2, NB, basis * RB, GW), BF16)
-    keep, send = pl.pallas_call(
+    keep, keep_edge, send, send_edge = pl.pallas_call(
         compute_kernel,
-        out_shape=partial,
+        out_shape=(wide, wide, narrow, narrow),
         in_specs=[pl.BlockSpec(memory_space=pltpu.HBM)] * len(operands),
-        out_specs=(vmem,) * 2,
+        out_specs=(vmem,) * 4,
         scratch_shapes=local_copies
         + [
             pltpu.VMEM((NB * RB, source.shape[3]), BF16),
@@ -325,14 +332,14 @@
         compiler_params=limit,
     )(*(pltpu.with_memory_space_constraint(a, pltpu.HBM) for a in operands))
 
-    both = keep + lax.ppermute(send, "visit", SIBLING).astype(F32)
-
+    edge = keep_edge + lax.ppermute(send_edge, "visit", SIBLING).astype(F32)
     count = lax.axis_size("band")
-    after = both[:, :, :, RB : RB + EDGE].astype(BF16)
-    before = both[:, :, :, RB + EDGE :].astype(BF16)
+    after = edge[:, :, :, :EDGE].astype(BF16)
+    before = edge[:, :, :, EDGE:].astype(BF16)
     after = lax.ppermute(after, "band", [(i, (i + 1) % count) for i in range(count)])
     before = lax.ppermute(before, "band", [((i + 1) % count, i) for i in range(count)])
-    own = both[:, :, :, :RB] + jnp.concatenate([after, before], axis=3).astype(F32)
+    own = keep + lax.ppermute(send, "visit", SIBLING).astype(F32)
+    own = own + jnp.concatenate([after, before], axis=3).astype(F32)
 
     from_x = [
         lax.ppermute(own[d].astype(BF16), "visit", ACROSS_X[d - 1]) for d in range(1, XN)

time: 56.1 us -> 53.9 us (0.961)
  waiting for transfers between devices: 16.7 us -> 15.4 us
  Pallas kernels: 13.8 us -> 12.7 us
    ppermute x1 -> x2, waiting for transfers between devices: 2.65 us -> 1.4 us  [the longest x1 1.4 us: local(): edge = keep_edge + lax.ppermute(send_edge, 'visit', SIBLING).astype(F32)]
    pallas_call x1, Pallas kernels: 13.8 us -> 12.7 us  [local(): pl.pallas_call(compute_kernel, out_shape=(wide, wide, narrow, narrow), in...]
  transfers between devices with their start and end apart: 6 -> 7, of which waited for: 5 -> 5; matrix products, arithmetic and copies ran while one was open for 0% -> 0% of each run, Pallas kernels for 0% -> 0%
where the time goes in v5:
time: 53.9 us; the launch traced here: 53.8 us
  blocking collectives  17.3 us (32%)
  waiting for transfers between devices  15.4 us (29%)
  Pallas kernels  12.7 us (24%)
  starting transfers between devices  7.05 us (13%)
  other arithmetic  1.15 us (2%)
    all_to_all x1, blocking collectives, local(): lax.all_to_all(plane.astype(BF16), 'visit', 0, 0, axis_index_groups=ALONG...  17.3 us
    pallas_call x1, Pallas kernels, local(): pl.pallas_call(compute_kernel, out_shape=(wide, wide, narrow, narrow), in...  12.7 us
    ppermute x1, waiting for transfers between devices, local(): lax.ppermute(after, 'band', [(i, (i + 1) % count) for i in range(count)])  6.32 us
    ppermute x3, waiting for transfers between devices, local(): lax.ppermute(own[d].astype(BF16), 'visit', ACROSS_X[d - 1])  4.86 us
    ppermute x3, starting transfers between devices, local(): lax.ppermute(own[d].astype(BF16), 'visit', ACROSS_X[d - 1])  4.17 us
    ppermute x1, waiting for transfers between devices, local(): lax.ppermute(before, 'band', [((i + 1) % count, i) for i in range(count)])  2.86 us
    ppermute x1, starting transfers between devices, local(): lax.ppermute(after, 'band', [(i, (i + 1) % count) for i in range(count)])  2.01 us
    ppermute x1, waiting for transfers between devices, local(): edge = keep_edge + lax.ppermute(send_edge, 'visit', SIBLING).astype(F32)  1.4 us
  transfers between devices with their start and end apart: 7, of which 5 were waited for; matrix products, arithmetic and copies ran while one was open for 0% of the time, Pallas kernels for 0%

profile of v5, /device:TPU:24, one launch (start us, length us, event | category | flops | bytes accessed | tf_op | source)
XLA Modules:
  0.0 53.8 jit_solution(4864309004659723729)
XLA Ops:
  0.0 12.7 %shard_map.118 = (f32[4,8,2,32,128]{4,3,2,1,0:T(8,128)S(1)}, f32[4,8,2,32,128]{4,3,2,1,0:T(8,128)S(1)}, bf16[4,8,2,32,128]{4,3,2,1,0:T(8,128)(2,1)S(1)}, bf16[4,8,2,32,128]{4,3,2,1,0:T(8,128)(2,1)S(1)}) custom-call(s32[1,64]{1,0:T(1,128)} %off_hbm.1, s32[1,2]{1,0:T(1,128)} %ids_hbm.1, bf16[1,2,40,8448]{3,2,1,0:T(8,128)(2,1)} %source_hbm.1, ...), custom_call_target="tpu_custom_call" | custom-call | tf_op jit(solution)/shard_map/pallas_call | solution.py:317
  12.7 0.3 collective-permute-start.1
  13.0 0.5 collective-permute-start
  13.5 1.4 %collective-permute-done.1 = bf16[4,8,2,32,128]{4,3,2,1,0:T(8,128)(2,1)S(1)} collective-permute-done((bf16[4,8,2,32,128]{4,3,2,1,0:T(8,128)(2,1)S(1)}, bf16[4,8,2,32,128]{4,3,2,1,0:T(8,128)(2,1)S(1)}, u32[]{:S(2)}, u32[]{:S(2)}) %collective-permute-start.1) | collective-permute-done | bytes 524320 | tf_op jit(solution)/shard_map/ppermute | solution.py:335
  14.9 0.2 add_convert_fusion
  15.1 2.0 %collective-permute-start.2 = (bf16[4,8,2,16,128]{4,3,2,1,0:T(8,128)(2,1)S(1)}, bf16[4,8,2,16,128]{4,3,2,1,0:T(8,128)(2,1)S(1)}, u32[]{:S(2)}, u32[]{:S(2)}) collective-permute-start(bf16[4,8,2,16,128]{4,3,2,1,0:T(8,128)(2,1)S(1)} %get-tuple-element.18), channel_id=1, source_target_pairs={{0,1},{1,2},{2,3},{3,0},{4,5},{5,6},{6,7},{7,4},{8,9},{9,10},{10,1... | collective-permute-start | bytes 786440 | tf_op jit(solution)/shard_map/ppermute | solution.py:339
  17.1 0.1 collective-permute-start.3
  17.2 0.0 collective-permute-done
  17.2 6.3 %collective-permute-done.2 = bf16[4,8,2,16,128]{4,3,2,1,0:T(8,128)(2,1)S(1)} collective-permute-done((bf16[4,8,2,16,128]{4,3,2,1,0:T(8,128)(2,1)S(1)}, bf16[4,8,2,16,128]{4,3,2,1,0:T(8,128)(2,1)S(1)}, u32[]{:S(2)}, u32[]{:S(2)}) %collective-permute-start.2) | collective-permute-done | bytes 262176 | tf_op jit(solution)/shard_map/ppermute | solution.py:339
  23.6 2.9 %collective-permute-done.3 = bf16[4,8,2,16,128]{4,3,2,1,0:T(8,128)(2,1)S(1)} collective-permute-done((bf16[4,8,2,16,128]{4,3,2,1,0:T(8,128)(2,1)S(1)}, bf16[4,8,2,16,128]{4,3,2,1,0:T(8,128)(2,1)S(1)}, u32[]{:S(2)}, u32[]{:S(2)}) %collective-permute-start.3) | collective-permute-done | bytes 262176 | tf_op jit(solution)/shard_map/ppermute | solution.py:340
  26.4 0.3 fusion.2
  26.7 0.1 collective-permute-start.4
  26.8 2.0 %collective-permute-start.6 = (bf16[8,2,32,128]{3,2,1,0:T(8,128)(2,1)S(1)}, bf16[8,2,32,128]{3,2,1,0:T(8,128)(2,1)S(1)}, u32[]{:S(2)}, u32[]{:S(2)}) collective-permute-start(bf16[8,2,32,128]{3,2,1,0:T(8,128)(2,1)S(1)} %get-tuple-element.16), channel_id=1, source_target_pairs={{0,24},{4,28},{8,16},{12,20},{16,8},{20,12},{24,0},{28,4},{32,56},... | collective-permute-start | bytes 393224 | tf_op jit(solution)/shard_map/ppermute | solution.py:345
  28.8 2.1 %collective-permute-start.5 = (bf16[8,2,32,128]{3,2,1,0:T(8,128)(2,1)S(1)}, bf16[8,2,32,128]{3,2,1,0:T(8,128)(2,1)S(1)}, u32[]{:S(2)}, u32[]{:S(2)}) collective-permute-start(bf16[8,2,32,128]{3,2,1,0:T(8,128)(2,1)S(1)} %get-tuple-element.17), channel_id=1, source_target_pairs={{0,16},{4,20},{8,24},{12,28},{16,0},{20,4},{24,8},{28,12},{32,48},... | collective-permute-start | bytes 393224 | tf_op jit(solution)/shard_map/ppermute | solution.py:345
  30.9 2.2 %collective-permute-done.4 = bf16[8,2,32,128]{3,2,1,0:T(8,128)(2,1)S(1)} collective-permute-done((bf16[8,2,32,128]{3,2,1,0:T(8,128)(2,1)S(1)}, bf16[8,2,32,128]{3,2,1,0:T(8,128)(2,1)S(1)}, u32[]{:S(2)}, u32[]{:S(2)}) %collective-permute-start.4) | collective-permute-done | bytes 131104 | tf_op jit(solution)/shard_map/ppermute | solution.py:345
  33.1 2.7 %collective-permute-done.6 = bf16[8,2,32,128]{3,2,1,0:T(8,128)(2,1)S(1)} collective-permute-done((bf16[8,2,32,128]{3,2,1,0:T(8,128)(2,1)S(1)}, bf16[8,2,32,128]{3,2,1,0:T(8,128)(2,1)S(1)}, u32[]{:S(2)}, u32[]{:S(2)}) %collective-permute-start.6) | collective-permute-done | bytes 131104 | tf_op jit(solution)/shard_map/ppermute | solution.py:345
  35.8 0.0 collective-permute-done.5
  35.8 0.1 fusion.1
  35.8 17.3 %all_to_all.5 = bf16[8,2,32,128]{3,2,1,0:T(8,128)(2,1)S(1)} all-to-all(bf16[8,2,32,128]{3,2,1,0:T(8,128)(2,1)S(1)} %fusion.1), channel_id=1, replica_groups={{0,32,64,96,128,160,192,224},{4,36,68,100,132,164,196,228},{8,40,72,104..., dimensions={0} | all-to-all | bytes 262144 | tf_op jit(solution)/shard_map/all_to_all | solution.py:348
  53.1 0.6 %convert_reduce_fusion = f32[2,32,128]{2,1,0:T(8,128)} fusion(bf16[8,2,32,128]{3,2,1,0:T(8,128)(2,1)S(1)} %all_to_all.5), kind=kLoop, calls=%fused_computation.5 | loop fusion | flops 122880 | bytes 163840 | tf_op jit(solution)/shard_map/reduce_sum | solution.py:351
  (2 shorter events, 0.1 us)
Async XLA Ops:
  12.7 2.2 %collective-permute-start.1 = (bf16[4,8,2,32,128]{4,3,2,1,0:T(8,128)(2,1)S(1)}, bf16[4,8,2,32,128]{4,3,2,1,0:T(8,128)(2,1)S(1)}, u32[]{:S(2)}, u32[]{:S(2)}) collective-permute-start(bf16[4,8,2,32,128]{4,3,2,1,0:T(8,128)(2,1)S(1)} %get-tuple-element.12), channel_id=1, source_target_pairs={{0,4},{4,0},{8,12},{12,8},{16,20},{20,16},{24,28},{28,24},{32,36},... | collective-permute-start | bytes 1572872 | tf_op jit(solution)/shard_map/ppermute | solution.py:335
  13.0 4.3 %collective-permute-start = (bf16[4,8,2,32,128]{4,3,2,1,0:T(8,128)(2,1)S(1)}, bf16[4,8,2,32,128]{4,3,2,1,0:T(8,128)(2,1)S(1)}, u32[]{:S(2)}, u32[]{:S(2)}) collective-permute-start(bf16[4,8,2,32,128]{4,3,2,1,0:T(8,128)(2,1)S(1)} %get-tuple-element.10), channel_id=1, source_target_pairs={{0,4},{4,0},{8,12},{12,8},{16,20},{20,16},{24,28},{28,24},{32,36},... | collective-permute-start | bytes 1572872 | tf_op jit(solution)/shard_map/ppermute | solution.py:341
  15.1 8.4 %collective-permute-start.2 = (bf16[4,8,2,16,128]{4,3,2,1,0:T(8,128)(2,1)S(1)}, bf16[4,8,2,16,128]{4,3,2,1,0:T(8,128)(2,1)S(1)}, u32[]{:S(2)}, u32[]{:S(2)}) collective-permute-start(bf16[4,8,2,16,128]{4,3,2,1,0:T(8,128)(2,1)S(1)} %get-tuple-element.18), channel_id=1, source_target_pairs={{0,1},{1,2},{2,3},{3,0},{4,5},{5,6},{6,7},{7,4},{8,9},{9,10},{10,1... | collective-permute-start | bytes 786440 | tf_op jit(solution)/shard_map/ppermute | solution.py:339
  17.1 9.3 %collective-permute-start.3 = (bf16[4,8,2,16,128]{4,3,2,1,0:T(8,128)(2,1)S(1)}, bf16[4,8,2,16,128]{4,3,2,1,0:T(8,128)(2,1)S(1)}, u32[]{:S(2)}, u32[]{:S(2)}) collective-permute-start(bf16[4,8,2,16,128]{4,3,2,1,0:T(8,128)(2,1)S(1)} %get-tuple-element.19), channel_id=1, source_target_pairs={{1,0},{2,1},{3,2},{0,3},{5,4},{6,5},{7,6},{4,7},{9,8},{10,9},{11,1... | collective-permute-start | bytes 786440 | tf_op jit(solution)/shard_map/ppermute | solution.py:340
  26.7 6.4 %collective-permute-start.4 = (bf16[8,2,32,128]{3,2,1,0:T(8,128)(2,1)S(1)}, bf16[8,2,32,128]{3,2,1,0:T(8,128)(2,1)S(1)}, u32[]{:S(2)}, u32[]{:S(2)}) collective-permute-start(bf16[8,2,32,128]{3,2,1,0:T(8,128)(2,1)S(1)} %get-tuple-element.15), channel_id=1, source_target_pairs={{0,8},{4,12},{8,0},{12,4},{16,24},{20,28},{24,16},{28,20},{32,40},... | collective-permute-start | bytes 393224 | tf_op jit(solution)/shard_map/ppermute | solution.py:345
  26.8 8.9 %collective-permute-start.6 = (bf16[8,2,32,128]{3,2,1,0:T(8,128)(2,1)S(1)}, bf16[8,2,32,128]{3,2,1,0:T(8,128)(2,1)S(1)}, u32[]{:S(2)}, u32[]{:S(2)}) collective-permute-start(bf16[8,2,32,128]{3,2,1,0:T(8,128)(2,1)S(1)} %get-tuple-element.16), channel_id=1, source_target_pairs={{0,24},{4,28},{8,16},{12,20},{16,8},{20,12},{24,0},{28,4},{32,56},... | collective-permute-start | bytes 393224 | tf_op jit(solution)/shard_map/ppermute | solution.py:345
  28.8 7.0 %collective-permute-start.5 = (bf16[8,2,32,128]{3,2,1,0:T(8,128)(2,1)S(1)}, bf16[8,2,32,128]{3,2,1,0:T(8,128)(2,1)S(1)}, u32[]{:S(2)}, u32[]{:S(2)}) collective-permute-start(bf16[8,2,32,128]{3,2,1,0:T(8,128)(2,1)S(1)} %get-tuple-element.17), channel_id=1, source_target_pairs={{0,16},{4,20},{8,24},{12,28},{16,0},{20,4},{24,8},{28,12},{32,48},... | collective-permute-start | bytes 393224 | tf_op jit(solution)/shard_map/ppermute | solution.py:345

commit v6 on v5

--- a/solution.py
+++ b/solution.py
@@ -334,17 +334,21 @@
 
     edge = keep_edge + lax.ppermute(send_edge, "visit", SIBLING).astype(F32)
     count = lax.axis_size("band")
-    after = edge[:, :, :, :EDGE].astype(BF16)
-    before = edge[:, :, :, EDGE:].astype(BF16)
-    after = lax.ppermute(after, "band", [(i, (i + 1) % count) for i in range(count)])
-    before = lax.ppermute(before, "band", [((i + 1) % count, i) for i in range(count)])
+
+    def along_y(rows):
+        after = rows[:, :, :, :EDGE].astype(BF16)
+        before = rows[:, :, :, EDGE:].astype(BF16)
+        after = lax.ppermute(after, "band", [(i, (i + 1) % count) for i in range(count)])
+        before = lax.ppermute(before, "band", [((i + 1) % count, i) for i in range(count)])
+        return jnp.concatenate([after, before], axis=3).astype(F32)
+
+    moving = along_y(edge[1:])
+    staying = along_y(edge[:1])
     own = keep + lax.ppermute(send, "visit", SIBLING).astype(F32)
-    own = own + jnp.concatenate([after, before], axis=3).astype(F32)
-
-    from_x = [
-        lax.ppermute(own[d].astype(BF16), "visit", ACROSS_X[d - 1]) for d in range(1, XN)
-    ]
-    plane = own[0] + sum(part.astype(F32) for part in from_x)
+    moving = (own[1:] + moving).astype(BF16)
+
+    from_x = [lax.ppermute(moving[d - 1], "visit", ACROSS_X[d - 1]) for d in range(1, XN)]
+    plane = own[0] + staying[0] + sum(part.astype(F32) for part in from_x)
     from_z = lax.all_to_all(
         plane.astype(BF16), "visit", 0, 0, axis_index_groups=ALONG_Z, tiled=True
     )

time: 53.9 us -> 53.2 us (0.987)
  waiting for transfers between devices: 15.4 us -> 12.7 us
  starting transfers between devices: 7.05 us -> 9.75 us
  blocking collectives: 17.3 us -> 16.6 us
    ppermute x5 -> x7, starting transfers between devices: 6.28 us -> 8.98 us  [the longest x3 4.78 us: local(): lax.ppermute(moving[d - 1], 'visit', ACROSS_X[d - 1])]
    ppermute x5 -> x7, waiting for transfers between devices: 14 us -> 11.3 us  [the longest x2 6.97 us: along_y(): lax.ppermute(after, 'band', [(i, (i + 1) % count) for i in range(count)])]
    all_to_all x1, blocking collectives: 17.3 us -> 16.6 us  [local(): lax.all_to_all(plane.astype(BF16), 'visit', 0, 0, axis_index_groups=ALONG...]
  transfers between devices with their start and end apart: 7 -> 9, of which waited for: 5 -> 5; matrix products, arithmetic and copies ran while one was open for 0% -> 1% of each run, Pallas kernels for 0% -> 0%
where the time goes in v6:
time: 53.2 us; the launch traced here: 53.1 us
  blocking collectives  16.6 us (31%)
  Pallas kernels  12.7 us (24%)
  waiting for transfers between devices  12.7 us (24%)
  starting transfers between devices  9.75 us (18%)
  other arithmetic  1.2 us (2%)
    all_to_all x1, blocking collectives, local(): lax.all_to_all(plane.astype(BF16), 'visit', 0, 0, axis_index_groups=ALONG...  16.6 us
    pallas_call x1, Pallas kernels, local(): pl.pallas_call(compute_kernel, out_shape=(wide, wide, narrow, narrow), in...  12.7 us
    ppermute x2, waiting for transfers between devices, along_y(): lax.ppermute(after, 'band', [(i, (i + 1) % count) for i in range(count)])  6.97 us
    ppermute x3, starting transfers between devices, local(): lax.ppermute(moving[d - 1], 'visit', ACROSS_X[d - 1])  4.78 us
    ppermute x2, waiting for transfers between devices, along_y(): lax.ppermute(before, 'band', [((i + 1) % count, i) for i in range(count)])  4.35 us
    ppermute x2, starting transfers between devices, along_y(): lax.ppermute(after, 'band', [(i, (i + 1) % count) for i in range(count)])  2.37 us
    ppermute x2, starting transfers between devices, along_y(): lax.ppermute(before, 'band', [((i + 1) % count, i) for i in range(count)])  1.84 us
    ppermute x1, waiting for transfers between devices, local(): edge = keep_edge + lax.ppermute(send_edge, 'visit', SIBLING).astype(F32)  1.4 us
  transfers between devices with their start and end apart: 9, of which 5 were waited for; matrix products, arithmetic and copies ran while one was open for 1% of the time, Pallas kernels for 0%

profile of v6, /device:TPU:24, one launch (start us, length us, event | category | flops | bytes accessed | tf_op | source)
XLA Modules:
  0.0 53.1 jit_solution(931737286000620117)
XLA Ops:
  0.0 12.7 %shard_map.118 = (f32[4,8,2,32,128]{4,3,2,1,0:T(8,128)S(1)}, f32[4,8,2,32,128]{4,3,2,1,0:T(8,128)S(1)}, bf16[4,8,2,32,128]{4,3,2,1,0:T(8,128)(2,1)S(1)}, bf16[4,8,2,32,128]{4,3,2,1,0:T(8,128)(2,1)S(1)}) custom-call(s32[1,64]{1,0:T(1,128)} %off_hbm.1, s32[1,2]{1,0:T(1,128)} %ids_hbm.1, bf16[1,2,40,8448]{3,2,1,0:T(8,128)(2,1)} %source_hbm.1, ...), custom_call_target="tpu_custom_call" | custom-call | tf_op jit(solution)/shard_map/pallas_call | solution.py:317
  12.7 0.3 collective-permute-start.1
  13.0 0.5 collective-permute-start
  13.5 1.4 %collective-permute-done.1 = bf16[4,8,2,32,128]{4,3,2,1,0:T(8,128)(2,1)S(1)} collective-permute-done((bf16[4,8,2,32,128]{4,3,2,1,0:T(8,128)(2,1)S(1)}, bf16[4,8,2,32,128]{4,3,2,1,0:T(8,128)(2,1)S(1)}, u32[]{:S(2)}, u32[]{:S(2)}) %collective-permute-start.1) | collective-permute-done | bytes 524320 | tf_op jit(solution)/shard_map/ppermute | solution.py:335
  14.9 0.2 add_convert_fusion
  15.1 2.0 %collective-permute-start.4 = (bf16[3,8,2,16,128]{4,3,2,1,0:T(8,128)(2,1)S(1)}, bf16[3,8,2,16,128]{4,3,2,1,0:T(8,128)(2,1)S(1)}, u32[]{:S(2)}, u32[]{:S(2)}) collective-permute-start(bf16[3,8,2,16,128]{4,3,2,1,0:T(8,128)(2,1)S(1)} %get-tuple-element.15), channel_id=1, source_target_pairs={{0,1},{1,2},{2,3},{3,0},{4,5},{5,6},{6,7},{7,4},{8,9},{9,10},{10,1... | collective-permute-start | bytes 589832 | tf_op jit(solution)/shard_map/ppermute | solution.py:341
  17.1 0.1 collective-permute-start.5
  17.2 0.0 collective-permute-done
  17.2 0.2 convert_add_fusion
  17.4 4.7 %collective-permute-done.4 = bf16[3,8,2,16,128]{4,3,2,1,0:T(8,128)(2,1)S(1)} collective-permute-done((bf16[3,8,2,16,128]{4,3,2,1,0:T(8,128)(2,1)S(1)}, bf16[3,8,2,16,128]{4,3,2,1,0:T(8,128)(2,1)S(1)}, u32[]{:S(2)}, u32[]{:S(2)}) %collective-permute-start.4) | collective-permute-done | bytes 196640 | tf_op jit(solution)/shard_map/ppermute | solution.py:341
  22.1 2.9 %collective-permute-done.5 = bf16[3,8,2,16,128]{4,3,2,1,0:T(8,128)(2,1)S(1)} collective-permute-done((bf16[3,8,2,16,128]{4,3,2,1,0:T(8,128)(2,1)S(1)}, bf16[3,8,2,16,128]{4,3,2,1,0:T(8,128)(2,1)S(1)}, u32[]{:S(2)}, u32[]{:S(2)}) %collective-permute-start.5) | collective-permute-done | bytes 196640 | tf_op jit(solution)/shard_map/ppermute | solution.py:342
  25.0 0.1 fusion
  25.1 0.1 collective-permute-start.6
  25.2 2.6 %collective-permute-start.7 = (bf16[8,2,32,128]{3,2,1,0:T(8,128)(2,1)S(1)}, bf16[8,2,32,128]{3,2,1,0:T(8,128)(2,1)S(1)}, u32[]{:S(2)}, u32[]{:S(2)}) collective-permute-start(bf16[8,2,32,128]{3,2,1,0:T(8,128)(2,1)S(1)} %get-tuple-element.19), channel_id=1, source_target_pairs={{0,16},{4,20},{8,24},{12,28},{16,0},{20,4},{24,8},{28,12},{32,48},... | collective-permute-start | bytes 393224 | tf_op jit(solution)/shard_map/ppermute | solution.py:350
  27.9 2.0 %collective-permute-start.8 = (bf16[8,2,32,128]{3,2,1,0:T(8,128)(2,1)S(1)}, bf16[8,2,32,128]{3,2,1,0:T(8,128)(2,1)S(1)}, u32[]{:S(2)}, u32[]{:S(2)}) collective-permute-start(bf16[8,2,32,128]{3,2,1,0:T(8,128)(2,1)S(1)} %get-tuple-element.18), channel_id=1, source_target_pairs={{0,24},{4,28},{8,16},{12,20},{16,8},{20,12},{24,0},{28,4},{32,56},... | collective-permute-start | bytes 393224 | tf_op jit(solution)/shard_map/ppermute | solution.py:350
  29.9 0.4 collective-permute-start.2
  30.3 1.7 %collective-permute-start.3 = (bf16[1,8,2,16,128]{4,3,2,1,0:T(8,128)(2,1)S(1)}, bf16[1,8,2,16,128]{4,3,2,1,0:T(8,128)(2,1)S(1)}, u32[]{:S(2)}, u32[]{:S(2)}) collective-permute-start(bf16[1,8,2,16,128]{4,3,2,1,0:T(8,128)(2,1)S(1)} %get-tuple-element.14), channel_id=1, source_target_pairs={{1,0},{2,1},{3,2},{0,3},{5,4},{6,5},{7,6},{4,7},{9,8},{10,9},{11,1... | collective-permute-start | bytes 196616 | tf_op jit(solution)/shard_map/ppermute | solution.py:342
  32.0 2.2 %collective-permute-done.2 = bf16[1,8,2,16,128]{4,3,2,1,0:T(8,128)(2,1)S(1)} collective-permute-done((bf16[1,8,2,16,128]{4,3,2,1,0:T(8,128)(2,1)S(1)}, bf16[1,8,2,16,128]{4,3,2,1,0:T(8,128)(2,1)S(1)}, u32[]{:S(2)}, u32[]{:S(2)}) %collective-permute-start.2) | collective-permute-done | bytes 65568 | tf_op jit(solution)/shard_map/ppermute | solution.py:341
  34.3 1.5 %collective-permute-done.3 = bf16[1,8,2,16,128]{4,3,2,1,0:T(8,128)(2,1)S(1)} collective-permute-done((bf16[1,8,2,16,128]{4,3,2,1,0:T(8,128)(2,1)S(1)}, bf16[1,8,2,16,128]{4,3,2,1,0:T(8,128)(2,1)S(1)}, u32[]{:S(2)}, u32[]{:S(2)}) %collective-permute-start.3) | collective-permute-done | bytes 65568 | tf_op jit(solution)/shard_map/ppermute | solution.py:342
  35.8 0.0 collective-permute-done.6
  35.8 0.0 collective-permute-done.7
  35.8 0.0 collective-permute-done.8
  35.8 0.1 fusion.3
  35.9 16.6 %all_to_all.5 = bf16[8,2,32,128]{3,2,1,0:T(8,128)(2,1)S(1)} all-to-all(bf16[8,2,32,128]{3,2,1,0:T(8,128)(2,1)S(1)} %fusion.3), channel_id=1, replica_groups={{0,32,64,96,128,160,192,224},{4,36,68,100,132,164,196,228},{8,40,72,104..., dimensions={0} | all-to-all | bytes 262144 | tf_op jit(solution)/shard_map/all_to_all | solution.py:352
  52.4 0.6 %convert_reduce_fusion = f32[2,32,128]{2,1,0:T(8,128)} fusion(bf16[8,2,32,128]{3,2,1,0:T(8,128)(2,1)S(1)} %all_to_all.5), kind=kLoop, calls=%fused_computation.8 | loop fusion | flops 122880 | bytes 163840 | tf_op jit(solution)/shard_map/reduce_sum | solution.py:355
  (3 shorter events, 0.1 us)
Async XLA Ops:
  12.7 2.2 %collective-permute-start.1 = (bf16[4,8,2,32,128]{4,3,2,1,0:T(8,128)(2,1)S(1)}, bf16[4,8,2,32,128]{4,3,2,1,0:T(8,128)(2,1)S(1)}, u32[]{:S(2)}, u32[]{:S(2)}) collective-permute-start(bf16[4,8,2,32,128]{4,3,2,1,0:T(8,128)(2,1)S(1)} %get-tuple-element.12), channel_id=1, source_target_pairs={{0,4},{4,0},{8,12},{12,8},{16,20},{20,16},{24,28},{28,24},{32,36},... | collective-permute-start | bytes 1572872 | tf_op jit(solution)/shard_map/ppermute | solution.py:335
  13.0 4.2 %collective-permute-start = (bf16[4,8,2,32,128]{4,3,2,1,0:T(8,128)(2,1)S(1)}, bf16[4,8,2,32,128]{4,3,2,1,0:T(8,128)(2,1)S(1)}, u32[]{:S(2)}, u32[]{:S(2)}) collective-permute-start(bf16[4,8,2,32,128]{4,3,2,1,0:T(8,128)(2,1)S(1)} %get-tuple-element.10), channel_id=1, source_target_pairs={{0,4},{4,0},{8,12},{12,8},{16,20},{20,16},{24,28},{28,24},{32,36},... | collective-permute-start | bytes 1572872 | tf_op jit(solution)/shard_map/ppermute | solution.py:347
  15.1 7.0 %collective-permute-start.4 = (bf16[3,8,2,16,128]{4,3,2,1,0:T(8,128)(2,1)S(1)}, bf16[3,8,2,16,128]{4,3,2,1,0:T(8,128)(2,1)S(1)}, u32[]{:S(2)}, u32[]{:S(2)}) collective-permute-start(bf16[3,8,2,16,128]{4,3,2,1,0:T(8,128)(2,1)S(1)} %get-tuple-element.15), channel_id=1, source_target_pairs={{0,1},{1,2},{2,3},{3,0},{4,5},{5,6},{6,7},{7,4},{8,9},{9,10},{10,1... | collective-permute-start | bytes 589832 | tf_op jit(solution)/shard_map/ppermute | solution.py:341
  17.1 7.9 %collective-permute-start.5 = (bf16[3,8,2,16,128]{4,3,2,1,0:T(8,128)(2,1)S(1)}, bf16[3,8,2,16,128]{4,3,2,1,0:T(8,128)(2,1)S(1)}, u32[]{:S(2)}, u32[]{:S(2)}) collective-permute-start(bf16[3,8,2,16,128]{4,3,2,1,0:T(8,128)(2,1)S(1)} %get-tuple-element.16), channel_id=1, source_target_pairs={{1,0},{2,1},{3,2},{0,3},{5,4},{6,5},{7,6},{4,7},{9,8},{10,9},{11,1... | collective-permute-start | bytes 589832 | tf_op jit(solution)/shard_map/ppermute | solution.py:342
  25.1 10.6 %collective-permute-start.6 = (bf16[8,2,32,128]{3,2,1,0:T(8,128)(2,1)S(1)}, bf16[8,2,32,128]{3,2,1,0:T(8,128)(2,1)S(1)}, u32[]{:S(2)}, u32[]{:S(2)}) collective-permute-start(bf16[8,2,32,128]{3,2,1,0:T(8,128)(2,1)S(1)} %get-tuple-element.17), channel_id=1, source_target_pairs={{0,8},{4,12},{8,0},{12,4},{16,24},{20,28},{24,16},{28,20},{32,40},... | collective-permute-start | bytes 393224 | tf_op jit(solution)/shard_map/ppermute | solution.py:350
  25.2 10.5 %collective-permute-start.7 = (bf16[8,2,32,128]{3,2,1,0:T(8,128)(2,1)S(1)}, bf16[8,2,32,128]{3,2,1,0:T(8,128)(2,1)S(1)}, u32[]{:S(2)}, u32[]{:S(2)}) collective-permute-start(bf16[8,2,32,128]{3,2,1,0:T(8,128)(2,1)S(1)} %get-tuple-element.19), channel_id=1, source_target_pairs={{0,16},{4,20},{8,24},{12,28},{16,0},{20,4},{24,8},{28,12},{32,48},... | collective-permute-start | bytes 393224 | tf_op jit(solution)/shard_map/ppermute | solution.py:350
  27.9 7.9 %collective-permute-start.8 = (bf16[8,2,32,128]{3,2,1,0:T(8,128)(2,1)S(1)}, bf16[8,2,32,128]{3,2,1,0:T(8,128)(2,1)S(1)}, u32[]{:S(2)}, u32[]{:S(2)}) collective-permute-start(bf16[8,2,32,128]{3,2,1,0:T(8,128)(2,1)S(1)} %get-tuple-element.18), channel_id=1, source_target_pairs={{0,24},{4,28},{8,16},{12,20},{16,8},{20,12},{24,0},{28,4},{32,56},... | collective-permute-start | bytes 393224 | tf_op jit(solution)/shard_map/ppermute | solution.py:350
  29.9 4.3 %collective-permute-start.2 = (bf16[1,8,2,16,128]{4,3,2,1,0:T(8,128)(2,1)S(1)}, bf16[1,8,2,16,128]{4,3,2,1,0:T(8,128)(2,1)S(1)}, u32[]{:S(2)}, u32[]{:S(2)}) collective-permute-start(bf16[1,8,2,16,128]{4,3,2,1,0:T(8,128)(2,1)S(1)} %get-tuple-element.13), channel_id=1, source_target_pairs={{0,1},{1,2},{2,3},{3,0},{4,5},{5,6},{6,7},{7,4},{8,9},{9,10},{10,1... | collective-permute-start | bytes 196616 | tf_op jit(solution)/shard_map/ppermute | solution.py:341
  30.3 5.5 %collective-permute-start.3 = (bf16[1,8,2,16,128]{4,3,2,1,0:T(8,128)(2,1)S(1)}, bf16[1,8,2,16,128]{4,3,2,1,0:T(8,128)(2,1)S(1)}, u32[]{:S(2)}, u32[]{:S(2)}) collective-permute-start(bf16[1,8,2,16,128]{4,3,2,1,0:T(8,128)(2,1)S(1)} %get-tuple-element.14), channel_id=1, source_target_pairs={{1,0},{2,1},{3,2},{0,3},{5,4},{6,5},{7,6},{4,7},{9,8},{10,9},{11,1... | collective-permute-start | bytes 196616 | tf_op jit(solution)/shard_map/ppermute | solution.py:342

commit v7 on v6

--- a/solution.py
+++ b/solution.py
@@ -256,7 +256,7 @@
         for step in range(GROUP):
             if z < ZN:
                 filter_columns(z, lhs, step)
-            if step % 2 == 0 and ready <= blocks // 2:
+            if step < GROUP // 2 and ready <= blocks // 2:
                 before = col_step(ready, before)
                 ready += 1
             if z > 0:

time: 53.2 us -> 53.2 us (level)
  no operation moved by 1% of the time
where the time goes in v7:
time: 53.2 us; the launch traced here: 53.1 us
  blocking collectives  16.6 us (31%)
  waiting for transfers between devices  12.8 us (24%)
  Pallas kernels  12.6 us (24%)
  starting transfers between devices  9.75 us (18%)
  other arithmetic  1.2 us (2%)
    all_to_all x1, blocking collectives, local(): lax.all_to_all(plane.astype(BF16), 'visit', 0, 0, axis_index_groups=ALONG...  16.6 us
    pallas_call x1, Pallas kernels, local(): pl.pallas_call(compute_kernel, out_shape=(wide, wide, narrow, narrow), in...  12.6 us
    ppermute x2, waiting for transfers between devices, along_y(): lax.ppermute(after, 'band', [(i, (i + 1) % count) for i in range(count)])  6.97 us
    ppermute x3, starting transfers between devices, local(): lax.ppermute(moving[d - 1], 'visit', ACROSS_X[d - 1])  4.78 us
    ppermute x2, waiting for transfers between devices, along_y(): lax.ppermute(before, 'band', [((i + 1) % count, i) for i in range(count)])  4.39 us
    ppermute x2, starting transfers between devices, along_y(): lax.ppermute(after, 'band', [(i, (i + 1) % count) for i in range(count)])  2.41 us
    ppermute x2, starting transfers between devices, along_y(): lax.ppermute(before, 'band', [((i + 1) % count, i) for i in range(count)])  1.8 us
    ppermute x1, waiting for transfers between devices, local(): edge = keep_edge + lax.ppermute(send_edge, 'visit', SIBLING).astype(F32)  1.4 us
  transfers between devices with their start and end apart: 9, of which 5 were waited for; matrix products, arithmetic and copies ran while one was open for 1% of the time, Pallas kernels for 0%

profile of v7, /device:TPU:24, one launch (start us, length us, event | category | flops | bytes accessed | tf_op | source)
XLA Modules:
  0.0 53.1 jit_solution(18081329441176791669)
XLA Ops:
  0.0 12.6 %shard_map.118 = (f32[4,8,2,32,128]{4,3,2,1,0:T(8,128)S(1)}, f32[4,8,2,32,128]{4,3,2,1,0:T(8,128)S(1)}, bf16[4,8,2,32,128]{4,3,2,1,0:T(8,128)(2,1)S(1)}, bf16[4,8,2,32,128]{4,3,2,1,0:T(8,128)(2,1)S(1)}) custom-call(s32[1,64]{1,0:T(1,128)} %off_hbm.1, s32[1,2]{1,0:T(1,128)} %ids_hbm.1, bf16[1,2,40,8448]{3,2,1,0:T(8,128)(2,1)} %source_hbm.1, ...), custom_call_target="tpu_custom_call" | custom-call | tf_op jit(solution)/shard_map/pallas_call | solution.py:317
  12.6 0.3 collective-permute-start.1
  12.9 0.5 collective-permute-start
  13.4 1.4 %collective-permute-done.1 = bf16[4,8,2,32,128]{4,3,2,1,0:T(8,128)(2,1)S(1)} collective-permute-done((bf16[4,8,2,32,128]{4,3,2,1,0:T(8,128)(2,1)S(1)}, bf16[4,8,2,32,128]{4,3,2,1,0:T(8,128)(2,1)S(1)}, u32[]{:S(2)}, u32[]{:S(2)}) %collective-permute-start.1) | collective-permute-done | bytes 524320 | tf_op jit(solution)/shard_map/ppermute | solution.py:335
  14.8 0.2 add_convert_fusion
  15.0 2.0 %collective-permute-start.4 = (bf16[3,8,2,16,128]{4,3,2,1,0:T(8,128)(2,1)S(1)}, bf16[3,8,2,16,128]{4,3,2,1,0:T(8,128)(2,1)S(1)}, u32[]{:S(2)}, u32[]{:S(2)}) collective-permute-start(bf16[3,8,2,16,128]{4,3,2,1,0:T(8,128)(2,1)S(1)} %get-tuple-element.15), channel_id=1, source_target_pairs={{0,1},{1,2},{2,3},{3,0},{4,5},{5,6},{6,7},{7,4},{8,9},{9,10},{10,1... | collective-permute-start | bytes 589832 | tf_op jit(solution)/shard_map/ppermute | solution.py:341
  17.0 0.1 collective-permute-start.5
  17.1 0.0 collective-permute-done
  17.1 0.2 convert_add_fusion
  17.3 4.7 %collective-permute-done.4 = bf16[3,8,2,16,128]{4,3,2,1,0:T(8,128)(2,1)S(1)} collective-permute-done((bf16[3,8,2,16,128]{4,3,2,1,0:T(8,128)(2,1)S(1)}, bf16[3,8,2,16,128]{4,3,2,1,0:T(8,128)(2,1)S(1)}, u32[]{:S(2)}, u32[]{:S(2)}) %collective-permute-start.4) | collective-permute-done | bytes 196640 | tf_op jit(solution)/shard_map/ppermute | solution.py:341
  22.0 2.9 %collective-permute-done.5 = bf16[3,8,2,16,128]{4,3,2,1,0:T(8,128)(2,1)S(1)} collective-permute-done((bf16[3,8,2,16,128]{4,3,2,1,0:T(8,128)(2,1)S(1)}, bf16[3,8,2,16,128]{4,3,2,1,0:T(8,128)(2,1)S(1)}, u32[]{:S(2)}, u32[]{:S(2)}) %collective-permute-start.5) | collective-permute-done | bytes 196640 | tf_op jit(solution)/shard_map/ppermute | solution.py:342
  24.9 0.1 fusion
  25.1 0.1 collective-permute-start.6
  25.2 2.6 %collective-permute-start.7 = (bf16[8,2,32,128]{3,2,1,0:T(8,128)(2,1)S(1)}, bf16[8,2,32,128]{3,2,1,0:T(8,128)(2,1)S(1)}, u32[]{:S(2)}, u32[]{:S(2)}) collective-permute-start(bf16[8,2,32,128]{3,2,1,0:T(8,128)(2,1)S(1)} %get-tuple-element.19), channel_id=1, source_target_pairs={{0,16},{4,20},{8,24},{12,28},{16,0},{20,4},{24,8},{28,12},{32,48},... | collective-permute-start | bytes 393224 | tf_op jit(solution)/shard_map/ppermute | solution.py:350
  27.8 2.1 %collective-permute-start.8 = (bf16[8,2,32,128]{3,2,1,0:T(8,128)(2,1)S(1)}, bf16[8,2,32,128]{3,2,1,0:T(8,128)(2,1)S(1)}, u32[]{:S(2)}, u32[]{:S(2)}) collective-permute-start(bf16[8,2,32,128]{3,2,1,0:T(8,128)(2,1)S(1)} %get-tuple-element.18), channel_id=1, source_target_pairs={{0,24},{4,28},{8,16},{12,20},{16,8},{20,12},{24,0},{28,4},{32,56},... | collective-permute-start | bytes 393224 | tf_op jit(solution)/shard_map/ppermute | solution.py:350
  29.9 0.4 collective-permute-start.2
  30.2 1.7 %collective-permute-start.3 = (bf16[1,8,2,16,128]{4,3,2,1,0:T(8,128)(2,1)S(1)}, bf16[1,8,2,16,128]{4,3,2,1,0:T(8,128)(2,1)S(1)}, u32[]{:S(2)}, u32[]{:S(2)}) collective-permute-start(bf16[1,8,2,16,128]{4,3,2,1,0:T(8,128)(2,1)S(1)} %get-tuple-element.14), channel_id=1, source_target_pairs={{1,0},{2,1},{3,2},{0,3},{5,4},{6,5},{7,6},{4,7},{9,8},{10,9},{11,1... | collective-permute-start | bytes 196616 | tf_op jit(solution)/shard_map/ppermute | solution.py:342
  32.0 2.2 %collective-permute-done.2 = bf16[1,8,2,16,128]{4,3,2,1,0:T(8,128)(2,1)S(1)} collective-permute-done((bf16[1,8,2,16,128]{4,3,2,1,0:T(8,128)(2,1)S(1)}, bf16[1,8,2,16,128]{4,3,2,1,0:T(8,128)(2,1)S(1)}, u32[]{:S(2)}, u32[]{:S(2)}) %collective-permute-start.2) | collective-permute-done | bytes 65568 | tf_op jit(solution)/shard_map/ppermute | solution.py:341
  34.2 1.5 %collective-permute-done.3 = bf16[1,8,2,16,128]{4,3,2,1,0:T(8,128)(2,1)S(1)} collective-permute-done((bf16[1,8,2,16,128]{4,3,2,1,0:T(8,128)(2,1)S(1)}, bf16[1,8,2,16,128]{4,3,2,1,0:T(8,128)(2,1)S(1)}, u32[]{:S(2)}, u32[]{:S(2)}) %collective-permute-start.3) | collective-permute-done | bytes 65568 | tf_op jit(solution)/shard_map/ppermute | solution.py:342
  35.7 0.0 collective-permute-done.6
  35.7 0.0 collective-permute-done.7
  35.7 0.0 collective-permute-done.8
  35.7 0.1 fusion.3
  35.8 16.6 %all_to_all.5 = bf16[8,2,32,128]{3,2,1,0:T(8,128)(2,1)S(1)} all-to-all(bf16[8,2,32,128]{3,2,1,0:T(8,128)(2,1)S(1)} %fusion.3), channel_id=1, replica_groups={{0,32,64,96,128,160,192,224},{4,36,68,100,132,164,196,228},{8,40,72,104..., dimensions={0} | all-to-all | bytes 262144 | tf_op jit(solution)/shard_map/all_to_all | solution.py:352
  52.4 0.6 %convert_reduce_fusion = f32[2,32,128]{2,1,0:T(8,128)} fusion(bf16[8,2,32,128]{3,2,1,0:T(8,128)(2,1)S(1)} %all_to_all.5), kind=kLoop, calls=%fused_computation.8 | loop fusion | flops 122880 | bytes 163840 | tf_op jit(solution)/shard_map/reduce_sum | solution.py:355
  (3 shorter events, 0.1 us)
Async XLA Ops:
  12.6 2.2 %collective-permute-start.1 = (bf16[4,8,2,32,128]{4,3,2,1,0:T(8,128)(2,1)S(1)}, bf16[4,8,2,32,128]{4,3,2,1,0:T(8,128)(2,1)S(1)}, u32[]{:S(2)}, u32[]{:S(2)}) collective-permute-start(bf16[4,8,2,32,128]{4,3,2,1,0:T(8,128)(2,1)S(1)} %get-tuple-element.12), channel_id=1, source_target_pairs={{0,4},{4,0},{8,12},{12,8},{16,20},{20,16},{24,28},{28,24},{32,36},... | collective-permute-start | bytes 1572872 | tf_op jit(solution)/shard_map/ppermute | solution.py:335
  12.9 4.2 %collective-permute-start = (bf16[4,8,2,32,128]{4,3,2,1,0:T(8,128)(2,1)S(1)}, bf16[4,8,2,32,128]{4,3,2,1,0:T(8,128)(2,1)S(1)}, u32[]{:S(2)}, u32[]{:S(2)}) collective-permute-start(bf16[4,8,2,32,128]{4,3,2,1,0:T(8,128)(2,1)S(1)} %get-tuple-element.10), channel_id=1, source_target_pairs={{0,4},{4,0},{8,12},{12,8},{16,20},{20,16},{24,28},{28,24},{32,36},... | collective-permute-start | bytes 1572872 | tf_op jit(solution)/shard_map/ppermute | solution.py:347
  15.0 7.0 %collective-permute-start.4 = (bf16[3,8,2,16,128]{4,3,2,1,0:T(8,128)(2,1)S(1)}, bf16[3,8,2,16,128]{4,3,2,1,0:T(8,128)(2,1)S(1)}, u32[]{:S(2)}, u32[]{:S(2)}) collective-permute-start(bf16[3,8,2,16,128]{4,3,2,1,0:T(8,128)(2,1)S(1)} %get-tuple-element.15), channel_id=1, source_target_pairs={{0,1},{1,2},{2,3},{3,0},{4,5},{5,6},{6,7},{7,4},{8,9},{9,10},{10,1... | collective-permute-start | bytes 589832 | tf_op jit(solution)/shard_map/ppermute | solution.py:341
  17.0 7.9 %collective-permute-start.5 = (bf16[3,8,2,16,128]{4,3,2,1,0:T(8,128)(2,1)S(1)}, bf16[3,8,2,16,128]{4,3,2,1,0:T(8,128)(2,1)S(1)}, u32[]{:S(2)}, u32[]{:S(2)}) collective-permute-start(bf16[3,8,2,16,128]{4,3,2,1,0:T(8,128)(2,1)S(1)} %get-tuple-element.16), channel_id=1, source_target_pairs={{1,0},{2,1},{3,2},{0,3},{5,4},{6,5},{7,6},{4,7},{9,8},{10,9},{11,1... | collective-permute-start | bytes 589832 | tf_op jit(solution)/shard_map/ppermute | solution.py:342
  25.1 10.6 %collective-permute-start.6 = (bf16[8,2,32,128]{3,2,1,0:T(8,128)(2,1)S(1)}, bf16[8,2,32,128]{3,2,1,0:T(8,128)(2,1)S(1)}, u32[]{:S(2)}, u32[]{:S(2)}) collective-permute-start(bf16[8,2,32,128]{3,2,1,0:T(8,128)(2,1)S(1)} %get-tuple-element.17), channel_id=1, source_target_pairs={{0,8},{4,12},{8,0},{12,4},{16,24},{20,28},{24,16},{28,20},{32,40},... | collective-permute-start | bytes 393224 | tf_op jit(solution)/shard_map/ppermute | solution.py:350
  25.2 10.5 %collective-permute-start.7 = (bf16[8,2,32,128]{3,2,1,0:T(8,128)(2,1)S(1)}, bf16[8,2,32,128]{3,2,1,0:T(8,128)(2,1)S(1)}, u32[]{:S(2)}, u32[]{:S(2)}) collective-permute-start(bf16[8,2,32,128]{3,2,1,0:T(8,128)(2,1)S(1)} %get-tuple-element.19), channel_id=1, source_target_pairs={{0,16},{4,20},{8,24},{12,28},{16,0},{20,4},{24,8},{28,12},{32,48},... | collective-permute-start | bytes 393224 | tf_op jit(solution)/shard_map/ppermute | solution.py:350
  27.8 7.9 %collective-permute-start.8 = (bf16[8,2,32,128]{3,2,1,0:T(8,128)(2,1)S(1)}, bf16[8,2,32,128]{3,2,1,0:T(8,128)(2,1)S(1)}, u32[]{:S(2)}, u32[]{:S(2)}) collective-permute-start(bf16[8,2,32,128]{3,2,1,0:T(8,128)(2,1)S(1)} %get-tuple-element.18), channel_id=1, source_target_pairs={{0,24},{4,28},{8,16},{12,20},{16,8},{20,12},{24,0},{28,4},{32,56},... | collective-permute-start | bytes 393224 | tf_op jit(solution)/shard_map/ppermute | solution.py:350
  29.9 4.3 %collective-permute-start.2 = (bf16[1,8,2,16,128]{4,3,2,1,0:T(8,128)(2,1)S(1)}, bf16[1,8,2,16,128]{4,3,2,1,0:T(8,128)(2,1)S(1)}, u32[]{:S(2)}, u32[]{:S(2)}) collective-permute-start(bf16[1,8,2,16,128]{4,3,2,1,0:T(8,128)(2,1)S(1)} %get-tuple-element.13), channel_id=1, source_target_pairs={{0,1},{1,2},{2,3},{3,0},{4,5},{5,6},{6,7},{7,4},{8,9},{9,10},{10,1... | collective-permute-start | bytes 196616 | tf_op jit(solution)/shard_map/ppermute | solution.py:341
  30.2 5.5 %collective-permute-start.3 = (bf16[1,8,2,16,128]{4,3,2,1,0:T(8,128)(2,1)S(1)}, bf16[1,8,2,16,128]{4,3,2,1,0:T(8,128)(2,1)S(1)}, u32[]{:S(2)}, u32[]{:S(2)}) collective-permute-start(bf16[1,8,2,16,128]{4,3,2,1,0:T(8,128)(2,1)S(1)} %get-tuple-element.14), channel_id=1, source_target_pairs={{1,0},{2,1},{3,2},{0,3},{5,4},{6,5},{7,6},{4,7},{9,8},{10,9},{11,1... | collective-permute-start | bytes 196616 | tf_op jit(solution)/shard_map/ppermute | solution.py:342
